TPU v7x, 256 devices: a whole 4x4x8 slice. The times are simulated.
256 devices in a mesh: gx: 4 (over x), gy: 16 (over y_lo, z), gz: 4 (over y_hi, core).
Axes of the slice: x: 4, y: 4 (y_hi: 2, y_lo: 2; y = y_hi * 2 + y_lo), z: 8, core: 2. Of those that a mesh axis runs over, the one named last changes fastest.
Arguments:
- adjoint_now: float32 [160, 640, 512], P('gx', 'gy', 'gz'), may hold values from -6 to 6
- adjoint_late: float32 [160, 640, 512], P('gx', 'gy', 'gz'), may hold values from -6 to 6
- courant: float32 [160, 640, 512], P('gx', 'gy', 'gz'), may hold values from 0.05 to 0.18
- forward: bfloat16 [2, 160, 640, 512], P(None, 'gx', 'gy', 'gz'), may hold values from -6 to 6
- image_in: float32 [160, 640, 512], P('gx', 'gy', 'gz'), may hold values from -6 to 6
- traces: float32 [2, 65536], P(None, ('gy', 'gz')), may hold values from -6 to 6
- rec_owner: int32 [65536], P(('gy', 'gz')), may hold values from 0 to 255, as said below
- rec_cell: int32 [65536], P(('gy', 'gz')), may hold values from 0 to 204799, as said below
Outputs:
- adjoint_newest: float32 [160, 640, 512], P('gx', 'gy', 'gz')
- adjoint_middle: float32 [160, 640, 512], P('gx', 'gy', 'gz')
- image_out: float32 [160, 640, 512], P('gx', 'gy', 'gz')
Inputs may be any that keep to these rules, and one draw needn't show every extreme that they name: `rec_owner`: the owner is the flat mesh index (gx * 16 + gy) * 4 + gz of the device whose block holds the receiver's cell, always with gz = 0. Among the records of one index of gy+gz at most 64 have one owner, and in every such block one owner has exactly 64. `rec_cell`: the cell within the owner's block, numbered (x * 40 + y) * 128 + z, with depth z below 8.
All inputs are finite; a program needn't handle non-finite values.
Results may differ from a plain program's by a relative error of at most 0.0003.
Values sent between devices are 32-bit elements; how exact they have to be, the bound alone decides.
No kernel may reach another device: no remote copies, remote signals or barrier semaphores. Data moves between devices by JAX's collectives and lax.ppermute only.
A program may use at most 128 MiB of HBM per device.

v0:
```python
import math

import jax
import jax.numpy as jnp
from jax import lax
from jax.sharding import PartitionSpec as P

SURF = 8


COEFFS = (-205.0 / 72.0, 8.0 / 5.0, -1.0 / 5.0, 8.0 / 315.0, -1.0 / 560.0)


def padded_2(value, sides, width):
    for axis, dim in sides:
        devices, length = (lax.axis_size(axis), value.shape[dim])
        up = [(i, (i + 1) % devices) for i in range(devices - 1)]
        down = [(j, i) for i, j in up]
        last = lax.slice_in_dim(value, length - width, length, axis=dim)
        initial = lax.slice_in_dim(value, 0, width, axis=dim)
        before = lax.ppermute(last, axis, up)
        after = lax.ppermute(initial, axis, down)
        value = jnp.concatenate([before, value, after], axis=dim)
    return value


def axis_part(padded, axis, length):
    center = lax.slice_in_dim(padded, 4, 4 + length, axis=axis)
    summed = COEFFS[0] * center
    for shift in range(1, 5):
        upper = lax.slice_in_dim(padded, 4 + shift, 4 + shift + length, axis=axis)
        lower = lax.slice_in_dim(padded, 4 - shift, 4 - shift + length, axis=axis)
        summed = summed + COEFFS[shift] * (upper + lower)
    return summed


def inner_laplacian(padded):
    span_x, span_y, span_z = padded.shape
    along_x = padded[:, 4 : span_y - 4, 4 : span_z - 4]
    along_y = padded[4 : span_x - 4, :, 4 : span_z - 4]
    along_z = padded[4 : span_x - 4, 4 : span_y - 4, :]
    return (
        axis_part(along_x, 0, span_x - 8)
        + axis_part(along_y, 1, span_y - 8)
        + axis_part(along_z, 2, span_z - 8)
    )


def laplacian(field):
    padded = padded_2(field, (("gx", 0), ("gy", 1), ("gz", 2)), 4)
    return inner_laplacian(padded)


def plane_sources(values, cells, shape, layers):
    steps, total = values.shape
    size_x, size_y, size_z = shape
    plane = size_x * size_y
    block = math.gcd(total, 4096)
    turns = total // block
    high = values.astype(jnp.bfloat16)
    remain = values - high.astype(jnp.float32)
    middle = remain.astype(jnp.bfloat16)
    lowest = (remain - middle.astype(jnp.float32)).astype(jnp.bfloat16)
    pieces = jnp.concatenate([high, middle, lowest], axis=0)
    pieces = jnp.transpose(pieces.reshape(3 * steps, turns, block), (1, 0, 2))
    cell_blocks = cells.reshape(turns, block)
    plane_ids = jnp.arange(plane, dtype=jnp.int32)
    layer_ids = jnp.arange(layers, dtype=jnp.int32)

    def accumulate(summed, item):
        cell_block, piece_block = item
        flat_plane = cell_block // size_z
        depth = cell_block % size_z
        pick_plane = (flat_plane[:, None] == plane_ids[None, :]).astype(jnp.bfloat16)
        pick_layer = (depth[:, None] == layer_ids[None, :]).astype(jnp.bfloat16)
        weighted = pick_layer[:, :, None] * jnp.transpose(piece_block)[:, None, :]
        weighted = weighted.reshape(block, layers * 3 * steps)
        term = lax.dot_general(
            pick_plane, weighted, (((0,), (0,)), ((), ())), preferred_element_type=jnp.float32
        )
        return (summed + term, None)

    start = jnp.zeros((plane, layers * 3 * steps), jnp.float32)
    summed, unused = lax.scan(accumulate, start, (cell_blocks, pieces))
    summed = summed.reshape(plane, layers, 3, steps).sum(axis=2)
    summed = jnp.transpose(summed, (2, 0, 1)).reshape(steps, size_x, size_y, layers)
    return jnp.pad(summed, ((0, 0), (0, 0), (0, 0), (0, size_z - layers)))


def on_device(adjoint_now, adjoint_late, courant, forward, image_in, traces, rec_owner, rec_cell):
    shape = adjoint_now.shape
    steps = traces.shape[0]
    my_column = lax.axis_index("gx")
    my_device = (my_column * lax.axis_size("gy") + lax.axis_index("gy")) * lax.axis_size(
        "gz"
    ) + lax.axis_index("gz")
    all_traces, all_owners, all_cells = (
        lax.all_gather(traces, ("gy", "gz"), axis=1, tiled=True),
        lax.all_gather(rec_owner, ("gy", "gz"), axis=0, tiled=True),
        lax.all_gather(rec_cell, ("gy", "gz"), axis=0, tiled=True),
    )
    owned = all_owners == my_device
    packed_values = jnp.where(owned[None, :], all_traces, 0.0)
    sources = plane_sources(packed_values, all_cells, shape, min(SURF, shape[2]))
    image = image_in
    current = adjoint_now
    previous = adjoint_late
    for step in range(steps):
        fresh = 2.0 * current - previous + courant * (laplacian(current) + sources[step])
        image = image + forward[step].astype(jnp.float32) * fresh
        previous = current
        current = fresh
    return (current, previous, image)


def solution(mesh):
    return jax.shard_map(
        on_device,
        mesh=mesh,
        in_specs=(
            P("gx", "gy", "gz"),
            P("gx", "gy", "gz"),
            P("gx", "gy", "gz"),
            P(None, "gx", "gy", "gz"),
            P("gx", "gy", "gz"),
            P(None, ("gy", "gz")),
            P(("gy", "gz")),
            P(("gy", "gz")),
        ),
        out_specs=(P("gx", "gy", "gz"), P("gx", "gy", "gz"), P("gx", "gy", "gz")),
        check_vma=False,
    )
```

profile of v0, /device:TPU:101, one launch (start us, length us, event | category | flops | bytes accessed | tf_op | source)
XLA Modules:
  0.0 527.5 jit_solution(9841748446992937921)
XLA Ops:
  7.5 75.7 %all_gather.10 = s32[65536]{0:T(1024)S(1)} all-gather(s32[1024]{0:T(1024)} %param.16), channel_id=1, replica_groups=mesh['gx'=4,'gy'=16,'gz'=4] {'gy','gz'}, dimensions={0}, use_global_device_ids=true | all-gather | bytes 266240 | tf_op jit(solution)/shard_map/all_gather | solution.py:99
  83.2 73.3 %all_gather.11 = f32[2,65536]{1,0:T(2,128)S(1)} all-gather(f32[2,1024]{1,0:T(2,128)} %param.15), channel_id=1, replica_groups=mesh['gx'=4,'gy'=16,'gz'=4] {'gy','gz'}, dimensions={1}, use_global_device_ids=true | all-gather | bytes 532480 | tf_op jit(solution)/shard_map/all_gather | solution.py:98
  157.5 75.1 %all_gather.9 = s32[65536]{0:T(1024)S(1)} all-gather(s32[1024]{0:T(1024)S(1)} %copy-done.9), channel_id=1, replica_groups=mesh['gx'=4,'gy'=16,'gz'=4] {'gy','gz'}, dimensions={0}, use_global_device_ids=true | all-gather | bytes 266240 | tf_op jit(solution)/shard_map/all_gather | solution.py:100
  233.5 88.7 %while.13 = (s32[]{:T(128)}, f32[1600,48]{0,1:T(8,128)S(1)}, s32[16,4096]{1,0:T(8,128)S(1)}, bf16[16,6,4096]{2,1,0:T(8,128)(2,1)S(1)}, s32[]{:T(128)}, /*index=5*/s32[]{:T(128)}) while((s32[]{:T(128)}, f32[1600,48]{0,1:T(8,128)S(1)}, s32[16,4096]{1,0:T(8,128)S(1)}, bf16[16,6,4096]{2,1,0:T(8,128)(2,1)S(1)}, s32[]{:T(128)}, ...), condition=%wide.region_1.2_spmd.clone, body=%wide.region_0.1_spmd.clone.sunk | while | flops 636192768 | bytes 2580567 | solution.py:84
  233.8 5.2 fusion.102
  239.4 5.2 fusion.102
  244.9 5.2 fusion.102
  250.5 5.2 fusion.102
  256.0 5.2 fusion.102
  261.6 5.2 fusion.102
  267.1 5.2 fusion.102
  272.7 5.2 fusion.102
  278.2 5.2 fusion.102
  283.8 5.2 fusion.102
  289.3 5.2 fusion.102
  294.9 5.2 fusion.102
  300.4 5.2 fusion.102
  311.5 5.2 fusion.102
  317.0 5.2 fusion.102
  336.5 5.5 %collective-permute-start.3 = (f32[48,4,128]{2,0,1:T(8,128)}, f32[48,4,128]{2,0,1:T(8,128)}, u32[]{:S(2)}, u32[]{:S(2)}) collective-permute-start(f32[48,4,128]{2,0,1:T(8,128)} %copy.165), channel_id=1, source_target_pairs={{0,4},{4,8},{8,12},{12,16},{16,20},{20,24},{24,28},{28,32},{32,36}... | collective-permute-start | bytes 294920 | tf_op jit(solution)/shard_map/ppermute | solution.py:21
  387.4 8.5 %pad_maximum_fusion = (f32[48,48,132]{1,0,2:T(8,128)}, f32[48,48,132]{1,0,2:T(8,128)}) fusion(f32[48,48,4]{1,0,2:T(8,128)} %collective-permute-done.4, f32[48,4,128]{1,0,2:T(8,128)} %copy.133, f32[48,40,128]{1,0,2:T(8,128)S(1)} %copy.132, f32[48,4,128]{1,0,2:T(8,128)} %copy.135, f32[48,48,4]{1,0,2:T(8,128)} %collective-permute-done.5), kind=kLoop, calls=%fused_computation.33 | loop fusion | flops 1824768 | bytes 3686400 | tf_op jit(solution)/shard_map/concatenate | solution.py:23
  395.9 43.7 %fusion.19 = f32[40,40,128]{1,0,2:T(8,128)S(1)} fusion(f32[40,40,128]{1,0,2:T(8,128)} %copy.141, f32[48,4,128]{1,0,2:T(8,128)} %copy.135, f32[48,40,128]{1,0,2:T(8,128)} %copy-done, f32[48,4,128]{1,0,2:T(8,128)} %copy.133, f32[48,48,132]{1,0,2:T(8,128)} %get-tuple-element.129, f32[48,48,132]{1,0,2:T(8,128)} %get-tuple-element.128, f32[40,40,128]{1,0,2:T(8,128)} %copy.162, ...), kind=kLoop, calls=%fused_computation.61 | loop fusion | flops 10649600 | bytes 17666048 | tf_op jit(solution)/shard_map/add | solution.py:109
  497.4 6.8 %pad_maximum_fusion.1 = (f32[48,48,132]{1,0,2:T(8,128)}, f32[48,48,132]{1,0,2:T(8,128)}) fusion(f32[48,48,4]{1,0,2:T(8,128)S(1)} %collective-permute-done.10, f32[48,4,128]{1,0,2:T(8,128)S(1)} %copy-done.1, f32[4,40,128]{1,0,2:T(4,128)S(1)} %collective-permute-done.6, f32[40,40,128]{1,0,2:T(8,128)S(1)} %fusion.19, ...), kind=kLoop, calls=%fused_computation.35 | loop fusion | flops 3041280 | bytes 3686400 | tf_op jit(solution)/shard_map/concatenate | solution.py:23
  504.1 17.9 %fusion.82 = (f32[40,40,128]{1,0,2:T(8,128)}, f32[40,40,128]{1,0,2:T(8,128)}) fusion(f32[40,40,128]{1,0,2:T(8,128)} %copy.151, f32[40,40,128]{1,0,2:T(8,128)S(1)} %fusion.19, bf16[1,40,40,128]{2,1,3,0:T(8,128)(2,1)} %copy.167, bf16[1,40,40,128]{2,1,3,0:T(8,128)(2,1)} %copy.166, f32[40,40,128]{1,0,2:T(8,128)} %copy.141, ...), kind=kLoop, calls=%fused_computation.141 | loop fusion | flops 11878400 | bytes 19107840 | tf_op jit(solution)/shard_map/add | solution.py:110
  (189 shorter events, 140.4 us)
Async XLA Ops:
  0.6 156.9 %copy-start.9 = (s32[1024]{0:T(1024)S(1)}, s32[1024]{0:T(1024)}, u32[]{:S(2)}) copy-start(s32[1024]{0:T(1024)} %param.17) | copy-start | bytes 12292
  2.2 328.6 %collective-permute-start.1 = (f32[4,40,128]{2,1,0:T(8,128)}, f32[4,40,128]{2,1,0:T(8,128)}, u32[]{:S(2)}, u32[]{:S(2)}) collective-permute-start(f32[4,40,128]{2,1,0:T(8,128)} %get-tuple-element.154), channel_id=1, source_target_pairs={{0,64},{64,128},{128,192},{1,65},{65,129},{129,193},{2,66},{66,130... | collective-permute-start | bytes 245768 | tf_op jit(solution)/shard_map/ppermute | solution.py:21
  5.0 326.9 %collective-permute-start = (f32[4,40,128]{2,1,0:T(8,128)S(1)}, f32[4,40,128]{2,1,0:T(8,128)}, u32[]{:S(2)}, u32[]{:S(2)}) collective-permute-start(f32[4,40,128]{2,1,0:T(8,128)S(1)} %get-tuple-element.153), channel_id=1, source_target_pairs={{64,0},{128,64},{192,128},{65,1},{129,65},{193,129},{66,2},{130,66... | collective-permute-start | bytes 245768 | tf_op jit(solution)/shard_map/ppermute | solution.py:22
  233.5 88.8 %copy-start.6 = (f32[40,40,128]{2,1,0:T(8,128)S(1)}, f32[40,40,128]{2,1,0:T(8,128)}, u32[]{:S(2)}) copy-start(f32[40,40,128]{2,1,0:T(8,128)} %param.10) | copy-start | bytes 2457604
  322.3 3.0 copy-start.8
  331.9 1.0 copy-start.3
  333.0 9.1 %copy-start.7 = (f32[48,40,128]{2,1,0:T(8,128)}, f32[48,40,128]{2,1,0:T(8,128)S(1)}, u32[]{:S(2)}) copy-start(f32[48,40,128]{2,1,0:T(8,128)S(1)} %get-tuple-element.160) | copy-start | bytes 2949124
  333.8 12.2 %collective-permute-start.2 = (f32[48,4,128]{2,0,1:T(8,128)}, f32[48,4,128]{2,0,1:T(8,128)}, u32[]{:S(2)}, u32[]{:S(2)}) collective-permute-start(f32[48,4,128]{2,0,1:T(8,128)} %copy.164), channel_id=1, source_target_pairs={{4,0},{8,4},{12,8},{16,12},{20,16},{24,20},{28,24},{32,28},{36,32}... | collective-permute-start | bytes 294920 | tf_op jit(solution)/shard_map/ppermute | solution.py:22
  336.5 12.6 %collective-permute-start.3 = (f32[48,4,128]{2,0,1:T(8,128)}, f32[48,4,128]{2,0,1:T(8,128)}, u32[]{:S(2)}, u32[]{:S(2)}) collective-permute-start(f32[48,4,128]{2,0,1:T(8,128)} %copy.165), channel_id=1, source_target_pairs={{0,4},{4,8},{8,12},{12,16},{16,20},{20,24},{24,28},{28,32},{32,36}... | collective-permute-start | bytes 294920 | tf_op jit(solution)/shard_map/ppermute | solution.py:21
  346.0 41.4 %copy-start = (f32[48,40,128]{1,0,2:T(8,128)}, f32[48,40,128]{1,0,2:T(8,128)S(1)}, u32[]{:S(2)}) copy-start(f32[48,40,128]{1,0,2:T(8,128)S(1)} %copy.132) | copy-start | bytes 2949124
  352.2 9.1 %copy-start.4 = (f32[44,40,128]{2,1,0:T(8,128)S(1)}, f32[44,40,128]{2,1,0:T(8,128)}, u32[]{:S(2)}) copy-start(f32[44,40,128]{2,1,0:T(8,128)} %copy-done.3) | copy-start | bytes 2703364
  354.2 33.2 %collective-permute-start.4 = (f32[48,48,4]{1,0,2:T(8,128)}, f32[48,48,4]{1,0,2:T(8,128)}, u32[]{:S(2)}, u32[]{:S(2)}) collective-permute-start(f32[48,48,4]{1,0,2:T(8,128)} %get-tuple-element.130), channel_id=1, source_target_pairs={{1,0},{2,1},{3,2},{5,4},{6,5},{7,6},{9,8},{10,9},{11,10},{13,12},{... | collective-permute-start | bytes 110600 | tf_op jit(solution)/shard_map/ppermute | solution.py:22
  356.5 30.8 %collective-permute-start.5 = (f32[48,48,4]{1,0,2:T(8,128)}, f32[48,48,4]{1,0,2:T(8,128)}, u32[]{:S(2)}, u32[]{:S(2)}) collective-permute-start(f32[48,48,4]{1,0,2:T(8,128)} %get-tuple-element.131), channel_id=1, source_target_pairs={{0,1},{1,2},{2,3},{4,5},{5,6},{6,7},{8,9},{9,10},{10,11},{12,13},{... | collective-permute-start | bytes 110600 | tf_op jit(solution)/shard_map/ppermute | solution.py:21
  439.7 9.0 %collective-permute-start.6 = (f32[4,40,128]{1,0,2:T(4,128)S(1)}, f32[4,40,128]{1,0,2:T(4,128)S(1)}, u32[]{:S(2)}, u32[]{:S(2)}) collective-permute-start(f32[4,40,128]{1,0,2:T(4,128)S(1)} %get-tuple-element.137), channel_id=1, source_target_pairs={{64,0},{128,64},{192,128},{65,1},{129,65},{193,129},{66,2},{130,66... | collective-permute-start | bytes 245768 | tf_op jit(solution)/shard_map/ppermute | solution.py:22
  442.5 9.0 %collective-permute-start.7 = (f32[4,40,128]{1,0,2:T(4,128)S(1)}, f32[4,40,128]{1,0,2:T(4,128)S(1)}, u32[]{:S(2)}, u32[]{:S(2)}) collective-permute-start(f32[4,40,128]{1,0,2:T(4,128)S(1)} %get-tuple-element.136), channel_id=1, source_target_pairs={{0,64},{64,128},{128,192},{1,65},{65,129},{129,193},{2,66},{66,130... | collective-permute-start | bytes 245768 | tf_op jit(solution)/shard_map/ppermute | solution.py:21
  458.7 21.5 %collective-permute-start.8 = (f32[48,4,128]{2,0,1:T(8,128)}, f32[48,4,128]{2,0,1:T(8,128)}, u32[]{:S(2)}, u32[]{:S(2)}) collective-permute-start(f32[48,4,128]{2,0,1:T(8,128)} %copy.143), channel_id=1, source_target_pairs={{4,0},{8,4},{12,8},{16,12},{20,16},{24,20},{28,24},{32,28},{36,32}... | collective-permute-start | bytes 294920 | tf_op jit(solution)/shard_map/ppermute | solution.py:22
  463.7 19.6 %collective-permute-start.9 = (f32[48,4,128]{2,0,1:T(8,128)}, f32[48,4,128]{2,0,1:T(8,128)}, u32[]{:S(2)}, u32[]{:S(2)}) collective-permute-start(f32[48,4,128]{2,0,1:T(8,128)} %copy.145), channel_id=1, source_target_pairs={{0,4},{4,8},{8,12},{12,16},{16,20},{20,24},{24,28},{28,32},{32,36}... | collective-permute-start | bytes 294920 | tf_op jit(solution)/shard_map/ppermute | solution.py:21
  486.3 8.6 %copy-start.1 = (f32[48,4,128]{1,0,2:T(8,128)S(1)}, f32[48,4,128]{1,0,2:T(8,128)}, u32[]{:S(2)}) copy-start(f32[48,4,128]{1,0,2:T(8,128)} %copy.144) | copy-start | bytes 294916
  486.3 8.6 %copy-start.2 = (f32[48,4,128]{1,0,2:T(8,128)S(1)}, f32[48,4,128]{1,0,2:T(8,128)}, u32[]{:S(2)}) copy-start(f32[48,4,128]{1,0,2:T(8,128)} %copy.146) | copy-start | bytes 294916
  487.6 9.7 %collective-permute-start.10 = (f32[48,48,4]{1,0,2:T(8,128)S(1)}, f32[48,48,4]{1,0,2:T(8,128)S(1)}, u32[]{:S(2)}, u32[]{:S(2)}) collective-permute-start(f32[48,48,4]{1,0,2:T(8,128)S(1)} %get-tuple-element.126), channel_id=1, source_target_pairs={{1,0},{2,1},{3,2},{5,4},{6,5},{7,6},{9,8},{10,9},{11,10},{13,12},{... | collective-permute-start | bytes 110600 | tf_op jit(solution)/shard_map/ppermute | solution.py:22
  490.0 7.3 %collective-permute-start.11 = (f32[48,48,4]{1,0,2:T(8,128)S(1)}, f32[48,48,4]{1,0,2:T(8,128)S(1)}, u32[]{:S(2)}, u32[]{:S(2)}) collective-permute-start(f32[48,48,4]{1,0,2:T(8,128)S(1)} %get-tuple-element.127), channel_id=1, source_target_pairs={{0,1},{1,2},{2,3},{4,5},{5,6},{6,7},{8,9},{9,10},{10,11},{12,13},{... | collective-permute-start | bytes 110600 | tf_op jit(solution)/shard_map/ppermute | solution.py:21
  522.0 3.2 copy-start.5
where the time goes:
time: 537 us; the launch traced here: 527 us
  blocking collectives  224 us (42%)
  other arithmetic  87 us (16%)
  local copies, waits for them, and re-layouts  85.3 us (16%)
  matrix products  83.2 us (15%)
  starting transfers between devices  39.1 us (7%)
  waiting for transfers between devices  6.29 us (1%)
    dot_general x16, matrix products, accumulate(): lax.dot_general(pick_plane, weighted, (((0,), (0,)), ((), ())), preferred...  83.2 us
    all_gather x1, blocking collectives, on_device(): lax.all_gather(rec_owner, ('gy', 'gz'), axis=0, tiled=True)  75.7 us
    all_gather x1, blocking collectives, on_device(): lax.all_gather(rec_cell, ('gy', 'gz'), axis=0, tiled=True)  75.1 us
    all_gather x1, blocking collectives, on_device(): lax.all_gather(traces, ('gy', 'gz'), axis=1, tiled=True)  73.3 us
    unnamed x40, local copies, waits for them, and re-layouts  49.5 us
    add x1, other arithmetic, on_device(): 2.0 * current - previous + courant * (laplacian(current) + sources[step])  43.7 us
    ppermute x6, starting transfers between devices, padded_2(): before = lax.ppermute(last, axis, up)  25.2 us
    concatenate x4, other arithmetic, padded_2(): value = jnp.concatenate([before, value, after], axis=dim)  18.3 us
  transfers between devices with their start and end apart: 12, of which 2 were waited for; matrix products, arithmetic and copies ran while one was open for 29% of the time, Pallas kernels for 0%

commit v1 on v0

v1 whole, which is shorter than its diff:
```python
import functools

import jax
import jax.numpy as jnp
from jax import lax
from jax.experimental import pallas as pl
from jax.experimental.pallas import tpu as pltpu
from jax.sharding import PartitionSpec as P

COEFFS = (-205.0 / 72.0, 8.0 / 5.0, -1.0 / 5.0, 8.0 / 315.0, -1.0 / 560.0)
SURF = 8
CAP = 64
F32 = jnp.float32
BF16 = jnp.bfloat16
NT = (((1,), (1,)), ((), ()))
TN = (((0,), (0,)), ((), ()))


def split3(value):
    high = value.astype(BF16).astype(F32)
    rest = value - high
    middle = rest.astype(BF16).astype(F32)
    return high, middle, rest - middle


def iota(shape, dim):
    return lax.broadcasted_iota(jnp.int32, shape, dim)


def pack_kernel(n_gx, n_gy, n_gz, traces_ref, owner_ref, cell_ref, out_ref):
    me = lax.axis_index("gx")
    chunks = owner_ref.shape[0]
    owner_ids = iota((n_gy, 128), 0)
    picks = []
    for c in range(chunks):
        owner = owner_ref[c : c + 1, :]
        local = owner - me * (n_gy * n_gz)
        dest = lax.shift_right_arithmetic(local, n_gz.bit_length() - 1)
        picks.append(jnp.where(owner_ids == dest, 1.0, 0.0).astype(F32))
    all_picks = jnp.concatenate(picks, axis=0)
    before = (iota((128, 128), 0) < iota((128, 128), 1)).astype(F32).astype(BF16)
    prefix = jnp.dot(all_picks.astype(BF16), before, preferred_element_type=F32)
    offset = jnp.zeros((n_gy, 1), F32)
    slot_ids = iota((128, 128), 0)
    slots_low, slots_high, left, right = [], [], [], []
    for c in range(chunks):
        pick = picks[c]
        rank = jnp.sum(pick * (prefix[c * n_gy : (c + 1) * n_gy] + offset), axis=0, keepdims=True)
        offset = offset + jnp.sum(pick, axis=1, keepdims=True)
        rank = rank.astype(jnp.int32)
        slots_low.append(jnp.where(slot_ids == rank, 1.0, 0.0).astype(BF16))
        slots_high.append(jnp.where(slot_ids == rank + CAP, 1.0, 0.0).astype(BF16))
        first = traces_ref[0:1, c * 128 : (c + 1) * 128]
        second = traces_ref[1:2, c * 128 : (c + 1) * 128]
        cell = cell_ref[c : c + 1, :].astype(F32)
        left.append(
            jnp.concatenate([pick * s for s in split3(first) + split3(cell)], axis=0).astype(BF16)
        )
        right.append(jnp.concatenate([pick * s for s in split3(second)], axis=0).astype(BF16))
    low = jnp.concatenate(slots_low, axis=1)
    high = jnp.concatenate(slots_high, axis=1)
    left = lax.dot_general(jnp.concatenate(left, axis=1), low, NT, preferred_element_type=F32)
    right = lax.dot_general(jnp.concatenate(right, axis=1), high, NT, preferred_element_type=F32)

    def joined(value, at):
        parts = [value[(at + i) * n_gy : (at + i + 1) * n_gy] for i in range(3)]
        return parts[0] + parts[1] + parts[2]

    values = joined(left, 0) + joined(right, 0)
    cells = joined(left, 3)
    out_ref[...] = jnp.zeros_like(out_ref)
    for d in range(n_gy):
        out_ref[d, 0:1, :] = values[d : d + 1, :]
        out_ref[d, 1:2, :] = cells[d : d + 1, :]


def store_faces(read, cx, cy, xlo_ref, xhi_ref, ylo_ref, yhi_ref):
    half = cx // 2
    for i in range(4):
        xlo_ref[i] = read(i)
        xhi_ref[i] = read(cx - 4 + i)
    for x in range(half):
        one, two = read(x), read(x + half)
        ylo_ref[x] = jnp.concatenate([one[0:4], two[0:4]], axis=0)
        yhi_ref[x] = jnp.concatenate([one[cy - 4 : cy], two[cy - 4 : cy]], axis=0)


def depth_faces(value):
    rows = value.shape[0]
    at = iota((8, 128), 0)
    take = iota((8, 128), 1) == jnp.where(at < 4, at, at + 120)
    take = jnp.where(take, 1.0, 0.0).astype(BF16)
    parts = [
        lax.dot_general(take, s.astype(BF16), NT, preferred_element_type=F32) for s in split3(value)
    ]
    return parts[0] + parts[1] + parts[2]


def faces_kernel(now_ref, xlo_ref, xhi_ref, ylo_ref, yhi_ref, z_ref):
    cx, cy, cz = now_ref.shape
    store_faces(lambda x: now_ref[x], cx, cy, xlo_ref, xhi_ref, ylo_ref, yhi_ref)
    z_ref[...] = depth_faces(now_ref[...].reshape(cx * cy, cz))


def bin_records(recv_ref, cx, cy, cz):
    senders = recv_ref.shape[0]
    half = senders // 2
    values = recv_ref[:, 0, :]
    cells = recv_ref[:, 1, :]
    low = iota((half, 128), 1) < CAP
    rolled = pltpu.roll(values, CAP, 1)
    first = jnp.where(low, values[:half], rolled[half:])
    second = jnp.where(low, rolled[:half], values[half:])
    cell = jnp.where(low, cells[:half], pltpu.roll(cells, CAP, 1)[half:]).astype(jnp.int32)
    depth = lax.bitwise_and(cell, cz - 1)
    plane = lax.shift_right_logical(cell, cz.bit_length() - 1)
    at_x = plane // cy
    at_y = plane - at_x * cy
    column = at_x * SURF + depth
    columns = -(-cx * SURF // 128) * 128
    pieces = split3(first) + split3(second)
    row_ids = iota((cy, 128), 0)
    column_ids = iota((columns, 128), 0)
    total = None
    step = 4
    for begin in range(0, half, step):
        lefts, rights = [], []
        for s in range(begin, begin + step):
            hit = row_ids == at_y[s : s + 1]
            lefts.append(
                jnp.concatenate([jnp.where(hit, p[s : s + 1], 0.0) for p in pieces], axis=0).astype(BF16)
            )
            rights.append(jnp.where(column_ids == column[s : s + 1], 1.0, 0.0).astype(BF16))
        term = lax.dot_general(
            jnp.concatenate(lefts, axis=1), jnp.concatenate(rights, axis=1), NT,
            preferred_element_type=F32,
        )
        total = term if total is None else total + term
    part = [total[i * cy : (i + 1) * cy] for i in range(6)]
    return part[0] + part[1] + part[2], part[3] + part[4] + part[5]


def fill_padded(pad_ref, now_ref, xb_ref, xa_ref, yb_ref, ya_ref):
    cx, cy, cz = now_ref.shape
    half = cx // 2
    pad_ref[4 : 4 + cx, 8 : 8 + cy, :] = now_ref[...]
    pad_ref[0:4, 8 : 8 + cy, :] = xb_ref[...]
    pad_ref[4 + cx : 8 + cx, 8 : 8 + cy, :] = xa_ref[...]
    pad_ref[4 : 4 + half, 4:8, :] = yb_ref[:, 0:4, :]
    pad_ref[4 + half : 4 + cx, 4:8, :] = yb_ref[:, 4:8, :]
    pad_ref[4 : 4 + half, 8 + cy : 12 + cy, :] = ya_ref[:, 0:4, :]
    pad_ref[4 + half : 4 + cx, 8 + cy : 12 + cy, :] = ya_ref[:, 4:8, :]


def depth_correction(own, below, above):
    at = iota(own.shape, 0)
    delta = jnp.where(at < 4, above, below) - own
    row = iota((8, 128), 0)
    lane = iota((8, 128), 1)
    distance = jnp.where(row < 4, 128 + row - lane, lane + 8 - row)
    weight = jnp.zeros((8, 128), F32)
    for j in range(1, 5):
        weight = jnp.where(distance == j, COEFFS[j], weight)
    return lax.dot_general(
        delta, weight, TN, precision=lax.Precision.HIGHEST, preferred_element_type=F32
    )


def lap_at(pad_ref, zc_ref, x, cy):
    center = pad_ref[x + 4, 8 : 8 + cy, :]
    total = (3.0 * COEFFS[0]) * center + zc_ref[x]
    for j in range(1, 5):
        pair = pad_ref[x + 4 - j, 8 : 8 + cy, :] + pad_ref[x + 4 + j, 8 : 8 + cy, :]
        pair = pair + (pad_ref[x + 4, 8 - j : 8 - j + cy, :] + pad_ref[x + 4, 8 + j : 8 + j + cy, :])
        pair = pair + (pltpu.roll(center, j, 1) + pltpu.roll(center, 128 - j, 1))
        total = total + COEFFS[j] * pair
    return center, total


def source_at(sources, x, low):
    group, shift = x // 16, (x % 16) * SURF
    piece = sources[:, group * 128 : (group + 1) * 128]
    if shift:
        piece = pltpu.roll(piece, 128 - shift, 1)
    return jnp.where(low, piece, 0.0)


def first_kernel(
    recv_ref, now_ref, late_ref, courant_ref, forward_ref, image_ref,
    xb_ref, xa_ref, yb_ref, ya_ref, z_ref, zb_ref, za_ref,
    fresh_ref, image_out_ref, source_ref, xlo_ref, xhi_ref, ylo_ref, yhi_ref, zf_ref,
    pad_ref, zc_ref,
):
    cx, cy, cz = now_ref.shape
    fill_padded(pad_ref, now_ref, xb_ref, xa_ref, yb_ref, ya_ref)
    zc_ref[...] = depth_correction(z_ref[...], zb_ref[...], za_ref[...]).reshape(cx, cy, cz)
    sources, later = bin_records(recv_ref, cx, cy, cz)
    source_ref[...] = later
    low = iota((cy, cz), 1) < SURF
    for x in range(cx):
        center, lap = lap_at(pad_ref, zc_ref, x, cy)
        lap = lap + source_at(sources, x, low)
        fresh = 2.0 * center - late_ref[x] + courant_ref[x] * lap
        fresh_ref[x] = fresh
        image_out_ref[x] = image_ref[x] + forward_ref[0, x].astype(F32) * fresh
    store_faces(lambda x: fresh_ref[x], cx, cy, xlo_ref, xhi_ref, ylo_ref, yhi_ref)
    zf_ref[...] = depth_faces(fresh_ref[...].reshape(cx * cy, cz))


def second_kernel(
    now_ref, late_ref, courant_ref, forward_ref, image_ref, source_ref,
    xb_ref, xa_ref, yb_ref, ya_ref, z_ref, zb_ref, za_ref,
    fresh_ref, image_out_ref,
    pad_ref, zc_ref,
):
    cx, cy, cz = now_ref.shape
    fill_padded(pad_ref, now_ref, xb_ref, xa_ref, yb_ref, ya_ref)
    zc_ref[...] = depth_correction(z_ref[...], zb_ref[...], za_ref[...]).reshape(cx, cy, cz)
    sources = source_ref[...]
    low = iota((cy, cz), 1) < SURF
    for x in range(cx):
        center, lap = lap_at(pad_ref, zc_ref, x, cy)
        lap = lap + source_at(sources, x, low)
        fresh = 2.0 * center - late_ref[x] + courant_ref[x] * lap
        fresh_ref[x] = fresh
        image_out_ref[x] = image_ref[x] + forward_ref[1, x].astype(F32) * fresh


def shift(value, axis, by):
    count = lax.axis_size(axis)
    pairs = [(i, i + by) for i in range(count) if 0 <= i + by < count]
    return lax.ppermute(value, axis, pairs)


def exchange(faces):
    xlo, xhi, ylo, yhi, z = faces
    yb, ya = shift(yhi, "gy", 1), shift(ylo, "gy", -1)
    xb, xa = shift(xhi, "gx", 1), shift(xlo, "gx", -1)
    zb, za = shift(z, "gz", 1), shift(z, "gz", -1)
    return xb, xa, yb, ya, z, zb, za


def struct(*shape):
    return jax.ShapeDtypeStruct(shape, F32)


def call(kernel, outs, flops, args, scratch=()):
    vmem = pl.BlockSpec(memory_space=pltpu.VMEM)
    size = sum(a.size * a.dtype.itemsize for a in args) + sum(o.size * 4 for o in outs)
    return pl.pallas_call(
        kernel,
        out_shape=outs,
        in_specs=[vmem] * len(args),
        out_specs=[vmem] * len(outs),
        scratch_shapes=list(scratch),
        compiler_params=pltpu.CompilerParams(vmem_limit_bytes=40 * 2**20),
        cost_estimate=pl.CostEstimate(flops=flops, bytes_accessed=size, transcendentals=0),
    )(*args)


def on_device(adjoint_now, adjoint_late, courant, forward, image_in, traces, rec_owner, rec_cell):
    cx, cy, cz = adjoint_now.shape
    n_gx, n_gy, n_gz = (lax.axis_size(a) for a in ("gx", "gy", "gz"))
    chunks = rec_owner.shape[0] // 128
    block = struct(cx, cy, cz)
    faces = (
        struct(4, cy, cz), struct(4, cy, cz),
        struct(cx // 2, 8, cz), struct(cx // 2, 8, cz), struct(8, cx * cy),
    )
    (packed,) = call(
        functools.partial(pack_kernel, n_gx, n_gy, n_gz),
        (struct(n_gy * n_gz, 2, 128),), 10**7,
        (traces, rec_owner.reshape(chunks, 128), rec_cell.reshape(chunks, 128)),
    )
    received = lax.all_to_all(packed, ("gz", "gy"), 0, 0)
    halo = exchange(call(faces_kernel, faces, 10**7, (adjoint_now,)))
    scratch = (pltpu.VMEM((cx + 8, cy + 16, cz), F32), pltpu.VMEM((cx, cy, cz), F32))
    columns = -(-cx * SURF // 128) * 128
    middle, image, later, *out_faces = call(
        first_kernel, (block, block, struct(cy, columns)) + faces, 10**8,
        (received, adjoint_now, adjoint_late, courant, forward, image_in) + halo, scratch,
    )
    halo = exchange(out_faces)
    newest, image = call(
        second_kernel, (block, block), 10**8,
        (middle, adjoint_now, courant, forward, image, later) + halo, scratch,
    )
    return newest, middle, image


def solution(mesh):
    grid = P("gx", "gy", "gz")
    return jax.shard_map(
        on_device,
        mesh=mesh,
        in_specs=(
            grid, grid, grid, P(None, "gx", "gy", "gz"), grid,
            P(None, ("gy", "gz")), P(("gy", "gz")), P(("gy", "gz")),
        ),
        out_specs=(grid, grid, grid),
        check_vma=False,
    )
```

time: 537 us -> 78.4 us (0.15)
  the two profiles are of different devices: /device:TPU:101 before, /device:TPU:30 now
where the time goes in v1:
time: 78.4 us; the launch traced here: 77.6 us
  starting transfers between devices  48.4 us (62%)
  waiting for transfers between devices  10.1 us (13%)
  Pallas kernels  9.41 us (12%)
  local copies, waits for them, and re-layouts  8.92 us (11%)
  between operations  0.84 us (1%)
    ppermute x12, starting transfers between devices, shift(): return lax.ppermute(value, axis, pairs)  36.3 us
    all_to_all x1, starting transfers between devices, on_device(): received = lax.all_to_all(packed, ('gz', 'gy'), 0, 0)  12 us
    ppermute x12, waiting for transfers between devices, shift(): return lax.ppermute(value, axis, pairs)  10.1 us
    pallas_call x4, Pallas kernels, call(): pl.pallas_call(kernel, out_shape=outs, in_specs=[vmem] * len(args), out_s...  9.41 us
    unnamed x22, local copies, waits for them, and re-layouts  8.92 us
  transfers between devices with their start and end apart: 13, of which 2 were waited for; matrix products, arithmetic and copies ran while one was open for 0% of the time, Pallas kernels for 1%

profile of v1, /device:TPU:30, one launch (start us, length us, event | category | flops | bytes accessed | tf_op | source)
XLA Modules:
  0.0 77.6 jit_solution(16261074417754826852)
XLA Ops:
  2.7 1.1 %shard_map.103 = f32[64,2,128]{2,1,0:T(2,128)} custom-call(f32[2,1024]{1,0:T(2,128)S(1)} %copy-done.8, s32[8,128]{1,0:T(8,128)S(1)} %bitcast.2, s32[8,128]{1,0:T(8,128)S(1)} %bitcast.3), custom_call_target="tpu_custom_call" | custom-call | flops 10000000 | bytes 81920 | tf_op jit(solution)/shard_map/pallas_call | solution.py:250
  3.8 12.0 %all-to-all-start = ((f32[64,2,128]{2,1,0:T(2,128)}), f32[64,2,128]{2,1,0:T(2,128)S(1)}, u32[]{:S(2)}, u32[]{:S(2)}) async-start(f32[64,2,128]{2,1,0:T(2,128)} %shard_map.103), calls=%async_computation | async-start | bytes 131072 | tf_op jit(solution)/shard_map/all_to_all | solution.py:275
  15.8 1.1 %copy-done = f32[40,40,128]{2,1,0:T(8,128)S(1)} copy-done((f32[40,40,128]{2,1,0:T(8,128)S(1)}, f32[40,40,128]{2,1,0:T(8,128)}, u32[]{:S(2)}) %copy-start) | copy-done | bytes 819224
  17.4 3.0 %collective-permute-start.5 = (f32[8,1600]{1,0:T(8,128)S(1)}, f32[8,1600]{1,0:T(8,128)S(1)}, u32[]{:S(2)}, u32[]{:S(2)}) collective-permute-start(f32[8,1600]{1,0:T(8,128)S(1)} %get-tuple-element.22.z_ref), channel_id=1, source_target_pairs={{1,0},{2,1},{3,2},{5,4},{6,5},{7,6},{9,8},{10,9},{11,10},{13,12},{... | collective-permute-start | bytes 153608 | tf_op jit(solution)/shard_map/ppermute | solution.py:232
  20.4 1.3 %collective-permute-start = (f32[4,40,128]{2,1,0:T(8,128)S(1)}, f32[4,40,128]{2,1,0:T(8,128)S(1)}, u32[]{:S(2)}, u32[]{:S(2)}) collective-permute-start(f32[4,40,128]{2,1,0:T(8,128)S(1)} %get-tuple-element.18), channel_id=1, source_target_pairs={{0,64},{64,128},{128,192},{1,65},{65,129},{129,193},{2,66},{66,130... | collective-permute-start | bytes 245768 | tf_op jit(solution)/shard_map/ppermute | solution.py:232
  21.7 4.6 %collective-permute-start.1 = (f32[4,40,128]{2,1,0:T(8,128)S(1)}, f32[4,40,128]{2,1,0:T(8,128)S(1)}, u32[]{:S(2)}, u32[]{:S(2)}) collective-permute-start(f32[4,40,128]{2,1,0:T(8,128)S(1)} %get-tuple-element.19), channel_id=1, source_target_pairs={{64,0},{128,64},{192,128},{65,1},{129,65},{193,129},{66,2},{130,66... | collective-permute-start | bytes 245768 | tf_op jit(solution)/shard_map/ppermute | solution.py:232
  26.3 3.4 %collective-permute-start.2 = (f32[20,8,128]{2,1,0:T(8,128)S(1)}, f32[20,8,128]{2,1,0:T(8,128)S(1)}, u32[]{:S(2)}, u32[]{:S(2)}) collective-permute-start(f32[20,8,128]{2,1,0:T(8,128)S(1)} %get-tuple-element.20), channel_id=1, source_target_pairs={{0,4},{4,8},{8,12},{12,16},{16,20},{20,24},{24,28},{28,32},{32,36}... | collective-permute-start | bytes 245768 | tf_op jit(solution)/shard_map/ppermute | solution.py:232
  29.7 4.6 %collective-permute-start.3 = (f32[20,8,128]{2,1,0:T(8,128)S(1)}, f32[20,8,128]{2,1,0:T(8,128)S(1)}, u32[]{:S(2)}, u32[]{:S(2)}) collective-permute-start(f32[20,8,128]{2,1,0:T(8,128)S(1)} %get-tuple-element.21), channel_id=1, source_target_pairs={{4,0},{8,4},{12,8},{16,12},{20,16},{24,20},{28,24},{32,28},{36,32}... | collective-permute-start | bytes 245768 | tf_op jit(solution)/shard_map/ppermute | solution.py:232
  34.3 1.9 %collective-permute-start.4 = (f32[8,1600]{1,0:T(8,128)S(1)}, f32[8,1600]{1,0:T(8,128)S(1)}, u32[]{:S(2)}, u32[]{:S(2)}) collective-permute-start(f32[8,1600]{1,0:T(8,128)S(1)} %get-tuple-element.22.z_ref), channel_id=1, source_target_pairs={{0,1},{1,2},{2,3},{4,5},{5,6},{6,7},{8,9},{9,10},{10,11},{12,13},{... | collective-permute-start | bytes 153608 | tf_op jit(solution)/shard_map/ppermute | solution.py:232
  36.2 5.0 %collective-permute-done.4.zb_ref = f32[8,1600]{1,0:T(8,128)S(1)} collective-permute-done((f32[8,1600]{1,0:T(8,128)S(1)}, f32[8,1600]{1,0:T(8,128)S(1)}, u32[]{:S(2)}, u32[]{:S(2)}) %collective-permute-start.4) | collective-permute-done | bytes 51232 | tf_op jit(solution)/shard_map/ppermute | solution.py:232
  41.3 1.1 %copy-done.2 = f32[40,40,128]{2,1,0:T(8,128)S(1)} copy-done((f32[40,40,128]{2,1,0:T(8,128)S(1)}, f32[40,40,128]{2,1,0:T(8,128)}, u32[]{:S(2)}) %copy-start.2) | copy-done | bytes 819224
  42.4 1.1 %copy-done.3 = bf16[2,40,40,128]{3,2,1,0:T(8,128)(2,1)S(1)} copy-done((bf16[2,40,40,128]{3,2,1,0:T(8,128)(2,1)S(1)}, bf16[2,40,40,128]{3,2,1,0:T(8,128)(2,1)}, u32[]{:S(2)}) %copy-start.3) | copy-done | bytes 819224
  43.6 1.1 %copy-done.6 = f32[40,40,128]{2,1,0:T(8,128)S(1)} copy-done((f32[40,40,128]{2,1,0:T(8,128)S(1)}, f32[40,40,128]{2,1,0:T(8,128)}, u32[]{:S(2)}) %copy-start.6) | copy-done | bytes 819224
  44.7 1.1 %copy-done.7 = f32[40,40,128]{2,1,0:T(8,128)S(1)} copy-done((f32[40,40,128]{2,1,0:T(8,128)S(1)}, f32[40,40,128]{2,1,0:T(8,128)}, u32[]{:S(2)}) %copy-start.7) | copy-done | bytes 819224
  45.9 4.2 %shard_map.105 = (f32[40,40,128]{2,1,0:T(8,128)}, f32[40,40,128]{2,1,0:T(8,128)S(1)}, f32[40,384]{1,0:T(8,128)S(1)}, f32[4,40,128]{2,1,0:T(8,128)S(1)}, f32[4,40...) custom-call(f32[64,2,128]{2,1,0:T(2,128)S(1)} %all-to-all-done.recv_ref, ...), custom_call_target="tpu_custom_call" | custom-call | flops 100000000 | bytes 6721536 | tf_op jit(solution)/shard_map/pallas_call | solution.py:250
  50.1 1.9 %collective-permute-start.11 = (f32[8,1600]{1,0:T(8,128)S(1)}, f32[8,1600]{1,0:T(8,128)S(1)}, u32[]{:S(2)}, u32[]{:S(2)}) collective-permute-start(f32[8,1600]{1,0:T(8,128)S(1)} %get-tuple-element.30.z_ref), channel_id=1, source_target_pairs={{1,0},{2,1},{3,2},{5,4},{6,5},{7,6},{9,8},{10,9},{11,10},{13,12},{... | collective-permute-start | bytes 153608 | tf_op jit(solution)/shard_map/ppermute | solution.py:232
  52.0 1.3 %collective-permute-start.6 = (f32[4,40,128]{2,1,0:T(8,128)S(1)}, f32[4,40,128]{2,1,0:T(8,128)S(1)}, u32[]{:S(2)}, u32[]{:S(2)}) collective-permute-start(f32[4,40,128]{2,1,0:T(8,128)S(1)} %get-tuple-element.26), channel_id=1, source_target_pairs={{0,64},{64,128},{128,192},{1,65},{65,129},{129,193},{2,66},{66,130... | collective-permute-start | bytes 245768 | tf_op jit(solution)/shard_map/ppermute | solution.py:232
  53.3 4.6 %collective-permute-start.7 = (f32[4,40,128]{2,1,0:T(8,128)S(1)}, f32[4,40,128]{2,1,0:T(8,128)S(1)}, u32[]{:S(2)}, u32[]{:S(2)}) collective-permute-start(f32[4,40,128]{2,1,0:T(8,128)S(1)} %get-tuple-element.27), channel_id=1, source_target_pairs={{64,0},{128,64},{192,128},{65,1},{129,65},{193,129},{66,2},{130,66... | collective-permute-start | bytes 245768 | tf_op jit(solution)/shard_map/ppermute | solution.py:232
  57.8 1.9 %collective-permute-start.8 = (f32[20,8,128]{2,1,0:T(8,128)S(1)}, f32[20,8,128]{2,1,0:T(8,128)S(1)}, u32[]{:S(2)}, u32[]{:S(2)}) collective-permute-start(f32[20,8,128]{2,1,0:T(8,128)S(1)} %get-tuple-element.28), channel_id=1, source_target_pairs={{0,4},{4,8},{8,12},{12,16},{16,20},{20,24},{24,28},{28,32},{32,36}... | collective-permute-start | bytes 245768 | tf_op jit(solution)/shard_map/ppermute | solution.py:232
  59.8 6.0 %collective-permute-start.9 = (f32[20,8,128]{2,1,0:T(8,128)S(1)}, f32[20,8,128]{2,1,0:T(8,128)S(1)}, u32[]{:S(2)}, u32[]{:S(2)}) collective-permute-start(f32[20,8,128]{2,1,0:T(8,128)S(1)} %get-tuple-element.29), channel_id=1, source_target_pairs={{4,0},{8,4},{12,8},{16,12},{20,16},{24,20},{28,24},{32,28},{36,32}... | collective-permute-start | bytes 245768 | tf_op jit(solution)/shard_map/ppermute | solution.py:232
  65.8 1.9 %collective-permute-start.10 = (f32[8,1600]{1,0:T(8,128)S(1)}, f32[8,1600]{1,0:T(8,128)S(1)}, u32[]{:S(2)}, u32[]{:S(2)}) collective-permute-start(f32[8,1600]{1,0:T(8,128)S(1)} %get-tuple-element.30.z_ref), channel_id=1, source_target_pairs={{0,1},{1,2},{2,3},{4,5},{5,6},{6,7},{8,9},{9,10},{10,11},{12,13},{... | collective-permute-start | bytes 153608 | tf_op jit(solution)/shard_map/ppermute | solution.py:232
  67.7 5.0 %collective-permute-done.10.zb_ref = f32[8,1600]{1,0:T(8,128)S(1)} collective-permute-done((f32[8,1600]{1,0:T(8,128)S(1)}, f32[8,1600]{1,0:T(8,128)S(1)}, u32[]{:S(2)}, u32[]{:S(2)}) %collective-permute-start.10) | collective-permute-done | bytes 51232 | tf_op jit(solution)/shard_map/ppermute | solution.py:232
  72.8 1.1 %copy-done.5 = f32[40,40,128]{2,1,0:T(8,128)S(1)} copy-done((f32[40,40,128]{2,1,0:T(8,128)S(1)}, f32[40,40,128]{2,1,0:T(8,128)}, u32[]{:S(2)}) %copy-start.5) | copy-done | bytes 819224
  73.9 3.7 %shard_map.106 = (f32[40,40,128]{2,1,0:T(8,128)}, f32[40,40,128]{2,1,0:T(8,128)}) custom-call(f32[40,40,128]{2,1,0:T(8,128)S(1)} %copy-done.5, f32[40,40,128]{2,1,0:T(8,128)S(1)} %copy-done.1, f32[40,40,128]{2,1,0:T(8,128)S(1)} %copy-done.2, bf16[2,40,40,128]{3,2,1,0:T(8,128)(2,1)S(1)} %copy-done.4, f32[40,40,128]{2,1,0:T(8,128)S(1)} %get-tuple-element.24.image_ref, ...), custom_call_target="tpu_custom_call" | custom-call | flops 100000000 | bytes 6277120 | tf_op jit(solution)/shard_map/pallas_call | solution.py:250
  (28 shorter events, 2.6 us)
Async XLA Ops:
  0.6 0.7 copy-start.8
  1.3 0.7 copy-start.9
  2.0 0.7 copy-start.10
  3.8 37.5 %all-to-all-start = ((f32[64,2,128]{2,1,0:T(2,128)}), f32[64,2,128]{2,1,0:T(2,128)S(1)}, u32[]{:S(2)}, u32[]{:S(2)}) async-start(f32[64,2,128]{2,1,0:T(2,128)} %shard_map.103), calls=%async_computation | async-start | bytes 131072 | tf_op jit(solution)/shard_map/all_to_all | solution.py:275
  15.8 1.1 %copy-start = (f32[40,40,128]{2,1,0:T(8,128)S(1)}, f32[40,40,128]{2,1,0:T(8,128)}, u32[]{:S(2)}) copy-start(f32[40,40,128]{2,1,0:T(8,128)} %late_ref.3) | copy-start | bytes 2457604
  17.0 24.3 %copy-start.1 = (f32[40,40,128]{2,1,0:T(8,128)S(1)}, f32[40,40,128]{2,1,0:T(8,128)}, u32[]{:S(2)}) copy-start(f32[40,40,128]{2,1,0:T(8,128)} %late_ref.3) | copy-start | bytes 2457604
  17.4 16.8 %collective-permute-start.5 = (f32[8,1600]{1,0:T(8,128)S(1)}, f32[8,1600]{1,0:T(8,128)S(1)}, u32[]{:S(2)}, u32[]{:S(2)}) collective-permute-start(f32[8,1600]{1,0:T(8,128)S(1)} %get-tuple-element.22.z_ref), channel_id=1, source_target_pairs={{1,0},{2,1},{3,2},{5,4},{6,5},{7,6},{9,8},{10,9},{11,10},{13,12},{... | collective-permute-start | bytes 153608 | tf_op jit(solution)/shard_map/ppermute | solution.py:232
  20.4 20.8 %collective-permute-start = (f32[4,40,128]{2,1,0:T(8,128)S(1)}, f32[4,40,128]{2,1,0:T(8,128)S(1)}, u32[]{:S(2)}, u32[]{:S(2)}) collective-permute-start(f32[4,40,128]{2,1,0:T(8,128)S(1)} %get-tuple-element.18), channel_id=1, source_target_pairs={{0,64},{64,128},{128,192},{1,65},{65,129},{129,193},{2,66},{66,130... | collective-permute-start | bytes 245768 | tf_op jit(solution)/shard_map/ppermute | solution.py:232
  21.7 19.5 %collective-permute-start.1 = (f32[4,40,128]{2,1,0:T(8,128)S(1)}, f32[4,40,128]{2,1,0:T(8,128)S(1)}, u32[]{:S(2)}, u32[]{:S(2)}) collective-permute-start(f32[4,40,128]{2,1,0:T(8,128)S(1)} %get-tuple-element.19), channel_id=1, source_target_pairs={{64,0},{128,64},{192,128},{65,1},{129,65},{193,129},{66,2},{130,66... | collective-permute-start | bytes 245768 | tf_op jit(solution)/shard_map/ppermute | solution.py:232
  26.3 14.9 %collective-permute-start.2 = (f32[20,8,128]{2,1,0:T(8,128)S(1)}, f32[20,8,128]{2,1,0:T(8,128)S(1)}, u32[]{:S(2)}, u32[]{:S(2)}) collective-permute-start(f32[20,8,128]{2,1,0:T(8,128)S(1)} %get-tuple-element.20), channel_id=1, source_target_pairs={{0,4},{4,8},{8,12},{12,16},{16,20},{20,24},{24,28},{28,32},{32,36}... | collective-permute-start | bytes 245768 | tf_op jit(solution)/shard_map/ppermute | solution.py:232
  29.7 11.6 %collective-permute-start.3 = (f32[20,8,128]{2,1,0:T(8,128)S(1)}, f32[20,8,128]{2,1,0:T(8,128)S(1)}, u32[]{:S(2)}, u32[]{:S(2)}) collective-permute-start(f32[20,8,128]{2,1,0:T(8,128)S(1)} %get-tuple-element.21), channel_id=1, source_target_pairs={{4,0},{8,4},{12,8},{16,12},{20,16},{24,20},{28,24},{32,28},{36,32}... | collective-permute-start | bytes 245768 | tf_op jit(solution)/shard_map/ppermute | solution.py:232
  34.3 7.0 %collective-permute-start.4 = (f32[8,1600]{1,0:T(8,128)S(1)}, f32[8,1600]{1,0:T(8,128)S(1)}, u32[]{:S(2)}, u32[]{:S(2)}) collective-permute-start(f32[8,1600]{1,0:T(8,128)S(1)} %get-tuple-element.22.z_ref), channel_id=1, source_target_pairs={{0,1},{1,2},{2,3},{4,5},{5,6},{6,7},{8,9},{9,10},{10,11},{12,13},{... | collective-permute-start | bytes 153608 | tf_op jit(solution)/shard_map/ppermute | solution.py:232
  41.3 1.1 %copy-start.2 = (f32[40,40,128]{2,1,0:T(8,128)S(1)}, f32[40,40,128]{2,1,0:T(8,128)}, u32[]{:S(2)}) copy-start(f32[40,40,128]{2,1,0:T(8,128)} %courant_ref.3) | copy-start | bytes 2457604
  42.4 1.1 %copy-start.3 = (bf16[2,40,40,128]{3,2,1,0:T(8,128)(2,1)S(1)}, bf16[2,40,40,128]{3,2,1,0:T(8,128)(2,1)}, u32[]{:S(2)}) copy-start(bf16[2,40,40,128]{3,2,1,0:T(8,128)(2,1)} %forward_ref.3) | copy-start | bytes 2457604
  43.6 1.1 %copy-start.6 = (f32[40,40,128]{2,1,0:T(8,128)S(1)}, f32[40,40,128]{2,1,0:T(8,128)}, u32[]{:S(2)}) copy-start(f32[40,40,128]{2,1,0:T(8,128)} %late_ref.2) | copy-start | bytes 2457604
  44.7 1.1 %copy-start.7 = (f32[40,40,128]{2,1,0:T(8,128)S(1)}, f32[40,40,128]{2,1,0:T(8,128)}, u32[]{:S(2)}) copy-start(f32[40,40,128]{2,1,0:T(8,128)} %image_ref.1) | copy-start | bytes 2457604
  45.8 26.9 %copy-start.4 = (bf16[2,40,40,128]{3,2,1,0:T(8,128)(2,1)S(1)}, bf16[2,40,40,128]{3,2,1,0:T(8,128)(2,1)}, u32[]{:S(2)}) copy-start(bf16[2,40,40,128]{3,2,1,0:T(8,128)(2,1)} %forward_ref.3) | copy-start | bytes 2457604
  50.1 15.7 %collective-permute-start.11 = (f32[8,1600]{1,0:T(8,128)S(1)}, f32[8,1600]{1,0:T(8,128)S(1)}, u32[]{:S(2)}, u32[]{:S(2)}) collective-permute-start(f32[8,1600]{1,0:T(8,128)S(1)} %get-tuple-element.30.z_ref), channel_id=1, source_target_pairs={{1,0},{2,1},{3,2},{5,4},{6,5},{7,6},{9,8},{10,9},{11,10},{13,12},{... | collective-permute-start | bytes 153608 | tf_op jit(solution)/shard_map/ppermute | solution.py:232
  52.0 20.8 %collective-permute-start.6 = (f32[4,40,128]{2,1,0:T(8,128)S(1)}, f32[4,40,128]{2,1,0:T(8,128)S(1)}, u32[]{:S(2)}, u32[]{:S(2)}) collective-permute-start(f32[4,40,128]{2,1,0:T(8,128)S(1)} %get-tuple-element.26), channel_id=1, source_target_pairs={{0,64},{64,128},{128,192},{1,65},{65,129},{129,193},{2,66},{66,130... | collective-permute-start | bytes 245768 | tf_op jit(solution)/shard_map/ppermute | solution.py:232
  53.3 19.5 %collective-permute-start.7 = (f32[4,40,128]{2,1,0:T(8,128)S(1)}, f32[4,40,128]{2,1,0:T(8,128)S(1)}, u32[]{:S(2)}, u32[]{:S(2)}) collective-permute-start(f32[4,40,128]{2,1,0:T(8,128)S(1)} %get-tuple-element.27), channel_id=1, source_target_pairs={{64,0},{128,64},{192,128},{65,1},{129,65},{193,129},{66,2},{130,66... | collective-permute-start | bytes 245768 | tf_op jit(solution)/shard_map/ppermute | solution.py:232
  57.8 14.9 %collective-permute-start.8 = (f32[20,8,128]{2,1,0:T(8,128)S(1)}, f32[20,8,128]{2,1,0:T(8,128)S(1)}, u32[]{:S(2)}, u32[]{:S(2)}) collective-permute-start(f32[20,8,128]{2,1,0:T(8,128)S(1)} %get-tuple-element.28), channel_id=1, source_target_pairs={{0,4},{4,8},{8,12},{12,16},{16,20},{20,24},{24,28},{28,32},{32,36}... | collective-permute-start | bytes 245768 | tf_op jit(solution)/shard_map/ppermute | solution.py:232
  59.8 13.0 %collective-permute-start.9 = (f32[20,8,128]{2,1,0:T(8,128)S(1)}, f32[20,8,128]{2,1,0:T(8,128)S(1)}, u32[]{:S(2)}, u32[]{:S(2)}) collective-permute-start(f32[20,8,128]{2,1,0:T(8,128)S(1)} %get-tuple-element.29), channel_id=1, source_target_pairs={{4,0},{8,4},{12,8},{16,12},{20,16},{24,20},{28,24},{32,28},{36,32}... | collective-permute-start | bytes 245768 | tf_op jit(solution)/shard_map/ppermute | solution.py:232
  65.8 7.0 %collective-permute-start.10 = (f32[8,1600]{1,0:T(8,128)S(1)}, f32[8,1600]{1,0:T(8,128)S(1)}, u32[]{:S(2)}, u32[]{:S(2)}) collective-permute-start(f32[8,1600]{1,0:T(8,128)S(1)} %get-tuple-element.30.z_ref), channel_id=1, source_target_pairs={{0,1},{1,2},{2,3},{4,5},{5,6},{6,7},{8,9},{9,10},{10,11},{12,13},{... | collective-permute-start | bytes 153608 | tf_op jit(solution)/shard_map/ppermute | solution.py:232
  72.8 1.1 %copy-start.5 = (f32[40,40,128]{2,1,0:T(8,128)S(1)}, f32[40,40,128]{2,1,0:T(8,128)}, u32[]{:S(2)}) copy-start(f32[40,40,128]{2,1,0:T(8,128)} %get-tuple-element.16.now_ref) | copy-start | bytes 2457604

commit v2 on v1

v2 whole, which is shorter than its diff:
```python
import functools

import jax
import jax.numpy as jnp
from jax import lax
from jax.experimental import pallas as pl
from jax.experimental.pallas import tpu as pltpu
from jax.sharding import PartitionSpec as P

COEFFS = (-205.0 / 72.0, 8.0 / 5.0, -1.0 / 5.0, 8.0 / 315.0, -1.0 / 560.0)
SURF = 8
CAP = 64
CHUNK = 20
UNROLL = 20
F32 = jnp.float32
BF16 = jnp.bfloat16
NT = (((1,), (1,)), ((), ()))
TN = (((0,), (0,)), ((), ()))


def split3(value):
    high = value.astype(BF16).astype(F32)
    rest = value - high
    middle = rest.astype(BF16).astype(F32)
    return high, middle, rest - middle


def iota(shape, dim):
    return lax.broadcasted_iota(jnp.int32, shape, dim)


def pack_records(n_gy, n_gz, traces_ref, owner_ref, cell_ref, out_ref):
    me = lax.axis_index("gx")
    chunks = owner_ref.shape[0]
    owner_ids = iota((n_gy, 128), 0)
    picks = []
    for c in range(chunks):
        owner = owner_ref[c : c + 1, :]
        local = owner - me * (n_gy * n_gz)
        dest = lax.shift_right_arithmetic(local, n_gz.bit_length() - 1)
        picks.append(jnp.where(owner_ids == dest, 1.0, 0.0).astype(F32))
    all_picks = jnp.concatenate(picks, axis=0)
    before = (iota((128, 128), 0) < iota((128, 128), 1)).astype(F32).astype(BF16)
    prefix = jnp.dot(all_picks.astype(BF16), before, preferred_element_type=F32)
    offset = jnp.zeros((n_gy, 1), F32)
    slot_ids = iota((128, 128), 0)
    slots_low, slots_high, left, right = [], [], [], []
    for c in range(chunks):
        pick = picks[c]
        rank = jnp.sum(pick * (prefix[c * n_gy : (c + 1) * n_gy] + offset), axis=0, keepdims=True)
        offset = offset + jnp.sum(pick, axis=1, keepdims=True)
        rank = rank.astype(jnp.int32)
        slots_low.append(jnp.where(slot_ids == rank, 1.0, 0.0).astype(BF16))
        slots_high.append(jnp.where(slot_ids == rank + CAP, 1.0, 0.0).astype(BF16))
        first = traces_ref[0:1, c * 128 : (c + 1) * 128]
        second = traces_ref[1:2, c * 128 : (c + 1) * 128]
        cell = cell_ref[c : c + 1, :].astype(F32)
        left.append(
            jnp.concatenate([pick * s for s in split3(first) + split3(cell)], axis=0).astype(BF16)
        )
        right.append(jnp.concatenate([pick * s for s in split3(second)], axis=0).astype(BF16))
    low = jnp.concatenate(slots_low, axis=1)
    high = jnp.concatenate(slots_high, axis=1)
    left = lax.dot_general(jnp.concatenate(left, axis=1), low, NT, preferred_element_type=F32)
    right = lax.dot_general(jnp.concatenate(right, axis=1), high, NT, preferred_element_type=F32)

    def joined(value, at):
        parts = [value[(at + i) * n_gy : (at + i + 1) * n_gy] for i in range(3)]
        return parts[0] + parts[1] + parts[2]

    values = joined(left, 0) + joined(right, 0)
    cells = joined(left, 3)
    out_ref[...] = jnp.zeros_like(out_ref)
    for d in range(n_gy):
        out_ref[d, 0:1, :] = values[d : d + 1, :]
        out_ref[d, 1:2, :] = cells[d : d + 1, :]


def is_even(axis):
    return lax.rem(lax.axis_index(axis), 2) == 0


def store_y_faces(read, half, cy, y0_ref, y1_ref, begin, end):
    y_even = is_even("gy")
    for x in range(begin, end):
        one, two = read(x), read(x + half)
        lo = jnp.concatenate([one[0:4], two[0:4]], axis=0)
        hi = jnp.concatenate([one[cy - 4 : cy], two[cy - 4 : cy]], axis=0)
        y0_ref[x] = jnp.where(y_even, hi, lo)
        y1_ref[x] = jnp.where(y_even, lo, hi)


def x_faces(ref):
    cx = ref.shape[0]
    first = jnp.where(is_even("gx"), cx - 4, 0)
    return ref.at[pl.ds(first, 4)], ref.at[pl.ds(cx - 4 - first, 4)]


class Copier:
    def __init__(self, sems):
        self.sems, self.used, self.open = sems, 0, []

    def start(self, src, dst):
        copy = pltpu.make_async_copy(src, dst, self.sems.at[self.used])
        self.used += 1
        copy.start()
        return copy

    def send(self, src, dst):
        self.open.append(self.start(src, dst))

    def close(self):
        for copy in self.open:
            copy.wait()


def depth_faces(value):
    at = iota((8, 128), 0)
    take = iota((8, 128), 1) == jnp.where(at < 4, at, at + 120)
    take = jnp.where(take, 1.0, 0.0).astype(BF16)
    parts = [
        lax.dot_general(take, s.astype(BF16), NT, preferred_element_type=F32) for s in split3(value)
    ]
    return parts[0] + parts[1] + parts[2]


def send_kernel(
    n_gy, n_gz, traces_hbm, owner_hbm, cell_hbm, now_hbm,
    packed_hbm, x0_hbm, x1_hbm, y0_hbm, y1_hbm, z_hbm,
    traces_ref, owner_ref, cell_ref, now_ref, packed_ref, y0_ref, y1_ref, z_ref, sems,
):
    cx, cy, cz = now_ref.shape
    copier = Copier(sems)
    pairs = ((traces_hbm, traces_ref), (owner_hbm, owner_ref), (cell_hbm, cell_ref))
    records = [copier.start(src, dst) for src, dst in pairs]
    now = copier.start(now_hbm, now_ref)
    for copy in records:
        copy.wait()
    pack_records(n_gy, n_gz, traces_ref, owner_ref, cell_ref, packed_ref)
    copier.send(packed_ref, packed_hbm)
    now.wait()
    for src, dst in zip(x_faces(now_ref), (x0_hbm, x1_hbm)):
        copier.send(src, dst)
    store_y_faces(lambda x: now_ref[x], cx // 2, cy, y0_ref, y1_ref, 0, cx // 2)
    copier.send(y0_ref, y0_hbm)
    copier.send(y1_ref, y1_hbm)
    z_ref[...] = depth_faces(now_ref[...].reshape(cx * cy, cz))
    copier.send(z_ref, z_hbm)
    copier.close()


def bin_records(recv_ref, cx, cy, cz):
    senders = recv_ref.shape[0]
    half = senders // 2
    values = recv_ref[:, 0, :]
    cells = recv_ref[:, 1, :]
    low = iota((half, 128), 1) < CAP
    rolled = pltpu.roll(values, CAP, 1)
    first = jnp.where(low, values[:half], rolled[half:])
    second = jnp.where(low, rolled[:half], values[half:])
    cell = jnp.where(low, cells[:half], pltpu.roll(cells, CAP, 1)[half:]).astype(jnp.int32)
    depth = lax.bitwise_and(cell, cz - 1)
    plane = lax.shift_right_logical(cell, cz.bit_length() - 1)
    at_x = plane // cy
    at_y = plane - at_x * cy
    column = at_x * SURF + depth
    columns = -(-cx * SURF // 128) * 128
    pieces = split3(first) + split3(second)
    row_ids = iota((cy, 128), 0)
    column_ids = iota((columns, 128), 0)
    total = None
    step = 4
    for begin in range(0, half, step):
        lefts, rights = [], []
        for s in range(begin, begin + step):
            hit = row_ids == at_y[s : s + 1]
            lefts.append(
                jnp.concatenate([jnp.where(hit, p[s : s + 1], 0.0) for p in pieces], axis=0).astype(BF16)
            )
            rights.append(jnp.where(column_ids == column[s : s + 1], 1.0, 0.0).astype(BF16))
        term = lax.dot_general(
            jnp.concatenate(lefts, axis=1), jnp.concatenate(rights, axis=1), NT,
            preferred_element_type=F32,
        )
        total = term if total is None else total + term
    part = [total[i * cy : (i + 1) * cy] for i in range(6)]
    return part[0] + part[1] + part[2], part[3] + part[4] + part[5]


def start_halo(copier, pad_ref, halo_hbm, halo_refs):
    cx, cy = pad_ref.shape[0] - 8, pad_ref.shape[1] - 16
    first = jnp.where(is_even("gx"), 4 + cx, 0)
    places = (
        pad_ref.at[pl.ds(first, 4), 8 : 8 + cy, :],
        pad_ref.at[pl.ds(4 + cx - first, 4), 8 : 8 + cy, :],
    ) + tuple(halo_refs)
    return [copier.start(src, dst) for src, dst in zip(halo_hbm, places)]


def fill_y(pad_ref, y0_ref, y1_ref):
    cx, cy = pad_ref.shape[0] - 8, pad_ref.shape[1] - 16
    half = cx // 2
    y_even = is_even("gy")
    for x in range(half):
        one, two = y0_ref[x], y1_ref[x]
        before, after = jnp.where(y_even, two, one), jnp.where(y_even, one, two)
        pad_ref[4 + x, 4:8, :] = before[0:4]
        pad_ref[4 + half + x, 4:8, :] = before[4:8]
        pad_ref[4 + x, 8 + cy : 12 + cy, :] = after[0:4]
        pad_ref[4 + half + x, 8 + cy : 12 + cy, :] = after[4:8]


def depth_correction(own, zero, one):
    upper = (iota(own.shape, 0) < 4) == is_even("gz")
    delta = jnp.where(upper, zero, one) - own
    row = iota((8, 128), 0)
    lane = iota((8, 128), 1)
    distance = jnp.where(row < 4, 128 + row - lane, lane + 8 - row)
    weight = jnp.zeros((8, 128), F32)
    for j in range(1, 5):
        weight = jnp.where(distance == j, COEFFS[j], weight)
    return lax.dot_general(
        delta, weight, TN, precision=lax.Precision.HIGHEST, preferred_element_type=F32
    )


def lap_at(pad_ref, zc_ref, x, cy):
    center = pad_ref[x + 4, 8 : 8 + cy, :]
    total = (3.0 * COEFFS[0]) * center + zc_ref[x]
    for j in range(1, 5):
        pair = pad_ref[x + 4 - j, 8 : 8 + cy, :] + pad_ref[x + 4 + j, 8 : 8 + cy, :]
        pair = pair + (pad_ref[x + 4, 8 - j : 8 - j + cy, :] + pad_ref[x + 4, 8 + j : 8 + j + cy, :])
        pair = pair + (pltpu.roll(center, j, 1) + pltpu.roll(center, 128 - j, 1))
        total = total + COEFFS[j] * pair
    return center, total


def spread_sources(sources, out_ref):
    for group in range(out_ref.shape[0]):
        out_ref[group] = sources[:, group * 128 : (group + 1) * 128]


def source_at(source_ref, x, low):
    piece = source_ref[x // 16]
    piece = pltpu.roll(piece, lax.rem(128 - lax.rem(x, 16) * SURF, 128), 1)
    return jnp.where(low, piece, 0.0)


def center_copy(copier, hbm, pad_ref):
    cx, cy = pad_ref.shape[0] - 8, pad_ref.shape[1] - 16
    return copier.start(hbm, pad_ref.at[4 : 4 + cx, 8 : 8 + cy, :])


def start_chunks(copier, pairs, cx):
    chunks = []
    for begin in range(0, cx, CHUNK):
        part = pl.ds(begin, CHUNK)
        chunks.append([copier.start(src.at[part], dst.at[part]) for src, dst in pairs])
    return chunks


def first_kernel(
    recv_hbm, x0_hbm, x1_hbm, y0_hbm, y1_hbm, z_hbm, z0_hbm, z1_hbm,
    now_hbm, late_hbm, courant_hbm,
    fresh_hbm, source_hbm, xs0_hbm, xs1_hbm, ys0_hbm, ys1_hbm, zs_hbm,
    recv_ref, pad_ref, y0_ref, y1_ref, z_ref, z0_ref, z1_ref, zc_ref, late_ref, courant_ref,
    fresh_ref, source_ref, later_ref, ys0_ref, ys1_ref, zs_ref, sems,
):
    cx, cy, cz = fresh_ref.shape
    copier = Copier(sems)
    recv = copier.start(recv_hbm, recv_ref)
    halo = start_halo(
        copier, pad_ref, (x0_hbm, x1_hbm, y0_hbm, y1_hbm, z_hbm, z0_hbm, z1_hbm),
        (y0_ref, y1_ref, z_ref, z0_ref, z1_ref),
    )
    now = center_copy(copier, now_hbm, pad_ref)
    chunks = start_chunks(copier, ((late_hbm, late_ref), (courant_hbm, courant_ref)), cx)
    recv.wait()
    sources, later = bin_records(recv_ref, cx, cy, cz)
    spread_sources(sources, source_ref)
    spread_sources(later, later_ref)
    copier.send(later_ref, source_hbm)
    for copy in halo:
        copy.wait()
    fill_y(pad_ref, y0_ref, y1_ref)
    zc_ref[...] = depth_correction(z_ref[...], z0_ref[...], z1_ref[...]).reshape(cx, cy, cz)
    now.wait()
    low = iota((cy, cz), 1) < SURF

    def body(x, carry):
        center, lap = lap_at(pad_ref, zc_ref, x, cy)
        lap = lap + source_at(source_ref, x, low)
        fresh_ref[x] = 2.0 * center - late_ref[x] + courant_ref[x] * lap
        return carry

    for c, copies in enumerate(chunks):
        for copy in copies:
            copy.wait()
        part = pl.ds(c * CHUNK, CHUNK)
        lax.fori_loop(c * CHUNK, (c + 1) * CHUNK, body, 0, unroll=UNROLL)
        copier.send(fresh_ref.at[part], fresh_hbm.at[part])
    for src, dst in zip(x_faces(fresh_ref), (xs0_hbm, xs1_hbm)):
        copier.send(src, dst)
    store_y_faces(lambda x: fresh_ref[x], cx // 2, cy, ys0_ref, ys1_ref, 0, cx // 2)
    copier.send(ys0_ref, ys0_hbm)
    copier.send(ys1_ref, ys1_hbm)
    zs_ref[...] = depth_faces(fresh_ref[...].reshape(cx * cy, cz))
    copier.send(zs_ref, zs_hbm)
    copier.close()


def second_kernel(
    now_hbm, source_hbm, x0_hbm, x1_hbm, y0_hbm, y1_hbm, z_hbm, z0_hbm, z1_hbm,
    late_hbm, courant_hbm, forward_hbm, image_hbm,
    fresh_hbm, image_out_hbm,
    source_ref, pad_ref, y0_ref, y1_ref, z_ref, z0_ref, z1_ref, zc_ref, late_ref, courant_ref,
    forward0_ref, forward1_ref, image_ref, fresh_ref, sems,
):
    cx, cy, cz = fresh_ref.shape
    copier = Copier(sems)
    halo = start_halo(
        copier, pad_ref, (x0_hbm, x1_hbm, y0_hbm, y1_hbm, z_hbm, z0_hbm, z1_hbm),
        (y0_ref, y1_ref, z_ref, z0_ref, z1_ref),
    )
    now = center_copy(copier, now_hbm, pad_ref)
    source = copier.start(source_hbm, source_ref)
    chunks = start_chunks(
        copier,
        (
            (late_hbm, late_ref), (courant_hbm, courant_ref), (image_hbm, image_ref),
            (forward_hbm.at[0], forward0_ref), (forward_hbm.at[1], forward1_ref),
        ),
        cx,
    )
    for copy in halo:
        copy.wait()
    fill_y(pad_ref, y0_ref, y1_ref)
    zc_ref[...] = depth_correction(z_ref[...], z0_ref[...], z1_ref[...]).reshape(cx, cy, cz)
    now.wait()
    source.wait()
    low = iota((cy, cz), 1) < SURF

    def body(x, carry):
        center, lap = lap_at(pad_ref, zc_ref, x, cy)
        lap = lap + source_at(source_ref, x, low)
        fresh = 2.0 * center - late_ref[x] + courant_ref[x] * lap
        fresh_ref[x] = fresh
        image = image_ref[x] + forward0_ref[x].astype(F32) * center
        image_ref[x] = image + forward1_ref[x].astype(F32) * fresh
        return carry

    for c, copies in enumerate(chunks):
        for copy in copies:
            copy.wait()
        part = pl.ds(c * CHUNK, CHUNK)
        lax.fori_loop(c * CHUNK, (c + 1) * CHUNK, body, 0, unroll=UNROLL)
        copier.send(fresh_ref.at[part], fresh_hbm.at[part])
        copier.send(image_ref.at[part], image_out_hbm.at[part])
    copier.close()


def swap(value, axis, parity):
    pairs = []
    for i in range(parity, lax.axis_size(axis) - 1, 2):
        pairs += [(i, i + 1), (i + 1, i)]
    return lax.ppermute(value, axis, pairs)


def exchange(x0, x1, y0, y1, z):
    return (
        swap(x0, "gx", 0), swap(x1, "gx", 1),
        swap(y0, "gy", 0), swap(y1, "gy", 1),
        z, swap(z, "gz", 0), swap(z, "gz", 1),
    )


def struct(*shape):
    return jax.ShapeDtypeStruct(shape, F32)


def vm(*shape, dtype=F32):
    return pltpu.VMEM(shape, dtype)


def call(kernel, outs, args, scratch, copies):
    anywhere = pl.BlockSpec(memory_space=pl.ANY)
    size = sum(a.size * a.dtype.itemsize for a in args) + sum(o.size * 4 for o in outs)
    return pl.pallas_call(
        kernel,
        out_shape=outs,
        in_specs=[anywhere] * len(args),
        out_specs=[anywhere] * len(outs),
        scratch_shapes=list(scratch) + [pltpu.SemaphoreType.DMA((copies,))],
        compiler_params=pltpu.CompilerParams(vmem_limit_bytes=60 * 2**20),
        cost_estimate=pl.CostEstimate(flops=10**10, bytes_accessed=size, transcendentals=0),
    )(*args)


def on_device(adjoint_now, adjoint_late, courant, forward, image_in, traces, rec_owner, rec_cell):
    cx, cy, cz = adjoint_now.shape
    n_gy, n_gz = lax.axis_size("gy"), lax.axis_size("gz")
    chunks = rec_owner.shape[0] // 128
    groups = -(-cx * SURF // 128)
    block = struct(cx, cy, cz)
    x_face, y_face = struct(4, cy, cz), struct(cx // 2, 8, cz)
    faces = (x_face, x_face, y_face, y_face, struct(8, cx * cy))
    grid, y_in, z_in = vm(cx, cy, cz), vm(cx // 2, 8, cz), vm(8, cx * cy)
    pad = vm(cx + 8, cy + 16, cz)
    slots = (n_gy * n_gz, 2, 128)
    packed, *out_faces = call(
        functools.partial(send_kernel, n_gy, n_gz), (struct(*slots),) + faces,
        (traces, rec_owner.reshape(chunks, 128), rec_cell.reshape(chunks, 128), adjoint_now),
        (
            vm(*traces.shape), vm(chunks, 128, dtype=jnp.int32), vm(chunks, 128, dtype=jnp.int32),
            grid, vm(*slots), y_in, y_in, z_in,
        ),
        10,
    )
    received = lax.all_to_all(packed, ("gz", "gy"), 0, 0)
    halo = exchange(*out_faces)
    turns = cx // CHUNK
    source = (groups, cy, 128)
    middle, later, *out_faces = call(
        first_kernel, (block, struct(*source)) + faces,
        (received,) + halo + (adjoint_now, adjoint_late, courant),
        (
            vm(*slots), pad, y_in, y_in, z_in, z_in, z_in, grid, grid, grid,
            grid, vm(*source), vm(*source), y_in, y_in, z_in,
        ),
        15 + 3 * turns,
    )
    halo = exchange(*out_faces)
    half = vm(cx, cy, cz, dtype=BF16)
    newest, image = call(
        second_kernel, (block, block),
        (middle, later) + halo + (adjoint_now, courant, forward, image_in),
        (
            vm(*source), pad, y_in, y_in, z_in, z_in, z_in, grid, grid, grid,
            half, half, grid, grid,
        ),
        9 + 7 * turns,
    )
    return newest, middle, image


def solution(mesh):
    grid = P("gx", "gy", "gz")
    return jax.shard_map(
        on_device,
        mesh=mesh,
        in_specs=(
            grid, grid, grid, P(None, "gx", "gy", "gz"), grid,
            P(None, ("gy", "gz")), P(("gy", "gz")), P(("gy", "gz")),
        ),
        out_specs=(grid, grid, grid),
        check_vma=False,
    )
```

time: 78.4 us -> 61.9 us (0.79)
  the two profiles are of different devices: /device:TPU:30 before, /device:TPU:13 now
where the time goes in v2:
time: 61.9 us; the launch traced here: 61.5 us
  starting transfers between devices  39.2 us (63%)
  Pallas kernels  14.6 us (24%)
  waiting for transfers between devices  4.81 us (8%)
  local copies, waits for them, and re-layouts  1.86 us (3%)
  between operations  1.07 us (2%)
    ppermute x12, starting transfers between devices, swap(): return lax.ppermute(value, axis, pairs)  26.6 us
    pallas_call x3, Pallas kernels, call(): pl.pallas_call(kernel, out_shape=outs, in_specs=[anywhere] * len(args), o...  14.6 us
    all_to_all x1, starting transfers between devices, on_device(): received = lax.all_to_all(packed, ('gz', 'gy'), 0, 0)  12.6 us
    ppermute x12, waiting for transfers between devices, swap(): return lax.ppermute(value, axis, pairs)  4.81 us
    unnamed x30, local copies, waits for them, and re-layouts  1.86 us
  transfers between devices with their start and end apart: 13, of which 4 were waited for; matrix products, arithmetic and copies ran while one was open for 0% of the time, Pallas kernels for 0%

profile of v2, /device:TPU:13, one launch (start us, length us, event | category | flops | bytes accessed | tf_op | source)
XLA Modules:
  0.0 61.5 jit_solution(15377071738814232082)
XLA Ops:
  0.6 2.6 %shard_map.103 = (f32[64,2,128]{2,1,0:T(2,128)}, f32[4,40,128]{2,1,0:T(8,128)}, f32[4,40,128]{2,1,0:T(8,128)}, f32[20,8,128]{2,1,0:T(8,128)}, f32[20,8,128]{2,1,0:T(8,128)}, /*index=5*/f32[8,1600]{1,0:T(8,128)}) custom-call(f32[2,1024]{1,0:T(2,128)} %traces_hbm.1, s32[8,128]{1,0:T(8,128)} %bitcast.2, s32[8,128]{1,0:T(8,128)} %bitcast.3, f32[40,40,128]{2,1,0:T(8,128)} %late_hbm.3), custom_call_target="tpu_custom_call" | custom-call | flops 10000000000 | bytes 1280000 | tf_op jit(solution)/shard_map/pallas_call | solution.py:388
  3.2 12.6 %all-to-all-start = ((f32[64,2,128]{2,1,0:T(2,128)}), f32[64,2,128]{2,1,0:T(2,128)S(1)}, u32[]{:S(2)}, u32[]{:S(2)}) async-start(f32[64,2,128]{2,1,0:T(2,128)} %get-tuple-element.18), calls=%async_computation | async-start | bytes 131072 | tf_op jit(solution)/shard_map/all_to_all | solution.py:419
  15.8 4.1 %collective-permute-start.5 = (f32[8,1600]{1,0:T(8,128)}, f32[8,1600]{1,0:T(8,128)S(1)}, u32[]{:S(2)}, u32[]{:S(2)}) collective-permute-start(f32[8,1600]{1,0:T(8,128)} %get-tuple-element.23.z_hbm), channel_id=1, source_target_pairs={{1,2},{2,1},{5,6},{6,5},{9,10},{10,9},{13,14},{14,13},{17,18},{18,... | collective-permute-start | bytes 153608 | tf_op jit(solution)/shard_map/ppermute | solution.py:366
  19.9 1.0 %collective-permute-start = (f32[4,40,128]{2,1,0:T(8,128)}, f32[4,40,128]{2,1,0:T(8,128)S(1)}, u32[]{:S(2)}, u32[]{:S(2)}) collective-permute-start(f32[4,40,128]{2,1,0:T(8,128)} %get-tuple-element.19), channel_id=1, source_target_pairs={{0,64},{64,0},{128,192},{192,128},{1,65},{65,1},{129,193},{193,129... | collective-permute-start | bytes 245768 | tf_op jit(solution)/shard_map/ppermute | solution.py:366
  20.9 1.9 %collective-permute-start.1 = (f32[4,40,128]{2,1,0:T(8,128)}, f32[4,40,128]{2,1,0:T(8,128)S(1)}, u32[]{:S(2)}, u32[]{:S(2)}) collective-permute-start(f32[4,40,128]{2,1,0:T(8,128)} %get-tuple-element.20), channel_id=1, source_target_pairs={{64,128},{128,64},{65,129},{129,65},{66,130},{130,66},{67,131},{13... | collective-permute-start | bytes 245768 | tf_op jit(solution)/shard_map/ppermute | solution.py:366
  22.8 1.3 %collective-permute-start.2 = (f32[20,8,128]{2,1,0:T(8,128)}, f32[20,8,128]{2,1,0:T(8,128)S(1)}, u32[]{:S(2)}, u32[]{:S(2)}) collective-permute-start(f32[20,8,128]{2,1,0:T(8,128)} %get-tuple-element.21), channel_id=1, source_target_pairs={{0,4},{4,0},{8,12},{12,8},{16,20},{20,16},{24,28},{28,24},{32,36},... | collective-permute-start | bytes 245768 | tf_op jit(solution)/shard_map/ppermute | solution.py:366
  24.1 5.2 %collective-permute-start.3 = (f32[20,8,128]{2,1,0:T(8,128)S(1)}, f32[20,8,128]{2,1,0:T(8,128)S(1)}, u32[]{:S(2)}, u32[]{:S(2)}) collective-permute-start(f32[20,8,128]{2,1,0:T(8,128)S(1)} %copy-done.3), channel_id=1, source_target_pairs={{4,8},{8,4},{12,16},{16,12},{20,24},{24,20},{28,32},{32,28},{36,40... | collective-permute-start | bytes 245768 | tf_op jit(solution)/shard_map/ppermute | solution.py:366
  29.3 0.1 collective-permute-start.4
  29.4 1.2 %collective-permute-done.4.z0_hbm = f32[8,1600]{1,0:T(8,128)S(1)} collective-permute-done((f32[8,1600]{1,0:T(8,128)S(1)}, f32[8,1600]{1,0:T(8,128)S(1)}, u32[]{:S(2)}, u32[]{:S(2)}) %collective-permute-start.4) | collective-permute-done | bytes 51232 | tf_op jit(solution)/shard_map/ppermute | solution.py:366
  30.6 0.0 copy-start.2
  30.7 0.7 %collective-permute-done.3.y1_hbm = f32[20,8,128]{2,1,0:T(8,128)S(1)} collective-permute-done((f32[20,8,128]{2,1,0:T(8,128)S(1)}, f32[20,8,128]{2,1,0:T(8,128)S(1)}, u32[]{:S(2)}, u32[]{:S(2)}) %collective-permute-start.3) | collective-permute-done | bytes 81952 | tf_op jit(solution)/shard_map/ppermute | solution.py:366
  31.4 0.6 copy-done.5
  32.0 0.6 copy-done
  32.6 7.0 %shard_map.104 = (f32[40,40,128]{2,1,0:T(8,128)}, f32[3,40,128]{2,1,0:T(8,128)}, f32[4,40,128]{2,1,0:T(8,128)}, f32[4,40,128]{2,1,0:T(8,128)}, f32[20,8,128]{2,1...) custom-call(f32[64,2,128]{2,1,0:T(2,128)} %copy-done, f32[4,40,128]{2,1,0:T(8,128)} %copy-done.1, ...), custom_call_target="tpu_custom_call" | custom-call | flops 10000000000 | bytes 4263936 | tf_op jit(solution)/shard_map/pallas_call | solution.py:388
  39.6 4.7 %collective-permute-start.11 = (f32[8,1600]{1,0:T(8,128)}, f32[8,1600]{1,0:T(8,128)S(1)}, u32[]{:S(2)}, u32[]{:S(2)}) collective-permute-start(f32[8,1600]{1,0:T(8,128)} %get-tuple-element.30.z_hbm), channel_id=1, source_target_pairs={{1,2},{2,1},{5,6},{6,5},{9,10},{10,9},{13,14},{14,13},{17,18},{18,... | collective-permute-start | bytes 153608 | tf_op jit(solution)/shard_map/ppermute | solution.py:366
  44.3 0.1 collective-permute-start.6
  44.4 3.6 %collective-permute-start.7 = (f32[4,40,128]{2,1,0:T(8,128)}, f32[4,40,128]{2,1,0:T(8,128)S(1)}, u32[]{:S(2)}, u32[]{:S(2)}) collective-permute-start(f32[4,40,128]{2,1,0:T(8,128)} %get-tuple-element.27), channel_id=1, source_target_pairs={{64,128},{128,64},{65,129},{129,65},{66,130},{130,66},{67,131},{13... | collective-permute-start | bytes 245768 | tf_op jit(solution)/shard_map/ppermute | solution.py:366
  48.1 0.1 collective-permute-start.8
  48.2 4.3 %collective-permute-start.9 = (f32[20,8,128]{2,1,0:T(8,128)}, f32[20,8,128]{2,1,0:T(8,128)S(1)}, u32[]{:S(2)}, u32[]{:S(2)}) collective-permute-start(f32[20,8,128]{2,1,0:T(8,128)} %get-tuple-element.29), channel_id=1, source_target_pairs={{4,8},{8,4},{12,16},{16,12},{20,24},{24,20},{28,32},{32,28},{36,40... | collective-permute-start | bytes 245768 | tf_op jit(solution)/shard_map/ppermute | solution.py:366
  52.5 0.3 collective-permute-start.10
  52.8 1.4 %collective-permute-done.10.z0_hbm = f32[8,1600]{1,0:T(8,128)S(1)} collective-permute-done((f32[8,1600]{1,0:T(8,128)}, f32[8,1600]{1,0:T(8,128)S(1)}, u32[]{:S(2)}, u32[]{:S(2)}) %collective-permute-start.10) | collective-permute-done | bytes 51232 | tf_op jit(solution)/shard_map/ppermute | solution.py:366
  54.3 1.4 %collective-permute-done.9.y1_hbm = f32[20,8,128]{2,1,0:T(8,128)S(1)} collective-permute-done((f32[20,8,128]{2,1,0:T(8,128)}, f32[20,8,128]{2,1,0:T(8,128)S(1)}, u32[]{:S(2)}, u32[]{:S(2)}) %collective-permute-start.9) | collective-permute-done | bytes 81952 | tf_op jit(solution)/shard_map/ppermute | solution.py:366
  55.7 0.6 copy-done.9
  56.3 5.0 %shard_map.105 = (f32[40,40,128]{2,1,0:T(8,128)}, f32[40,40,128]{2,1,0:T(8,128)}) custom-call(f32[40,40,128]{2,1,0:T(8,128)} %get-tuple-element.16.now_hbm, f32[3,40,128]{2,1,0:T(8,128)} %get-tuple-element.25.source_hbm, f32[4,40,128]{2,1,0:T(8,128)} %copy-done.6, f32[4,40,128]{2,1,0:T(8,128)} %copy-done.7, f32[20,8,128]{2,1,0:T(8,128)} %copy-done.8, ...), custom_call_target="tpu_custom_call" | custom-call | flops 10000000000 | bytes 6277120 | tf_op jit(solution)/shard_map/pallas_call | solution.py:388
  (35 shorter events, 0.1 us)
Async XLA Ops:
  3.2 20.9 %copy-start.3 = (f32[20,8,128]{2,1,0:T(8,128)S(1)}, f32[20,8,128]{2,1,0:T(8,128)}, u32[]{:S(2)}) copy-start(f32[20,8,128]{2,1,0:T(8,128)} %get-tuple-element.22) | copy-start | bytes 245764
  3.2 26.1 %copy-start.10 = (f32[8,1600]{1,0:T(8,128)S(1)}, f32[8,1600]{1,0:T(8,128)}, u32[]{:S(2)}) copy-start(f32[8,1600]{1,0:T(8,128)} %get-tuple-element.23.z_hbm) | copy-start | bytes 153604
  3.2 28.2 %all-to-all-start = ((f32[64,2,128]{2,1,0:T(2,128)}), f32[64,2,128]{2,1,0:T(2,128)S(1)}, u32[]{:S(2)}, u32[]{:S(2)}) async-start(f32[64,2,128]{2,1,0:T(2,128)} %get-tuple-element.18), calls=%async_computation | async-start | bytes 131072 | tf_op jit(solution)/shard_map/all_to_all | solution.py:419
  15.8 13.5 %collective-permute-start.5 = (f32[8,1600]{1,0:T(8,128)}, f32[8,1600]{1,0:T(8,128)S(1)}, u32[]{:S(2)}, u32[]{:S(2)}) collective-permute-start(f32[8,1600]{1,0:T(8,128)} %get-tuple-element.23.z_hbm), channel_id=1, source_target_pairs={{1,2},{2,1},{5,6},{6,5},{9,10},{10,9},{13,14},{14,13},{17,18},{18,... | collective-permute-start | bytes 153608 | tf_op jit(solution)/shard_map/ppermute | solution.py:366
  19.9 10.7 %collective-permute-start = (f32[4,40,128]{2,1,0:T(8,128)}, f32[4,40,128]{2,1,0:T(8,128)S(1)}, u32[]{:S(2)}, u32[]{:S(2)}) collective-permute-start(f32[4,40,128]{2,1,0:T(8,128)} %get-tuple-element.19), channel_id=1, source_target_pairs={{0,64},{64,0},{128,192},{192,128},{1,65},{65,1},{129,193},{193,129... | collective-permute-start | bytes 245768 | tf_op jit(solution)/shard_map/ppermute | solution.py:366
  20.9 9.7 %collective-permute-start.1 = (f32[4,40,128]{2,1,0:T(8,128)}, f32[4,40,128]{2,1,0:T(8,128)S(1)}, u32[]{:S(2)}, u32[]{:S(2)}) collective-permute-start(f32[4,40,128]{2,1,0:T(8,128)} %get-tuple-element.20), channel_id=1, source_target_pairs={{64,128},{128,64},{65,129},{129,65},{66,130},{130,66},{67,131},{13... | collective-permute-start | bytes 245768 | tf_op jit(solution)/shard_map/ppermute | solution.py:366
  22.8 7.8 %collective-permute-start.2 = (f32[20,8,128]{2,1,0:T(8,128)}, f32[20,8,128]{2,1,0:T(8,128)S(1)}, u32[]{:S(2)}, u32[]{:S(2)}) collective-permute-start(f32[20,8,128]{2,1,0:T(8,128)} %get-tuple-element.21), channel_id=1, source_target_pairs={{0,4},{4,0},{8,12},{12,8},{16,20},{20,16},{24,28},{28,24},{32,36},... | collective-permute-start | bytes 245768 | tf_op jit(solution)/shard_map/ppermute | solution.py:366
  24.1 7.3 %collective-permute-start.3 = (f32[20,8,128]{2,1,0:T(8,128)S(1)}, f32[20,8,128]{2,1,0:T(8,128)S(1)}, u32[]{:S(2)}, u32[]{:S(2)}) collective-permute-start(f32[20,8,128]{2,1,0:T(8,128)S(1)} %copy-done.3), channel_id=1, source_target_pairs={{4,8},{8,4},{12,16},{16,12},{20,24},{24,20},{28,32},{32,28},{36,40... | collective-permute-start | bytes 245768 | tf_op jit(solution)/shard_map/ppermute | solution.py:366
  29.3 2.1 %copy-start.11 = (f32[8,1600]{1,0:T(8,128)}, f32[8,1600]{1,0:T(8,128)S(1)}, u32[]{:S(2)}) copy-start(f32[8,1600]{1,0:T(8,128)S(1)} %collective-permute-done.5.z1_hbm) | copy-start | bytes 153604
  29.3 1.3 %collective-permute-start.4 = (f32[8,1600]{1,0:T(8,128)S(1)}, f32[8,1600]{1,0:T(8,128)S(1)}, u32[]{:S(2)}, u32[]{:S(2)}) collective-permute-start(f32[8,1600]{1,0:T(8,128)S(1)} %copy-done.10), channel_id=1, source_target_pairs={{0,1},{1,0},{2,3},{3,2},{4,5},{5,4},{6,7},{7,6},{8,9},{9,8},{10,11... | collective-permute-start | bytes 153608 | tf_op jit(solution)/shard_map/ppermute | solution.py:366
  30.6 0.8 %copy-start.13 = (f32[8,1600]{1,0:T(8,128)}, f32[8,1600]{1,0:T(8,128)S(1)}, u32[]{:S(2)}) copy-start(f32[8,1600]{1,0:T(8,128)S(1)} %collective-permute-done.4.z0_hbm) | copy-start | bytes 153604
  30.6 0.8 %copy-start.1 = (f32[4,40,128]{2,1,0:T(8,128)}, f32[4,40,128]{2,1,0:T(8,128)S(1)}, u32[]{:S(2)}) copy-start(f32[4,40,128]{2,1,0:T(8,128)S(1)} %collective-permute-done.x0_hbm) | copy-start | bytes 245764
  30.6 0.8 %copy-start.2 = (f32[4,40,128]{2,1,0:T(8,128)}, f32[4,40,128]{2,1,0:T(8,128)S(1)}, u32[]{:S(2)}) copy-start(f32[4,40,128]{2,1,0:T(8,128)S(1)} %collective-permute-done.1.x1_hbm) | copy-start | bytes 245764
  39.6 12.9 %collective-permute-start.11 = (f32[8,1600]{1,0:T(8,128)}, f32[8,1600]{1,0:T(8,128)S(1)}, u32[]{:S(2)}, u32[]{:S(2)}) collective-permute-start(f32[8,1600]{1,0:T(8,128)} %get-tuple-element.30.z_hbm), channel_id=1, source_target_pairs={{1,2},{2,1},{5,6},{6,5},{9,10},{10,9},{13,14},{14,13},{17,18},{18,... | collective-permute-start | bytes 153608 | tf_op jit(solution)/shard_map/ppermute | solution.py:366
  44.3 9.9 %collective-permute-start.6 = (f32[4,40,128]{2,1,0:T(8,128)}, f32[4,40,128]{2,1,0:T(8,128)S(1)}, u32[]{:S(2)}, u32[]{:S(2)}) collective-permute-start(f32[4,40,128]{2,1,0:T(8,128)} %get-tuple-element.26), channel_id=1, source_target_pairs={{0,64},{64,0},{128,192},{192,128},{1,65},{65,1},{129,193},{193,129... | collective-permute-start | bytes 245768 | tf_op jit(solution)/shard_map/ppermute | solution.py:366
  44.4 9.8 %collective-permute-start.7 = (f32[4,40,128]{2,1,0:T(8,128)}, f32[4,40,128]{2,1,0:T(8,128)S(1)}, u32[]{:S(2)}, u32[]{:S(2)}) collective-permute-start(f32[4,40,128]{2,1,0:T(8,128)} %get-tuple-element.27), channel_id=1, source_target_pairs={{64,128},{128,64},{65,129},{129,65},{66,130},{130,66},{67,131},{13... | collective-permute-start | bytes 245768 | tf_op jit(solution)/shard_map/ppermute | solution.py:366
  48.1 6.2 %collective-permute-start.8 = (f32[20,8,128]{2,1,0:T(8,128)}, f32[20,8,128]{2,1,0:T(8,128)S(1)}, u32[]{:S(2)}, u32[]{:S(2)}) collective-permute-start(f32[20,8,128]{2,1,0:T(8,128)} %get-tuple-element.28), channel_id=1, source_target_pairs={{0,4},{4,0},{8,12},{12,8},{16,20},{20,16},{24,28},{28,24},{32,36},... | collective-permute-start | bytes 245768 | tf_op jit(solution)/shard_map/ppermute | solution.py:366
  48.2 7.5 %collective-permute-start.9 = (f32[20,8,128]{2,1,0:T(8,128)}, f32[20,8,128]{2,1,0:T(8,128)S(1)}, u32[]{:S(2)}, u32[]{:S(2)}) collective-permute-start(f32[20,8,128]{2,1,0:T(8,128)} %get-tuple-element.29), channel_id=1, source_target_pairs={{4,8},{8,4},{12,16},{16,12},{20,24},{24,20},{28,32},{32,28},{36,40... | collective-permute-start | bytes 245768 | tf_op jit(solution)/shard_map/ppermute | solution.py:366
  52.5 3.2 %copy-start.12 = (f32[8,1600]{1,0:T(8,128)}, f32[8,1600]{1,0:T(8,128)S(1)}, u32[]{:S(2)}) copy-start(f32[8,1600]{1,0:T(8,128)S(1)} %collective-permute-done.11.z1_hbm) | copy-start | bytes 153604
  52.5 1.7 %collective-permute-start.10 = (f32[8,1600]{1,0:T(8,128)}, f32[8,1600]{1,0:T(8,128)S(1)}, u32[]{:S(2)}, u32[]{:S(2)}) collective-permute-start(f32[8,1600]{1,0:T(8,128)} %get-tuple-element.30.z_hbm), channel_id=1, source_target_pairs={{0,1},{1,0},{2,3},{3,2},{4,5},{5,4},{6,7},{7,6},{8,9},{9,8},{10,11... | collective-permute-start | bytes 153608 | tf_op jit(solution)/shard_map/ppermute | solution.py:366
  54.2 1.5 %copy-start.14 = (f32[8,1600]{1,0:T(8,128)}, f32[8,1600]{1,0:T(8,128)S(1)}, u32[]{:S(2)}) copy-start(f32[8,1600]{1,0:T(8,128)S(1)} %collective-permute-done.10.z0_hbm) | copy-start | bytes 153604
  54.2 1.5 %copy-start.6 = (f32[4,40,128]{2,1,0:T(8,128)}, f32[4,40,128]{2,1,0:T(8,128)S(1)}, u32[]{:S(2)}) copy-start(f32[4,40,128]{2,1,0:T(8,128)S(1)} %collective-permute-done.6.x0_hbm) | copy-start | bytes 245764
  54.2 1.5 %copy-start.7 = (f32[4,40,128]{2,1,0:T(8,128)}, f32[4,40,128]{2,1,0:T(8,128)S(1)}, u32[]{:S(2)}) copy-start(f32[4,40,128]{2,1,0:T(8,128)S(1)} %collective-permute-done.7.x1_hbm) | copy-start | bytes 245764
  54.3 1.5 %copy-start.8 = (f32[20,8,128]{2,1,0:T(8,128)}, f32[20,8,128]{2,1,0:T(8,128)S(1)}, u32[]{:S(2)}) copy-start(f32[20,8,128]{2,1,0:T(8,128)S(1)} %collective-permute-done.8.y0_hbm) | copy-start | bytes 245764
  (4 other events, 2.7 us)

commit v3 on v2

--- a/solution.py
+++ b/solution.py
@@ -76,24 +76,23 @@
         out_ref[d, 1:2, :] = cells[d : d + 1, :]
 
 
-def is_even(axis):
-    return lax.rem(lax.axis_index(axis), 2) == 0
-
-
-def store_y_faces(read, half, cy, y0_ref, y1_ref, begin, end):
-    y_even = is_even("gy")
-    for x in range(begin, end):
-        one, two = read(x), read(x + half)
-        lo = jnp.concatenate([one[0:4], two[0:4]], axis=0)
-        hi = jnp.concatenate([one[cy - 4 : cy], two[cy - 4 : cy]], axis=0)
-        y0_ref[x] = jnp.where(y_even, hi, lo)
-        y1_ref[x] = jnp.where(y_even, lo, hi)
+def store_y_faces(src_ref, low_ref, high_ref):
+    cx, cy, _ = src_ref.shape
+    half = cx // 2
+    for x in range(half):
+        one, two = src_ref[x], src_ref[x + half]
+        low_ref[x] = jnp.concatenate([one[0:4], two[0:4]], axis=0)
+        high_ref[x] = jnp.concatenate([one[cy - 4 : cy], two[cy - 4 : cy]], axis=0)
 
 
 def x_faces(ref):
     cx = ref.shape[0]
-    first = jnp.where(is_even("gx"), cx - 4, 0)
-    return ref.at[pl.ds(first, 4)], ref.at[pl.ds(cx - 4 - first, 4)]
+    return ref.at[0:4], ref.at[cx - 4 : cx]
+
+
+def at_edges(axis):
+    at = lax.axis_index(axis)
+    return at == 0, at == lax.axis_size(axis) - 1
 
 
 class Copier:
@@ -141,7 +140,7 @@
     now.wait()
     for src, dst in zip(x_faces(now_ref), (x0_hbm, x1_hbm)):
         copier.send(src, dst)
-    store_y_faces(lambda x: now_ref[x], cx // 2, cy, y0_ref, y1_ref, 0, cx // 2)
+    store_y_faces(now_ref, y0_ref, y1_ref)
     copier.send(y0_ref, y0_hbm)
     copier.send(y1_ref, y1_hbm)
     z_ref[...] = depth_faces(now_ref[...].reshape(cx * cy, cz))
@@ -189,30 +188,33 @@
 
 def start_halo(copier, pad_ref, halo_hbm, halo_refs):
     cx, cy = pad_ref.shape[0] - 8, pad_ref.shape[1] - 16
-    first = jnp.where(is_even("gx"), 4 + cx, 0)
-    places = (
-        pad_ref.at[pl.ds(first, 4), 8 : 8 + cy, :],
-        pad_ref.at[pl.ds(4 + cx - first, 4), 8 : 8 + cy, :],
-    ) + tuple(halo_refs)
-    return [copier.start(src, dst) for src, dst in zip(halo_hbm, places)]
-
-
-def fill_y(pad_ref, y0_ref, y1_ref):
-    cx, cy = pad_ref.shape[0] - 8, pad_ref.shape[1] - 16
+    places = (pad_ref.at[0:4, 8 : 8 + cy, :], pad_ref.at[4 + cx : 8 + cx, 8 : 8 + cy, :])
+    return [copier.start(src, dst) for src, dst in zip(halo_hbm, places + tuple(halo_refs))]
+
+
+def fill_xy(pad_ref, before_ref, after_ref):
+    cx, cy, cz = pad_ref.shape[0] - 8, pad_ref.shape[1] - 16, pad_ref.shape[2]
     half = cx // 2
-    y_even = is_even("gy")
+    for edge, begin in zip(at_edges("gx"), (0, 4 + cx)):
+
+        @pl.when(edge)
+        def _(begin=begin):
+            pad_ref[begin : begin + 4, 8 : 8 + cy, :] = jnp.zeros((4, cy, cz), F32)
+
+    first, last = at_edges("gy")
     for x in range(half):
-        one, two = y0_ref[x], y1_ref[x]
-        before, after = jnp.where(y_even, two, one), jnp.where(y_even, one, two)
+        before = jnp.where(first, 0.0, before_ref[x])
+        after = jnp.where(last, 0.0, after_ref[x])
         pad_ref[4 + x, 4:8, :] = before[0:4]
         pad_ref[4 + half + x, 4:8, :] = before[4:8]
         pad_ref[4 + x, 8 + cy : 12 + cy, :] = after[0:4]
         pad_ref[4 + half + x, 8 + cy : 12 + cy, :] = after[4:8]
 
 
-def depth_correction(own, zero, one):
-    upper = (iota(own.shape, 0) < 4) == is_even("gz")
-    delta = jnp.where(upper, zero, one) - own
+def depth_correction(own, before, after):
+    at = iota(own.shape, 0)
+    first, last = at_edges("gz")
+    delta = jnp.where(at < 4, jnp.where(last, 0.0, after), jnp.where(first, 0.0, before)) - own
     row = iota((8, 128), 0)
     lane = iota((8, 128), 1)
     distance = jnp.where(row < 4, 128 + row - lane, lane + 8 - row)
@@ -282,7 +284,7 @@
     copier.send(later_ref, source_hbm)
     for copy in halo:
         copy.wait()
-    fill_y(pad_ref, y0_ref, y1_ref)
+    fill_xy(pad_ref, y0_ref, y1_ref)
     zc_ref[...] = depth_correction(z_ref[...], z0_ref[...], z1_ref[...]).reshape(cx, cy, cz)
     now.wait()
     low = iota((cy, cz), 1) < SURF
@@ -301,7 +303,7 @@
         copier.send(fresh_ref.at[part], fresh_hbm.at[part])
     for src, dst in zip(x_faces(fresh_ref), (xs0_hbm, xs1_hbm)):
         copier.send(src, dst)
-    store_y_faces(lambda x: fresh_ref[x], cx // 2, cy, ys0_ref, ys1_ref, 0, cx // 2)
+    store_y_faces(fresh_ref, ys0_ref, ys1_ref)
     copier.send(ys0_ref, ys0_hbm)
     copier.send(ys1_ref, ys1_hbm)
     zs_ref[...] = depth_faces(fresh_ref[...].reshape(cx * cy, cz))
@@ -334,7 +336,7 @@
     )
     for copy in halo:
         copy.wait()
-    fill_y(pad_ref, y0_ref, y1_ref)
+    fill_xy(pad_ref, y0_ref, y1_ref)
     zc_ref[...] = depth_correction(z_ref[...], z0_ref[...], z1_ref[...]).reshape(cx, cy, cz)
     now.wait()
     source.wait()
@@ -359,18 +361,16 @@
     copier.close()
 
 
-def swap(value, axis, parity):
-    pairs = []
-    for i in range(parity, lax.axis_size(axis) - 1, 2):
-        pairs += [(i, i + 1), (i + 1, i)]
-    return lax.ppermute(value, axis, pairs)
-
-
-def exchange(x0, x1, y0, y1, z):
+def turn(value, axis, by):
+    count = lax.axis_size(axis)
+    return lax.ppermute(value, axis, [(i, (i + by) % count) for i in range(count)])
+
+
+def exchange(x_low, x_high, y_low, y_high, z):
     return (
-        swap(x0, "gx", 0), swap(x1, "gx", 1),
-        swap(y0, "gy", 0), swap(y1, "gy", 1),
-        z, swap(z, "gz", 0), swap(z, "gz", 1),
+        turn(x_high, "gx", 1), turn(x_low, "gx", -1),
+        turn(y_high, "gy", 1), turn(y_low, "gy", -1),
+        z, turn(z, "gz", 1), turn(z, "gz", -1),
     )
 
 

time: 61.9 us -> 57.6 us (0.931)
  the two profiles are of different devices: /device:TPU:13 before, /device:TPU:8 now
where the time goes in v3:
time: 57.6 us; the launch traced here: 57.4 us
  starting transfers between devices  29.5 us (51%)
  Pallas kernels  14.6 us (25%)
  waiting for transfers between devices  10.3 us (18%)
  local copies, waits for them, and re-layouts  1.98 us (3%)
  between operations  0.98 us (2%)
    ppermute x12, starting transfers between devices, turn(): lax.ppermute(value, axis, [(i, (i + by) % count) for i in range(count)])  17.3 us
    pallas_call x3, Pallas kernels, call(): pl.pallas_call(kernel, out_shape=outs, in_specs=[anywhere] * len(args), o...  14.6 us
    all_to_all x1, starting transfers between devices, on_device(): received = lax.all_to_all(packed, ('gz', 'gy'), 0, 0)  12.2 us
    ppermute x12, waiting for transfers between devices, turn(): lax.ppermute(value, axis, [(i, (i + by) % count) for i in range(count)])  10.3 us
    unnamed x30, local copies, waits for them, and re-layouts  1.98 us
  transfers between devices with their start and end apart: 13, of which 2 were waited for; matrix products, arithmetic and copies ran while one was open for 0% of the time, Pallas kernels for 0%

profile of v3, /device:TPU:8, one launch (start us, length us, event | category | flops | bytes accessed | tf_op | source)
XLA Modules:
  0.0 57.4 jit_solution(16949107197940395648)
XLA Ops:
  0.6 2.6 %shard_map.103 = (f32[64,2,128]{2,1,0:T(2,128)}, f32[4,40,128]{2,1,0:T(8,128)}, f32[4,40,128]{2,1,0:T(8,128)}, f32[20,8,128]{2,1,0:T(8,128)}, f32[20,8,128]{2,1,0:T(8,128)}, /*index=5*/f32[8,1600]{1,0:T(8,128)}) custom-call(f32[2,1024]{1,0:T(2,128)} %traces_hbm.1, s32[8,128]{1,0:T(8,128)} %bitcast.2, s32[8,128]{1,0:T(8,128)} %bitcast.3, f32[40,40,128]{2,1,0:T(8,128)} %late_hbm.3), custom_call_target="tpu_custom_call" | custom-call | flops 10000000000 | bytes 1280000 | tf_op jit(solution)/shard_map/pallas_call | solution.py:388
  3.2 12.2 %all-to-all-start = ((f32[64,2,128]{2,1,0:T(2,128)}), f32[64,2,128]{2,1,0:T(2,128)S(1)}, u32[]{:S(2)}, u32[]{:S(2)}) async-start(f32[64,2,128]{2,1,0:T(2,128)} %get-tuple-element.18), calls=%async_computation | async-start | bytes 131072 | tf_op jit(solution)/shard_map/all_to_all | solution.py:419
  15.5 2.1 %collective-permute-start.5 = (f32[8,1600]{1,0:T(8,128)}, f32[8,1600]{1,0:T(8,128)S(1)}, u32[]{:S(2)}, u32[]{:S(2)}) collective-permute-start(f32[8,1600]{1,0:T(8,128)} %get-tuple-element.23.z_hbm), channel_id=1, source_target_pairs={{0,3},{1,0},{2,1},{3,2},{4,7},{5,4},{6,5},{7,6},{8,11},{9,8},{10,9... | collective-permute-start | bytes 153608 | tf_op jit(solution)/shard_map/ppermute | solution.py:366
  17.6 1.5 %collective-permute-start = (f32[4,40,128]{2,1,0:T(8,128)}, f32[4,40,128]{2,1,0:T(8,128)S(1)}, u32[]{:S(2)}, u32[]{:S(2)}) collective-permute-start(f32[4,40,128]{2,1,0:T(8,128)} %get-tuple-element.19), channel_id=1, source_target_pairs={{0,64},{64,128},{128,192},{192,0},{1,65},{65,129},{129,193},{193,1... | collective-permute-start | bytes 245768 | tf_op jit(solution)/shard_map/ppermute | solution.py:366
  19.1 1.7 %collective-permute-start.1 = (f32[4,40,128]{2,1,0:T(8,128)}, f32[4,40,128]{2,1,0:T(8,128)S(1)}, u32[]{:S(2)}, u32[]{:S(2)}) collective-permute-start(f32[4,40,128]{2,1,0:T(8,128)} %get-tuple-element.20), channel_id=1, source_target_pairs={{0,192},{64,0},{128,64},{192,128},{1,193},{65,1},{129,65},{193,129... | collective-permute-start | bytes 245768 | tf_op jit(solution)/shard_map/ppermute | solution.py:366
  20.9 1.5 %collective-permute-start.2 = (f32[20,8,128]{2,1,0:T(8,128)}, f32[20,8,128]{2,1,0:T(8,128)S(1)}, u32[]{:S(2)}, u32[]{:S(2)}) collective-permute-start(f32[20,8,128]{2,1,0:T(8,128)} %get-tuple-element.21), channel_id=1, source_target_pairs={{0,4},{4,8},{8,12},{12,16},{16,20},{20,24},{24,28},{28,32},{32,36}... | collective-permute-start | bytes 245768 | tf_op jit(solution)/shard_map/ppermute | solution.py:366
  22.3 2.7 %collective-permute-start.3 = (f32[20,8,128]{2,1,0:T(8,128)S(1)}, f32[20,8,128]{2,1,0:T(8,128)S(1)}, u32[]{:S(2)}, u32[]{:S(2)}) collective-permute-start(f32[20,8,128]{2,1,0:T(8,128)S(1)} %copy-done.3), channel_id=1, source_target_pairs={{0,60},{4,0},{8,4},{12,8},{16,12},{20,16},{24,20},{28,24},{32,28},... | collective-permute-start | bytes 245768 | tf_op jit(solution)/shard_map/ppermute | solution.py:366
  25.0 0.1 collective-permute-start.4
  25.1 5.0 %collective-permute-done.4.z0_hbm = f32[8,1600]{1,0:T(8,128)S(1)} collective-permute-done((f32[8,1600]{1,0:T(8,128)S(1)}, f32[8,1600]{1,0:T(8,128)S(1)}, u32[]{:S(2)}, u32[]{:S(2)}) %collective-permute-start.4) | collective-permute-done | bytes 51232 | tf_op jit(solution)/shard_map/ppermute | solution.py:366
  30.2 0.5 copy-done.13
  30.8 0.0 copy-done.2
  30.8 0.0 copy-done.5
  30.9 0.6 %copy-done = f32[64,2,128]{2,1,0:T(2,128)} copy-done((f32[64,2,128]{2,1,0:T(2,128)}, f32[64,2,128]{2,1,0:T(2,128)S(1)}, u32[]{:S(2)}) %copy-start) | copy-done | bytes 65560
  31.5 7.0 %shard_map.104 = (f32[40,40,128]{2,1,0:T(8,128)}, f32[3,40,128]{2,1,0:T(8,128)}, f32[4,40,128]{2,1,0:T(8,128)}, f32[4,40,128]{2,1,0:T(8,128)}, f32[20,8,128]{2,1...) custom-call(f32[64,2,128]{2,1,0:T(2,128)} %copy-done, f32[4,40,128]{2,1,0:T(8,128)} %copy-done.1, ...), custom_call_target="tpu_custom_call" | custom-call | flops 10000000000 | bytes 4263936 | tf_op jit(solution)/shard_map/pallas_call | solution.py:388
  38.5 0.1 collective-permute-start.11
  38.6 0.5 collective-permute-start.6
  39.1 3.0 %collective-permute-start.7 = (f32[4,40,128]{2,1,0:T(8,128)}, f32[4,40,128]{2,1,0:T(8,128)S(1)}, u32[]{:S(2)}, u32[]{:S(2)}) collective-permute-start(f32[4,40,128]{2,1,0:T(8,128)} %get-tuple-element.27), channel_id=1, source_target_pairs={{0,192},{64,0},{128,64},{192,128},{1,193},{65,1},{129,65},{193,129... | collective-permute-start | bytes 245768 | tf_op jit(solution)/shard_map/ppermute | solution.py:366
  42.1 4.1 %collective-permute-start.9 = (f32[20,8,128]{2,1,0:T(8,128)}, f32[20,8,128]{2,1,0:T(8,128)S(1)}, u32[]{:S(2)}, u32[]{:S(2)}) collective-permute-start(f32[20,8,128]{2,1,0:T(8,128)} %get-tuple-element.29), channel_id=1, source_target_pairs={{0,60},{4,0},{8,4},{12,8},{16,12},{20,16},{24,20},{28,24},{32,28},... | collective-permute-start | bytes 245768 | tf_op jit(solution)/shard_map/ppermute | solution.py:366
  46.2 5.3 %collective-permute-done.10.z0_hbm = f32[8,1600]{1,0:T(8,128)S(1)} collective-permute-done((f32[8,1600]{1,0:T(8,128)}, f32[8,1600]{1,0:T(8,128)S(1)}, u32[]{:S(2)}, u32[]{:S(2)}) %collective-permute-start.10) | collective-permute-done | bytes 51232 | tf_op jit(solution)/shard_map/ppermute | solution.py:366
  51.6 0.5 copy-done.14
  52.1 0.0 copy-done.7
  52.2 0.0 copy-done.8
  52.2 0.0 copy-done.9
  52.3 5.0 %shard_map.105 = (f32[40,40,128]{2,1,0:T(8,128)}, f32[40,40,128]{2,1,0:T(8,128)}) custom-call(f32[40,40,128]{2,1,0:T(8,128)} %get-tuple-element.16.now_hbm, f32[3,40,128]{2,1,0:T(8,128)} %get-tuple-element.25.source_hbm, f32[4,40,128]{2,1,0:T(8,128)} %copy-done.6, f32[4,40,128]{2,1,0:T(8,128)} %copy-done.7, f32[20,8,128]{2,1,0:T(8,128)} %copy-done.8, ...), custom_call_target="tpu_custom_call" | custom-call | flops 10000000000 | bytes 6277120 | tf_op jit(solution)/shard_map/pallas_call | solution.py:388
  (35 shorter events, 0.1 us)
Async XLA Ops:
  3.2 19.1 %copy-start.3 = (f32[20,8,128]{2,1,0:T(8,128)S(1)}, f32[20,8,128]{2,1,0:T(8,128)}, u32[]{:S(2)}) copy-start(f32[20,8,128]{2,1,0:T(8,128)} %get-tuple-element.22) | copy-start | bytes 245764
  3.2 21.8 %copy-start.10 = (f32[8,1600]{1,0:T(8,128)S(1)}, f32[8,1600]{1,0:T(8,128)}, u32[]{:S(2)}) copy-start(f32[8,1600]{1,0:T(8,128)} %get-tuple-element.23.z_hbm) | copy-start | bytes 153604
  3.2 27.0 %all-to-all-start = ((f32[64,2,128]{2,1,0:T(2,128)}), f32[64,2,128]{2,1,0:T(2,128)S(1)}, u32[]{:S(2)}, u32[]{:S(2)}) async-start(f32[64,2,128]{2,1,0:T(2,128)} %get-tuple-element.18), calls=%async_computation | async-start | bytes 131072 | tf_op jit(solution)/shard_map/all_to_all | solution.py:419
  15.5 9.5 %collective-permute-start.5 = (f32[8,1600]{1,0:T(8,128)}, f32[8,1600]{1,0:T(8,128)S(1)}, u32[]{:S(2)}, u32[]{:S(2)}) collective-permute-start(f32[8,1600]{1,0:T(8,128)} %get-tuple-element.23.z_hbm), channel_id=1, source_target_pairs={{0,3},{1,0},{2,1},{3,2},{4,7},{5,4},{6,5},{7,6},{8,11},{9,8},{10,9... | collective-permute-start | bytes 153608 | tf_op jit(solution)/shard_map/ppermute | solution.py:366
  17.6 12.5 %collective-permute-start = (f32[4,40,128]{2,1,0:T(8,128)}, f32[4,40,128]{2,1,0:T(8,128)S(1)}, u32[]{:S(2)}, u32[]{:S(2)}) collective-permute-start(f32[4,40,128]{2,1,0:T(8,128)} %get-tuple-element.19), channel_id=1, source_target_pairs={{0,64},{64,128},{128,192},{192,0},{1,65},{65,129},{129,193},{193,1... | collective-permute-start | bytes 245768 | tf_op jit(solution)/shard_map/ppermute | solution.py:366
  19.1 11.0 %collective-permute-start.1 = (f32[4,40,128]{2,1,0:T(8,128)}, f32[4,40,128]{2,1,0:T(8,128)S(1)}, u32[]{:S(2)}, u32[]{:S(2)}) collective-permute-start(f32[4,40,128]{2,1,0:T(8,128)} %get-tuple-element.20), channel_id=1, source_target_pairs={{0,192},{64,0},{128,64},{192,128},{1,193},{65,1},{129,65},{193,129... | collective-permute-start | bytes 245768 | tf_op jit(solution)/shard_map/ppermute | solution.py:366
  20.9 9.3 %collective-permute-start.2 = (f32[20,8,128]{2,1,0:T(8,128)}, f32[20,8,128]{2,1,0:T(8,128)S(1)}, u32[]{:S(2)}, u32[]{:S(2)}) collective-permute-start(f32[20,8,128]{2,1,0:T(8,128)} %get-tuple-element.21), channel_id=1, source_target_pairs={{0,4},{4,8},{8,12},{12,16},{16,20},{20,24},{24,28},{28,32},{32,36}... | collective-permute-start | bytes 245768 | tf_op jit(solution)/shard_map/ppermute | solution.py:366
  22.3 7.9 %collective-permute-start.3 = (f32[20,8,128]{2,1,0:T(8,128)S(1)}, f32[20,8,128]{2,1,0:T(8,128)S(1)}, u32[]{:S(2)}, u32[]{:S(2)}) collective-permute-start(f32[20,8,128]{2,1,0:T(8,128)S(1)} %copy-done.3), channel_id=1, source_target_pairs={{0,60},{4,0},{8,4},{12,8},{16,12},{20,16},{24,20},{28,24},{32,28},... | collective-permute-start | bytes 245768 | tf_op jit(solution)/shard_map/ppermute | solution.py:366
  25.0 5.2 %copy-start.11 = (f32[8,1600]{1,0:T(8,128)}, f32[8,1600]{1,0:T(8,128)S(1)}, u32[]{:S(2)}) copy-start(f32[8,1600]{1,0:T(8,128)S(1)} %collective-permute-done.5.z1_hbm) | copy-start | bytes 153604
  25.0 5.1 %collective-permute-start.4 = (f32[8,1600]{1,0:T(8,128)S(1)}, f32[8,1600]{1,0:T(8,128)S(1)}, u32[]{:S(2)}, u32[]{:S(2)}) collective-permute-start(f32[8,1600]{1,0:T(8,128)S(1)} %copy-done.10), channel_id=1, source_target_pairs={{0,1},{1,2},{2,3},{3,0},{4,5},{5,6},{6,7},{7,4},{8,9},{9,10},{10,1... | collective-permute-start | bytes 153608 | tf_op jit(solution)/shard_map/ppermute | solution.py:366
  30.1 0.6 %copy-start.1 = (f32[4,40,128]{2,1,0:T(8,128)}, f32[4,40,128]{2,1,0:T(8,128)S(1)}, u32[]{:S(2)}) copy-start(f32[4,40,128]{2,1,0:T(8,128)S(1)} %collective-permute-done.x0_hbm) | copy-start | bytes 245764
  30.2 0.7 %copy-start.2 = (f32[4,40,128]{2,1,0:T(8,128)}, f32[4,40,128]{2,1,0:T(8,128)S(1)}, u32[]{:S(2)}) copy-start(f32[4,40,128]{2,1,0:T(8,128)S(1)} %collective-permute-done.1.x1_hbm) | copy-start | bytes 245764
  30.2 0.7 %copy-start.4 = (f32[20,8,128]{2,1,0:T(8,128)}, f32[20,8,128]{2,1,0:T(8,128)S(1)}, u32[]{:S(2)}) copy-start(f32[20,8,128]{2,1,0:T(8,128)S(1)} %collective-permute-done.2.y0_hbm) | copy-start | bytes 245764
  30.2 0.7 %copy-start.5 = (f32[20,8,128]{2,1,0:T(8,128)}, f32[20,8,128]{2,1,0:T(8,128)S(1)}, u32[]{:S(2)}) copy-start(f32[20,8,128]{2,1,0:T(8,128)S(1)} %collective-permute-done.3.y1_hbm) | copy-start | bytes 245764
  38.5 7.7 %collective-permute-start.11 = (f32[8,1600]{1,0:T(8,128)}, f32[8,1600]{1,0:T(8,128)S(1)}, u32[]{:S(2)}, u32[]{:S(2)}) collective-permute-start(f32[8,1600]{1,0:T(8,128)} %get-tuple-element.30.z_hbm), channel_id=1, source_target_pairs={{0,3},{1,0},{2,1},{3,2},{4,7},{5,4},{6,5},{7,6},{8,11},{9,8},{10,9... | collective-permute-start | bytes 153608 | tf_op jit(solution)/shard_map/ppermute | solution.py:366
  38.6 12.9 %collective-permute-start.6 = (f32[4,40,128]{2,1,0:T(8,128)}, f32[4,40,128]{2,1,0:T(8,128)S(1)}, u32[]{:S(2)}, u32[]{:S(2)}) collective-permute-start(f32[4,40,128]{2,1,0:T(8,128)} %get-tuple-element.26), channel_id=1, source_target_pairs={{0,64},{64,128},{128,192},{192,0},{1,65},{65,129},{129,193},{193,1... | collective-permute-start | bytes 245768 | tf_op jit(solution)/shard_map/ppermute | solution.py:366
  39.1 12.4 %collective-permute-start.7 = (f32[4,40,128]{2,1,0:T(8,128)}, f32[4,40,128]{2,1,0:T(8,128)S(1)}, u32[]{:S(2)}, u32[]{:S(2)}) collective-permute-start(f32[4,40,128]{2,1,0:T(8,128)} %get-tuple-element.27), channel_id=1, source_target_pairs={{0,192},{64,0},{128,64},{192,128},{1,193},{65,1},{129,65},{193,129... | collective-permute-start | bytes 245768 | tf_op jit(solution)/shard_map/ppermute | solution.py:366
  42.1 9.4 %collective-permute-start.8 = (f32[20,8,128]{2,1,0:T(8,128)}, f32[20,8,128]{2,1,0:T(8,128)S(1)}, u32[]{:S(2)}, u32[]{:S(2)}) collective-permute-start(f32[20,8,128]{2,1,0:T(8,128)} %get-tuple-element.28), channel_id=1, source_target_pairs={{0,4},{4,8},{8,12},{12,16},{16,20},{20,24},{24,28},{28,32},{32,36}... | collective-permute-start | bytes 245768 | tf_op jit(solution)/shard_map/ppermute | solution.py:366
  42.1 9.5 %collective-permute-start.9 = (f32[20,8,128]{2,1,0:T(8,128)}, f32[20,8,128]{2,1,0:T(8,128)S(1)}, u32[]{:S(2)}, u32[]{:S(2)}) collective-permute-start(f32[20,8,128]{2,1,0:T(8,128)} %get-tuple-element.29), channel_id=1, source_target_pairs={{0,60},{4,0},{8,4},{12,8},{16,12},{20,16},{24,20},{28,24},{32,28},... | collective-permute-start | bytes 245768 | tf_op jit(solution)/shard_map/ppermute | solution.py:366
  46.2 5.3 %copy-start.12 = (f32[8,1600]{1,0:T(8,128)}, f32[8,1600]{1,0:T(8,128)S(1)}, u32[]{:S(2)}) copy-start(f32[8,1600]{1,0:T(8,128)S(1)} %collective-permute-done.11.z1_hbm) | copy-start | bytes 153604
  46.2 5.3 %collective-permute-start.10 = (f32[8,1600]{1,0:T(8,128)}, f32[8,1600]{1,0:T(8,128)S(1)}, u32[]{:S(2)}, u32[]{:S(2)}) collective-permute-start(f32[8,1600]{1,0:T(8,128)} %get-tuple-element.30.z_hbm), channel_id=1, source_target_pairs={{0,1},{1,2},{2,3},{3,0},{4,5},{5,6},{6,7},{7,4},{8,9},{9,10},{10,1... | collective-permute-start | bytes 153608 | tf_op jit(solution)/shard_map/ppermute | solution.py:366
  51.5 0.7 %copy-start.7 = (f32[4,40,128]{2,1,0:T(8,128)}, f32[4,40,128]{2,1,0:T(8,128)S(1)}, u32[]{:S(2)}) copy-start(f32[4,40,128]{2,1,0:T(8,128)S(1)} %collective-permute-done.7.x1_hbm) | copy-start | bytes 245764
  51.5 0.7 %copy-start.8 = (f32[20,8,128]{2,1,0:T(8,128)}, f32[20,8,128]{2,1,0:T(8,128)S(1)}, u32[]{:S(2)}) copy-start(f32[20,8,128]{2,1,0:T(8,128)S(1)} %collective-permute-done.8.y0_hbm) | copy-start | bytes 245764
  51.5 0.7 %copy-start.9 = (f32[20,8,128]{2,1,0:T(8,128)}, f32[20,8,128]{2,1,0:T(8,128)S(1)}, u32[]{:S(2)}) copy-start(f32[20,8,128]{2,1,0:T(8,128)S(1)} %collective-permute-done.9.y1_hbm) | copy-start | bytes 245764
  (4 other events, 2.5 us)

commit v4 on v3

--- a/solution.py
+++ b/solution.py
@@ -221,9 +221,10 @@
     weight = jnp.zeros((8, 128), F32)
     for j in range(1, 5):
         weight = jnp.where(distance == j, COEFFS[j], weight)
-    return lax.dot_general(
-        delta, weight, TN, precision=lax.Precision.HIGHEST, preferred_element_type=F32
-    )
+    d, w = split3(delta), split3(weight)
+    left = jnp.concatenate([d[0], d[1], d[2], d[0], d[1], d[0]], axis=0).astype(BF16)
+    right = jnp.concatenate([w[0], w[0], w[0], w[1], w[1], w[2]], axis=0).astype(BF16)
+    return lax.dot_general(left, right, TN, preferred_element_type=F32)
 
 
 def lap_at(pad_ref, zc_ref, x, cy):
@@ -367,11 +368,12 @@
 
 
 def exchange(x_low, x_high, y_low, y_high, z):
-    return (
-        turn(x_high, "gx", 1), turn(x_low, "gx", -1),
-        turn(y_high, "gy", 1), turn(y_low, "gy", -1),
-        z, turn(z, "gz", 1), turn(z, "gz", -1),
-    )
+    z_before, z_after = turn(z, "gz", 1), turn(z, "gz", -1)
+    y_before, y_after = turn(y_high, "gy", 1), turn(y_low, "gy", -1)
+    x_before = turn(x_high, "gx", 1)
+    x_low, z_before, z_after = lax.optimization_barrier((x_low, z_before, z_after))
+    x_after = turn(x_low, "gx", -1)
+    return x_before, x_after, y_before, y_after, z, z_before, z_after
 
 
 def struct(*shape):
@@ -391,7 +393,7 @@
         in_specs=[anywhere] * len(args),
         out_specs=[anywhere] * len(outs),
         scratch_shapes=list(scratch) + [pltpu.SemaphoreType.DMA((copies,))],
-        compiler_params=pltpu.CompilerParams(vmem_limit_bytes=60 * 2**20),
+        compiler_params=pltpu.CompilerParams(vmem_limit_bytes=63_480_000),
         cost_estimate=pl.CostEstimate(flops=10**10, bytes_accessed=size, transcendentals=0),
     )(*args)
 

time: 57.6 us -> 54.5 us (0.946)
  the two profiles are of different devices: /device:TPU:8 before, /device:TPU:1 now
where the time goes in v4:
time: 54.5 us; the launch traced here: 54.3 us
  starting transfers between devices  32 us (59%)
  Pallas kernels  13.3 us (24%)
  waiting for transfers between devices  6.16 us (11%)
  local copies, waits for them, and re-layouts  1.86 us (3%)
  between operations  0.93 us (2%)
    ppermute x12, starting transfers between devices, turn(): lax.ppermute(value, axis, [(i, (i + by) % count) for i in range(count)])  20.5 us
    pallas_call x3, Pallas kernels, call(): pl.pallas_call(kernel, out_shape=outs, in_specs=[anywhere] * len(args), o...  13.3 us
    all_to_all x1, starting transfers between devices, on_device(): received = lax.all_to_all(packed, ('gz', 'gy'), 0, 0)  11.5 us
    ppermute x12, waiting for transfers between devices, turn(): lax.ppermute(value, axis, [(i, (i + by) % count) for i in range(count)])  3.55 us
    all_to_all x1, waiting for transfers between devices, on_device(): received = lax.all_to_all(packed, ('gz', 'gy'), 0, 0)  2.61 us
    unnamed x28, local copies, waits for them, and re-layouts  1.86 us
  transfers between devices with their start and end apart: 13, of which 4 were waited for; matrix products, arithmetic and copies ran while one was open for 0% of the time, Pallas kernels for 0%

profile of v4, /device:TPU:1, one launch (start us, length us, event | category | flops | bytes accessed | tf_op | source)
XLA Modules:
  0.0 54.3 jit_solution(9906753616011829899)
XLA Ops:
  0.6 2.6 %shard_map.103 = (f32[64,2,128]{2,1,0:T(2,128)}, f32[4,40,128]{2,1,0:T(8,128)}, f32[4,40,128]{2,1,0:T(8,128)}, f32[20,8,128]{2,1,0:T(8,128)}, f32[20,8,128]{2,1,0:T(8,128)}, /*index=5*/f32[8,1600]{1,0:T(8,128)}) custom-call(f32[2,1024]{1,0:T(2,128)} %traces_hbm.1, s32[8,128]{1,0:T(8,128)} %bitcast.2, s32[8,128]{1,0:T(8,128)} %bitcast.3, f32[40,40,128]{2,1,0:T(8,128)} %late_hbm.3), custom_call_target="tpu_custom_call" | custom-call | flops 10000000000 | bytes 1280000 | tf_op jit(solution)/shard_map/pallas_call | solution.py:390
  3.2 0.0 copy-start.1
  3.2 3.3 %collective-permute-start.2 = (f32[8,1600]{1,0:T(8,128)}, f32[8,1600]{1,0:T(8,128)S(1)}, u32[]{:S(2)}, u32[]{:S(2)}) collective-permute-start(f32[8,1600]{1,0:T(8,128)} %get-tuple-element.27.z_hbm), channel_id=1, source_target_pairs={{0,3},{1,0},{2,1},{3,2},{4,7},{5,4},{6,5},{7,6},{8,11},{9,8},{10,9... | collective-permute-start | bytes 153608 | tf_op jit(solution)/shard_map/ppermute | solution.py:367
  6.6 1.2 %collective-permute-start.1 = (f32[8,1600]{1,0:T(8,128)}, f32[8,1600]{1,0:T(8,128)S(1)}, u32[]{:S(2)}, u32[]{:S(2)}) collective-permute-start(f32[8,1600]{1,0:T(8,128)} %get-tuple-element.27.z_hbm), channel_id=1, source_target_pairs={{0,1},{1,2},{2,3},{3,0},{4,5},{5,6},{6,7},{7,4},{8,9},{9,10},{10,1... | collective-permute-start | bytes 153608 | tf_op jit(solution)/shard_map/ppermute | solution.py:367
  7.7 11.5 %all-to-all-start = ((f32[64,2,128]{2,1,0:T(2,128)}), f32[64,2,128]{2,1,0:T(2,128)S(1)}, u32[]{:S(2)}, u32[]{:S(2)}) async-start(f32[64,2,128]{2,1,0:T(2,128)} %get-tuple-element.24), calls=%async_computation | async-start | bytes 131072 | tf_op jit(solution)/shard_map/all_to_all | solution.py:421
  19.2 1.3 %collective-permute-start = (f32[4,40,128]{2,1,0:T(8,128)}, f32[4,40,128]{2,1,0:T(8,128)S(1)}, u32[]{:S(2)}, u32[]{:S(2)}) collective-permute-start(f32[4,40,128]{2,1,0:T(8,128)} %get-tuple-element.25), channel_id=1, source_target_pairs={{0,64},{64,128},{128,192},{192,0},{1,65},{65,129},{129,193},{193,1... | collective-permute-start | bytes 245768 | tf_op jit(solution)/shard_map/ppermute | solution.py:367
  20.5 1.4 %collective-permute-start.4 = (f32[20,8,128]{2,1,0:T(8,128)}, f32[20,8,128]{2,1,0:T(8,128)S(1)}, u32[]{:S(2)}, u32[]{:S(2)}) collective-permute-start(f32[20,8,128]{2,1,0:T(8,128)} %get-tuple-element.29), channel_id=1, source_target_pairs={{0,4},{4,8},{8,12},{12,16},{16,20},{20,24},{24,28},{28,32},{32,36}... | collective-permute-start | bytes 245768 | tf_op jit(solution)/shard_map/ppermute | solution.py:367
  21.8 2.2 %collective-permute-start.5 = (f32[20,8,128]{2,1,0:T(8,128)}, f32[20,8,128]{2,1,0:T(8,128)S(1)}, u32[]{:S(2)}, u32[]{:S(2)}) collective-permute-start(f32[20,8,128]{2,1,0:T(8,128)} %get-tuple-element.30), channel_id=1, source_target_pairs={{0,60},{4,0},{8,4},{12,8},{16,12},{20,16},{24,20},{28,24},{32,28},... | collective-permute-start | bytes 245768 | tf_op jit(solution)/shard_map/ppermute | solution.py:367
  24.1 1.5 %collective-permute-start.3 = (f32[4,40,128]{2,1,0:T(8,128)S(1)}, f32[4,40,128]{2,1,0:T(8,128)S(1)}, u32[]{:S(2)}, u32[]{:S(2)}) collective-permute-start(f32[4,40,128]{2,1,0:T(8,128)S(1)} %copy-done.1), channel_id=1, source_target_pairs={{0,192},{64,0},{128,64},{192,128},{1,193},{65,1},{129,65},{193,129... | collective-permute-start | bytes 245768 | tf_op jit(solution)/shard_map/ppermute | solution.py:367
  25.6 1.0 %collective-permute-done.4.y0_hbm = f32[20,8,128]{2,1,0:T(8,128)S(1)} collective-permute-done((f32[20,8,128]{2,1,0:T(8,128)}, f32[20,8,128]{2,1,0:T(8,128)S(1)}, u32[]{:S(2)}, u32[]{:S(2)}) %collective-permute-start.4) | collective-permute-done | bytes 81952 | tf_op jit(solution)/shard_map/ppermute | solution.py:367
  26.6 2.6 %all-to-all-done.recv_hbm = f32[64,2,128]{2,1,0:T(2,128)S(1)} async-done(((f32[64,2,128]{2,1,0:T(2,128)}), f32[64,2,128]{2,1,0:T(2,128)S(1)}, u32[]{:S(2)}, u32[]{:S(2)}) %all-to-all-start) | async-done | bytes 65568 | tf_op jit(solution)/shard_map/all_to_all | solution.py:421
  29.3 0.6 %copy-done = f32[64,2,128]{2,1,0:T(2,128)} copy-done((f32[64,2,128]{2,1,0:T(2,128)}, f32[64,2,128]{2,1,0:T(2,128)S(1)}, u32[]{:S(2)}) %copy-start) | copy-done | bytes 65560
  29.9 0.6 %copy-done.7 = f32[4,40,128]{2,1,0:T(8,128)} copy-done((f32[4,40,128]{2,1,0:T(8,128)}, f32[4,40,128]{2,1,0:T(8,128)S(1)}, u32[]{:S(2)}) %copy-start.7) | copy-done | bytes 81944
  30.5 5.8 %shard_map.104 = (f32[40,40,128]{2,1,0:T(8,128)}, f32[3,40,128]{2,1,0:T(8,128)}, f32[4,40,128]{2,1,0:T(8,128)}, f32[4,40,128]{2,1,0:T(8,128)}, f32[20,8,128]{2,1...) custom-call(f32[64,2,128]{2,1,0:T(2,128)} %copy-done, f32[4,40,128]{2,1,0:T(8,128)} %copy-done.2, ...), custom_call_target="tpu_custom_call" | custom-call | flops 10000000000 | bytes 4263936 | tf_op jit(solution)/shard_map/pallas_call | solution.py:390
  36.3 0.6 %collective-permute-start.8 = (f32[8,1600]{1,0:T(8,128)}, f32[8,1600]{1,0:T(8,128)S(1)}, u32[]{:S(2)}, u32[]{:S(2)}) collective-permute-start(f32[8,1600]{1,0:T(8,128)} %get-tuple-element.37.z_hbm), channel_id=1, source_target_pairs={{0,3},{1,0},{2,1},{3,2},{4,7},{5,4},{6,5},{7,6},{8,11},{9,8},{10,9... | collective-permute-start | bytes 153608 | tf_op jit(solution)/shard_map/ppermute | solution.py:367
  36.8 2.8 %collective-permute-start.7 = (f32[8,1600]{1,0:T(8,128)}, f32[8,1600]{1,0:T(8,128)S(1)}, u32[]{:S(2)}, u32[]{:S(2)}) collective-permute-start(f32[8,1600]{1,0:T(8,128)} %get-tuple-element.37.z_hbm), channel_id=1, source_target_pairs={{0,1},{1,2},{2,3},{3,0},{4,5},{5,6},{6,7},{7,4},{8,9},{9,10},{10,1... | collective-permute-start | bytes 153608 | tf_op jit(solution)/shard_map/ppermute | solution.py:367
  39.6 1.2 %collective-permute-start.6 = (f32[4,40,128]{2,1,0:T(8,128)}, f32[4,40,128]{2,1,0:T(8,128)S(1)}, u32[]{:S(2)}, u32[]{:S(2)}) collective-permute-start(f32[4,40,128]{2,1,0:T(8,128)} %get-tuple-element.35), channel_id=1, source_target_pairs={{0,64},{64,128},{128,192},{192,0},{1,65},{65,129},{129,193},{193,1... | collective-permute-start | bytes 245768 | tf_op jit(solution)/shard_map/ppermute | solution.py:367
  40.8 0.5 collective-permute-start.10
  41.3 3.1 %collective-permute-start.11 = (f32[20,8,128]{2,1,0:T(8,128)}, f32[20,8,128]{2,1,0:T(8,128)S(1)}, u32[]{:S(2)}, u32[]{:S(2)}) collective-permute-start(f32[20,8,128]{2,1,0:T(8,128)} %get-tuple-element.40), channel_id=1, source_target_pairs={{0,60},{4,0},{8,4},{12,8},{16,12},{20,16},{24,20},{28,24},{32,28},... | collective-permute-start | bytes 245768 | tf_op jit(solution)/shard_map/ppermute | solution.py:367
  44.4 1.5 %collective-permute-start.9 = (f32[4,40,128]{2,1,0:T(8,128)}, f32[4,40,128]{2,1,0:T(8,128)S(1)}, u32[]{:S(2)}, u32[]{:S(2)}) collective-permute-start(f32[4,40,128]{2,1,0:T(8,128)} %get-tuple-element.38), channel_id=1, source_target_pairs={{0,192},{64,0},{128,64},{192,128},{1,193},{65,1},{129,65},{193,129... | collective-permute-start | bytes 245768 | tf_op jit(solution)/shard_map/ppermute | solution.py:367
  46.0 0.5 collective-permute-done.10.y0_hbm
  46.4 2.1 %collective-permute-done.9.x1_hbm = f32[4,40,128]{2,1,0:T(8,128)S(1)} collective-permute-done((f32[4,40,128]{2,1,0:T(8,128)}, f32[4,40,128]{2,1,0:T(8,128)S(1)}, u32[]{:S(2)}, u32[]{:S(2)}) %collective-permute-start.9) | collective-permute-done | bytes 81952 | tf_op jit(solution)/shard_map/ppermute | solution.py:367
  48.5 0.6 %copy-done.9 = f32[4,40,128]{2,1,0:T(8,128)} copy-done((f32[4,40,128]{2,1,0:T(8,128)}, f32[4,40,128]{2,1,0:T(8,128)S(1)}, u32[]{:S(2)}) %copy-start.9) | copy-done | bytes 81944
  49.1 5.0 %shard_map.105 = (f32[40,40,128]{2,1,0:T(8,128)}, f32[40,40,128]{2,1,0:T(8,128)}) custom-call(f32[40,40,128]{2,1,0:T(8,128)} %get-tuple-element.22.now_hbm, f32[3,40,128]{2,1,0:T(8,128)} %get-tuple-element.34.source_hbm, f32[4,40,128]{2,1,0:T(8,128)} %copy-done.5, f32[4,40,128]{2,1,0:T(8,128)} %copy-done.9, f32[20,8,128]{2,1,0:T(8,128)} %copy-done.6, ...), custom_call_target="tpu_custom_call" | custom-call | flops 10000000000 | bytes 6277120 | tf_op jit(solution)/shard_map/pallas_call | solution.py:390
  (33 shorter events, 0.1 us)
Async XLA Ops:
  3.2 20.8 %copy-start.1 = (f32[4,40,128]{2,1,0:T(8,128)S(1)}, f32[4,40,128]{2,1,0:T(8,128)}, u32[]{:S(2)}) copy-start(f32[4,40,128]{2,1,0:T(8,128)} %get-tuple-element.28) | copy-start | bytes 245764
  3.2 20.8 %collective-permute-start.2 = (f32[8,1600]{1,0:T(8,128)}, f32[8,1600]{1,0:T(8,128)S(1)}, u32[]{:S(2)}, u32[]{:S(2)}) collective-permute-start(f32[8,1600]{1,0:T(8,128)} %get-tuple-element.27.z_hbm), channel_id=1, source_target_pairs={{0,3},{1,0},{2,1},{3,2},{4,7},{5,4},{6,5},{7,6},{8,11},{9,8},{10,9... | collective-permute-start | bytes 153608 | tf_op jit(solution)/shard_map/ppermute | solution.py:367
  6.6 17.5 %collective-permute-start.1 = (f32[8,1600]{1,0:T(8,128)}, f32[8,1600]{1,0:T(8,128)S(1)}, u32[]{:S(2)}, u32[]{:S(2)}) collective-permute-start(f32[8,1600]{1,0:T(8,128)} %get-tuple-element.27.z_hbm), channel_id=1, source_target_pairs={{0,1},{1,2},{2,3},{3,0},{4,5},{5,6},{6,7},{7,4},{8,9},{9,10},{10,1... | collective-permute-start | bytes 153608 | tf_op jit(solution)/shard_map/ppermute | solution.py:367
  7.7 21.5 %all-to-all-start = ((f32[64,2,128]{2,1,0:T(2,128)}), f32[64,2,128]{2,1,0:T(2,128)S(1)}, u32[]{:S(2)}, u32[]{:S(2)}) async-start(f32[64,2,128]{2,1,0:T(2,128)} %get-tuple-element.24), calls=%async_computation | async-start | bytes 131072 | tf_op jit(solution)/shard_map/all_to_all | solution.py:421
  19.2 6.4 %collective-permute-start = (f32[4,40,128]{2,1,0:T(8,128)}, f32[4,40,128]{2,1,0:T(8,128)S(1)}, u32[]{:S(2)}, u32[]{:S(2)}) collective-permute-start(f32[4,40,128]{2,1,0:T(8,128)} %get-tuple-element.25), channel_id=1, source_target_pairs={{0,64},{64,128},{128,192},{192,0},{1,65},{65,129},{129,193},{193,1... | collective-permute-start | bytes 245768 | tf_op jit(solution)/shard_map/ppermute | solution.py:367
  20.5 6.2 %collective-permute-start.4 = (f32[20,8,128]{2,1,0:T(8,128)}, f32[20,8,128]{2,1,0:T(8,128)S(1)}, u32[]{:S(2)}, u32[]{:S(2)}) collective-permute-start(f32[20,8,128]{2,1,0:T(8,128)} %get-tuple-element.29), channel_id=1, source_target_pairs={{0,4},{4,8},{8,12},{12,16},{16,20},{20,24},{24,28},{28,32},{32,36}... | collective-permute-start | bytes 245768 | tf_op jit(solution)/shard_map/ppermute | solution.py:367
  21.8 4.8 %collective-permute-start.5 = (f32[20,8,128]{2,1,0:T(8,128)}, f32[20,8,128]{2,1,0:T(8,128)S(1)}, u32[]{:S(2)}, u32[]{:S(2)}) collective-permute-start(f32[20,8,128]{2,1,0:T(8,128)} %get-tuple-element.30), channel_id=1, source_target_pairs={{0,60},{4,0},{8,4},{12,8},{16,12},{20,16},{24,20},{28,24},{32,28},... | collective-permute-start | bytes 245768 | tf_op jit(solution)/shard_map/ppermute | solution.py:367
  24.0 5.2 %copy-start.10 = (f32[8,1600]{1,0:T(8,128)}, f32[8,1600]{1,0:T(8,128)S(1)}, u32[]{:S(2)}) copy-start(f32[8,1600]{1,0:T(8,128)S(1)} %collective-permute-done.2.z1_hbm) | copy-start | bytes 153604
  24.0 5.2 %copy-start.11 = (f32[8,1600]{1,0:T(8,128)}, f32[8,1600]{1,0:T(8,128)S(1)}, u32[]{:S(2)}) copy-start(f32[8,1600]{1,0:T(8,128)S(1)} %collective-permute-done.1.z0_hbm) | copy-start | bytes 153604
  24.1 5.2 %collective-permute-start.3 = (f32[4,40,128]{2,1,0:T(8,128)S(1)}, f32[4,40,128]{2,1,0:T(8,128)S(1)}, u32[]{:S(2)}, u32[]{:S(2)}) collective-permute-start(f32[4,40,128]{2,1,0:T(8,128)S(1)} %copy-done.1), channel_id=1, source_target_pairs={{0,192},{64,0},{128,64},{192,128},{1,193},{65,1},{129,65},{193,129... | collective-permute-start | bytes 245768 | tf_op jit(solution)/shard_map/ppermute | solution.py:367
  25.6 3.6 %copy-start.2 = (f32[4,40,128]{2,1,0:T(8,128)}, f32[4,40,128]{2,1,0:T(8,128)S(1)}, u32[]{:S(2)}) copy-start(f32[4,40,128]{2,1,0:T(8,128)S(1)} %collective-permute-done.x0_hbm) | copy-start | bytes 245764
  26.6 2.6 %copy-start.3 = (f32[20,8,128]{2,1,0:T(8,128)}, f32[20,8,128]{2,1,0:T(8,128)S(1)}, u32[]{:S(2)}) copy-start(f32[20,8,128]{2,1,0:T(8,128)S(1)} %collective-permute-done.4.y0_hbm) | copy-start | bytes 245764
  26.6 2.7 %copy-start.4 = (f32[20,8,128]{2,1,0:T(8,128)}, f32[20,8,128]{2,1,0:T(8,128)S(1)}, u32[]{:S(2)}) copy-start(f32[20,8,128]{2,1,0:T(8,128)S(1)} %collective-permute-done.5.y1_hbm) | copy-start | bytes 245764
  36.3 8.1 %collective-permute-start.8 = (f32[8,1600]{1,0:T(8,128)}, f32[8,1600]{1,0:T(8,128)S(1)}, u32[]{:S(2)}, u32[]{:S(2)}) collective-permute-start(f32[8,1600]{1,0:T(8,128)} %get-tuple-element.37.z_hbm), channel_id=1, source_target_pairs={{0,3},{1,0},{2,1},{3,2},{4,7},{5,4},{6,5},{7,6},{8,11},{9,8},{10,9... | collective-permute-start | bytes 153608 | tf_op jit(solution)/shard_map/ppermute | solution.py:367
  36.8 7.5 %collective-permute-start.7 = (f32[8,1600]{1,0:T(8,128)}, f32[8,1600]{1,0:T(8,128)S(1)}, u32[]{:S(2)}, u32[]{:S(2)}) collective-permute-start(f32[8,1600]{1,0:T(8,128)} %get-tuple-element.37.z_hbm), channel_id=1, source_target_pairs={{0,1},{1,2},{2,3},{3,0},{4,5},{5,6},{6,7},{7,4},{8,9},{9,10},{10,1... | collective-permute-start | bytes 153608 | tf_op jit(solution)/shard_map/ppermute | solution.py:367
  39.6 6.4 %collective-permute-start.6 = (f32[4,40,128]{2,1,0:T(8,128)}, f32[4,40,128]{2,1,0:T(8,128)S(1)}, u32[]{:S(2)}, u32[]{:S(2)}) collective-permute-start(f32[4,40,128]{2,1,0:T(8,128)} %get-tuple-element.35), channel_id=1, source_target_pairs={{0,64},{64,128},{128,192},{192,0},{1,65},{65,129},{129,193},{193,1... | collective-permute-start | bytes 245768 | tf_op jit(solution)/shard_map/ppermute | solution.py:367
  40.8 5.6 %collective-permute-start.10 = (f32[20,8,128]{2,1,0:T(8,128)}, f32[20,8,128]{2,1,0:T(8,128)S(1)}, u32[]{:S(2)}, u32[]{:S(2)}) collective-permute-start(f32[20,8,128]{2,1,0:T(8,128)} %get-tuple-element.39), channel_id=1, source_target_pairs={{0,4},{4,8},{8,12},{12,16},{16,20},{20,24},{24,28},{28,32},{32,36}... | collective-permute-start | bytes 245768 | tf_op jit(solution)/shard_map/ppermute | solution.py:367
  41.3 5.1 %collective-permute-start.11 = (f32[20,8,128]{2,1,0:T(8,128)}, f32[20,8,128]{2,1,0:T(8,128)S(1)}, u32[]{:S(2)}, u32[]{:S(2)}) collective-permute-start(f32[20,8,128]{2,1,0:T(8,128)} %get-tuple-element.40), channel_id=1, source_target_pairs={{0,60},{4,0},{8,4},{12,8},{16,12},{20,16},{24,20},{28,24},{32,28},... | collective-permute-start | bytes 245768 | tf_op jit(solution)/shard_map/ppermute | solution.py:367
  44.4 4.1 %copy-start.12 = (f32[8,1600]{1,0:T(8,128)}, f32[8,1600]{1,0:T(8,128)S(1)}, u32[]{:S(2)}) copy-start(f32[8,1600]{1,0:T(8,128)S(1)} %collective-permute-done.8.z1_hbm) | copy-start | bytes 153604
  44.4 4.1 %copy-start.13 = (f32[8,1600]{1,0:T(8,128)}, f32[8,1600]{1,0:T(8,128)S(1)}, u32[]{:S(2)}) copy-start(f32[8,1600]{1,0:T(8,128)S(1)} %collective-permute-done.7.z0_hbm) | copy-start | bytes 153604
  44.4 4.1 %collective-permute-start.9 = (f32[4,40,128]{2,1,0:T(8,128)}, f32[4,40,128]{2,1,0:T(8,128)S(1)}, u32[]{:S(2)}, u32[]{:S(2)}) collective-permute-start(f32[4,40,128]{2,1,0:T(8,128)} %get-tuple-element.38), channel_id=1, source_target_pairs={{0,192},{64,0},{128,64},{192,128},{1,193},{65,1},{129,65},{193,129... | collective-permute-start | bytes 245768 | tf_op jit(solution)/shard_map/ppermute | solution.py:367
  46.0 2.5 %copy-start.5 = (f32[4,40,128]{2,1,0:T(8,128)}, f32[4,40,128]{2,1,0:T(8,128)S(1)}, u32[]{:S(2)}) copy-start(f32[4,40,128]{2,1,0:T(8,128)S(1)} %collective-permute-done.6.x0_hbm) | copy-start | bytes 245764
  46.4 2.1 %copy-start.6 = (f32[20,8,128]{2,1,0:T(8,128)}, f32[20,8,128]{2,1,0:T(8,128)S(1)}, u32[]{:S(2)}) copy-start(f32[20,8,128]{2,1,0:T(8,128)S(1)} %collective-permute-done.10.y0_hbm) | copy-start | bytes 245764
  46.4 2.1 %copy-start.8 = (f32[20,8,128]{2,1,0:T(8,128)}, f32[20,8,128]{2,1,0:T(8,128)S(1)}, u32[]{:S(2)}) copy-start(f32[20,8,128]{2,1,0:T(8,128)S(1)} %collective-permute-done.11.y1_hbm) | copy-start | bytes 245764
  (3 other events, 1.9 us)

commit v5 on v4

--- a/solution.py
+++ b/solution.py
@@ -11,7 +11,6 @@
 SURF = 8
 CAP = 64
 CHUNK = 20
-UNROLL = 20
 F32 = jnp.float32
 BF16 = jnp.bfloat16
 NT = (((1,), (1,)), ((), ()))
@@ -113,14 +112,21 @@
             copy.wait()
 
 
-def depth_faces(value):
-    at = iota((8, 128), 0)
-    take = iota((8, 128), 1) == jnp.where(at < 4, at, at + 120)
-    take = jnp.where(take, 1.0, 0.0).astype(BF16)
-    parts = [
-        lax.dot_general(take, s.astype(BF16), NT, preferred_element_type=F32) for s in split3(value)
-    ]
-    return parts[0] + parts[1] + parts[2]
+def depth_rows(cx, cy):
+    return -(-cx * cy // 128) * 8
+
+
+def depth_faces(src_ref, out_ref):
+    cx, cy, _ = src_ref.shape
+    per = cy // 8
+    group = lax.shift_right_logical(iota((8, 128), 1), 3)
+    for begin in range(0, cx * per, 16):
+        packed = jnp.zeros((8, 128), F32)
+        for i in range(begin, min(begin + 16, cx * per)):
+            k = i - begin
+            row = src_ref[i // per, i % per * 8 : i % per * 8 + 8, :]
+            packed = jnp.where(group == k, pltpu.roll(row, 4 + 8 * k, 1), packed)
+        out_ref[begin // 2 : begin // 2 + 8, :] = packed
 
 
 def send_kernel(
@@ -143,7 +149,7 @@
     store_y_faces(now_ref, y0_ref, y1_ref)
     copier.send(y0_ref, y0_hbm)
     copier.send(y1_ref, y1_hbm)
-    z_ref[...] = depth_faces(now_ref[...].reshape(cx * cy, cz))
+    depth_faces(now_ref, z_ref)
     copier.send(z_ref, z_hbm)
     copier.close()
 
@@ -211,29 +217,57 @@
         pad_ref[4 + half + x, 8 + cy : 12 + cy, :] = after[4:8]
 
 
-def depth_correction(own, before, after):
-    at = iota(own.shape, 0)
+def depth_correction(own_ref, before_ref, after_ref, out_ref):
+    own = own_ref[...]
+    cell = lax.bitwise_and(iota(own.shape, 1), 7)
     first, last = at_edges("gz")
-    delta = jnp.where(at < 4, jnp.where(last, 0.0, after), jnp.where(first, 0.0, before)) - own
-    row = iota((8, 128), 0)
-    lane = iota((8, 128), 1)
-    distance = jnp.where(row < 4, 128 + row - lane, lane + 8 - row)
-    weight = jnp.zeros((8, 128), F32)
+    before, after = jnp.where(first, 0.0, before_ref[...]), jnp.where(last, 0.0, after_ref[...])
+    high, middle, low = split3(jnp.where(cell < 4, before, after) - own)
+    source, target = iota((128, 128), 0), iota((128, 128), 1)
+    near = lax.shift_right_logical(source, 3) == lax.shift_right_logical(target, 3)
+    near = near & (lax.bitwise_and(source, 4) != lax.bitwise_and(target, 4))
+    distance = jnp.where(near, jnp.abs(source - target), 0)
+    weight = jnp.zeros((128, 128), F32)
     for j in range(1, 5):
         weight = jnp.where(distance == j, COEFFS[j], weight)
-    d, w = split3(delta), split3(weight)
-    left = jnp.concatenate([d[0], d[1], d[2], d[0], d[1], d[0]], axis=0).astype(BF16)
+    w = split3(weight)
+    left = jnp.concatenate([high, middle, low, high, middle, high], axis=1).astype(BF16)
     right = jnp.concatenate([w[0], w[0], w[0], w[1], w[1], w[2]], axis=0).astype(BF16)
-    return lax.dot_general(left, right, TN, preferred_element_type=F32)
+    result = jnp.dot(left, right, preferred_element_type=F32)
+    lane = iota((8, 128), 1)
+    outer = (lane < 4) | (lane >= 124)
+    for i in range(out_ref.shape[0]):
+        row = result[i // 16 * 8 : i // 16 * 8 + 8]
+        out_ref[i] = jnp.where(outer, pltpu.roll(row, 124 - i % 16 * 8, 1), 0.0)
+
+
+def depth_weights():
+    apart = jnp.abs(iota((128, 128), 0) - iota((128, 128), 1))
+    apart = jnp.minimum(apart, 128 - apart)
+    weight = jnp.zeros((128, 128), F32)
+    for j in range(1, 5):
+        weight = jnp.where(apart == j, COEFFS[j], weight)
+    high, middle, _ = split3(weight)
+    return jnp.concatenate([high, high, middle], axis=0).astype(BF16)
+
+
+def depth_part(pad_ref, weights, begin, cy, zc_ref):
+    rows = CHUNK * cy
+    value = pad_ref[4 + begin : 4 + begin + CHUNK, 8 : 8 + cy, :].reshape(rows, 128)
+    high, middle, _ = split3(value)
+    left = jnp.concatenate([high, middle, high], axis=1).astype(BF16)
+    result = jnp.dot(left, weights, preferred_element_type=F32)
+    at = begin * cy // 8
+    zc_ref[at : at + rows // 8] = zc_ref[at : at + rows // 8] + result.reshape(rows // 8, 8, 128)
 
 
 def lap_at(pad_ref, zc_ref, x, cy):
     center = pad_ref[x + 4, 8 : 8 + cy, :]
-    total = (3.0 * COEFFS[0]) * center + zc_ref[x]
+    per = cy // 8
+    total = (3.0 * COEFFS[0]) * center + zc_ref[x * per : (x + 1) * per].reshape(cy, center.shape[1])
     for j in range(1, 5):
         pair = pad_ref[x + 4 - j, 8 : 8 + cy, :] + pad_ref[x + 4 + j, 8 : 8 + cy, :]
         pair = pair + (pad_ref[x + 4, 8 - j : 8 - j + cy, :] + pad_ref[x + 4, 8 + j : 8 + j + cy, :])
-        pair = pair + (pltpu.roll(center, j, 1) + pltpu.roll(center, 128 - j, 1))
         total = total + COEFFS[j] * pair
     return center, total
 
@@ -245,7 +279,8 @@
 
 def source_at(source_ref, x, low):
     piece = source_ref[x // 16]
-    piece = pltpu.roll(piece, lax.rem(128 - lax.rem(x, 16) * SURF, 128), 1)
+    if x % 16:
+        piece = pltpu.roll(piece, 128 - x % 16 * SURF, 1)
     return jnp.where(low, piece, 0.0)
 
 
@@ -286,28 +321,30 @@
     for copy in halo:
         copy.wait()
     fill_xy(pad_ref, y0_ref, y1_ref)
-    zc_ref[...] = depth_correction(z_ref[...], z0_ref[...], z1_ref[...]).reshape(cx, cy, cz)
+    depth_correction(z_ref, z0_ref, z1_ref, zc_ref)
     now.wait()
     low = iota((cy, cz), 1) < SURF
-
-    def body(x, carry):
+    weights = depth_weights()
+
+    def step(x):
         center, lap = lap_at(pad_ref, zc_ref, x, cy)
         lap = lap + source_at(source_ref, x, low)
         fresh_ref[x] = 2.0 * center - late_ref[x] + courant_ref[x] * lap
-        return carry
 
     for c, copies in enumerate(chunks):
         for copy in copies:
             copy.wait()
         part = pl.ds(c * CHUNK, CHUNK)
-        lax.fori_loop(c * CHUNK, (c + 1) * CHUNK, body, 0, unroll=UNROLL)
+        depth_part(pad_ref, weights, c * CHUNK, cy, zc_ref)
+        for x in range(c * CHUNK, (c + 1) * CHUNK):
+            step(x)
         copier.send(fresh_ref.at[part], fresh_hbm.at[part])
     for src, dst in zip(x_faces(fresh_ref), (xs0_hbm, xs1_hbm)):
         copier.send(src, dst)
     store_y_faces(fresh_ref, ys0_ref, ys1_ref)
     copier.send(ys0_ref, ys0_hbm)
     copier.send(ys1_ref, ys1_hbm)
-    zs_ref[...] = depth_faces(fresh_ref[...].reshape(cx * cy, cz))
+    depth_faces(fresh_ref, zs_ref)
     copier.send(zs_ref, zs_hbm)
     copier.close()
 
@@ -338,25 +375,27 @@
     for copy in halo:
         copy.wait()
     fill_xy(pad_ref, y0_ref, y1_ref)
-    zc_ref[...] = depth_correction(z_ref[...], z0_ref[...], z1_ref[...]).reshape(cx, cy, cz)
+    depth_correction(z_ref, z0_ref, z1_ref, zc_ref)
     now.wait()
     source.wait()
     low = iota((cy, cz), 1) < SURF
-
-    def body(x, carry):
+    weights = depth_weights()
+
+    def step(x):
         center, lap = lap_at(pad_ref, zc_ref, x, cy)
         lap = lap + source_at(source_ref, x, low)
         fresh = 2.0 * center - late_ref[x] + courant_ref[x] * lap
         fresh_ref[x] = fresh
         image = image_ref[x] + forward0_ref[x].astype(F32) * center
         image_ref[x] = image + forward1_ref[x].astype(F32) * fresh
-        return carry
 
     for c, copies in enumerate(chunks):
         for copy in copies:
             copy.wait()
         part = pl.ds(c * CHUNK, CHUNK)
-        lax.fori_loop(c * CHUNK, (c + 1) * CHUNK, body, 0, unroll=UNROLL)
+        depth_part(pad_ref, weights, c * CHUNK, cy, zc_ref)
+        for x in range(c * CHUNK, (c + 1) * CHUNK):
+            step(x)
         copier.send(fresh_ref.at[part], fresh_hbm.at[part])
         copier.send(image_ref.at[part], image_out_hbm.at[part])
     copier.close()
@@ -405,9 +444,10 @@
     groups = -(-cx * SURF // 128)
     block = struct(cx, cy, cz)
     x_face, y_face = struct(4, cy, cz), struct(cx // 2, 8, cz)
-    faces = (x_face, x_face, y_face, y_face, struct(8, cx * cy))
-    grid, y_in, z_in = vm(cx, cy, cz), vm(cx // 2, 8, cz), vm(8, cx * cy)
+    faces = (x_face, x_face, y_face, y_face, struct(depth_rows(cx, cy), 128))
+    grid, y_in, z_in = vm(cx, cy, cz), vm(cx // 2, 8, cz), vm(depth_rows(cx, cy), 128)
     pad = vm(cx + 8, cy + 16, cz)
+    corrections = vm(cx * cy // 8, 8, cz)
     slots = (n_gy * n_gz, 2, 128)
     packed, *out_faces = call(
         functools.partial(send_kernel, n_gy, n_gz), (struct(*slots),) + faces,
@@ -426,7 +466,7 @@
         first_kernel, (block, struct(*source)) + faces,
         (received,) + halo + (adjoint_now, adjoint_late, courant),
         (
-            vm(*slots), pad, y_in, y_in, z_in, z_in, z_in, grid, grid, grid,
+            vm(*slots), pad, y_in, y_in, z_in, z_in, z_in, corrections, grid, grid,
             grid, vm(*source), vm(*source), y_in, y_in, z_in,
         ),
         15 + 3 * turns,
@@ -437,7 +477,7 @@
         second_kernel, (block, block),
         (middle, later) + halo + (adjoint_now, courant, forward, image_in),
         (
-            vm(*source), pad, y_in, y_in, z_in, z_in, z_in, grid, grid, grid,
+            vm(*source), pad, y_in, y_in, z_in, z_in, z_in, corrections, grid, grid,
             half, half, grid, grid,
         ),
         9 + 7 * turns,

time: 54.5 us -> 52.7 us (0.967)
  Pallas kernels: 13.3 us -> 11.6 us
    pallas_call x3, Pallas kernels: 13.3 us -> 11.6 us  [call(): pl.pallas_call(kernel, out_shape=outs, in_specs=[anywhere] * len(args), o...]
where the time goes in v5:
time: 52.7 us; the launch traced here: 52.5 us
  starting transfers between devices  32 us (61%)
  Pallas kernels  11.6 us (22%)
  waiting for transfers between devices  6.16 us (12%)
  local copies, waits for them, and re-layouts  1.86 us (4%)
  between operations  0.93 us (2%)
    ppermute x12, starting transfers between devices, turn(): lax.ppermute(value, axis, [(i, (i + by) % count) for i in range(count)])  20.5 us
    pallas_call x3, Pallas kernels, call(): pl.pallas_call(kernel, out_shape=outs, in_specs=[anywhere] * len(args), o...  11.6 us
    all_to_all x1, starting transfers between devices, on_device(): received = lax.all_to_all(packed, ('gz', 'gy'), 0, 0)  11.5 us
    ppermute x12, waiting for transfers between devices, turn(): lax.ppermute(value, axis, [(i, (i + by) % count) for i in range(count)])  3.55 us
    all_to_all x1, waiting for transfers between devices, on_device(): received = lax.all_to_all(packed, ('gz', 'gy'), 0, 0)  2.61 us
    unnamed x28, local copies, waits for them, and re-layouts  1.86 us
  transfers between devices with their start and end apart: 13, of which 4 were waited for; matrix products, arithmetic and copies ran while one was open for 0% of the time, Pallas kernels for 0%

profile of v5, /device:TPU:1, one launch (start us, length us, event | category | flops | bytes accessed | tf_op | source)
XLA Modules:
  0.0 52.5 jit_solution(2877439411514790469)
XLA Ops:
  0.6 2.2 %shard_map.103 = (f32[64,2,128]{2,1,0:T(2,128)}, f32[4,40,128]{2,1,0:T(8,128)}, f32[4,40,128]{2,1,0:T(8,128)}, f32[20,8,128]{2,1,0:T(8,128)}, f32[20,8,128]{2,1,0:T(8,128)}, /*index=5*/f32[104,128]{1,0:T(8,128)}) custom-call(f32[2,1024]{1,0:T(2,128)} %traces_hbm.1, s32[8,128]{1,0:T(8,128)} %bitcast.2, s32[8,128]{1,0:T(8,128)} %bitcast.3, f32[40,40,128]{2,1,0:T(8,128)} %late_hbm.3), custom_call_target="tpu_custom_call" | custom-call | flops 10000000000 | bytes 1282048 | tf_op jit(solution)/shard_map/pallas_call | solution.py:429
  2.8 0.0 copy-start.1
  2.8 3.3 %collective-permute-start.2 = (f32[104,128]{1,0:T(8,128)}, f32[104,128]{1,0:T(8,128)S(1)}, u32[]{:S(2)}, u32[]{:S(2)}) collective-permute-start(f32[104,128]{1,0:T(8,128)} %get-tuple-element.27.z_hbm), channel_id=1, source_target_pairs={{0,3},{1,0},{2,1},{3,2},{4,7},{5,4},{6,5},{7,6},{8,11},{9,8},{10,9... | collective-permute-start | bytes 159752 | tf_op jit(solution)/shard_map/ppermute | solution.py:406
  6.2 1.2 %collective-permute-start.1 = (f32[104,128]{1,0:T(8,128)}, f32[104,128]{1,0:T(8,128)S(1)}, u32[]{:S(2)}, u32[]{:S(2)}) collective-permute-start(f32[104,128]{1,0:T(8,128)} %get-tuple-element.27.z_hbm), channel_id=1, source_target_pairs={{0,1},{1,2},{2,3},{3,0},{4,5},{5,6},{6,7},{7,4},{8,9},{9,10},{10,1... | collective-permute-start | bytes 159752 | tf_op jit(solution)/shard_map/ppermute | solution.py:406
  7.3 11.5 %all-to-all-start = ((f32[64,2,128]{2,1,0:T(2,128)}), f32[64,2,128]{2,1,0:T(2,128)S(1)}, u32[]{:S(2)}, u32[]{:S(2)}) async-start(f32[64,2,128]{2,1,0:T(2,128)} %get-tuple-element.24), calls=%async_computation | async-start | bytes 131072 | tf_op jit(solution)/shard_map/all_to_all | solution.py:461
  18.8 1.3 %collective-permute-start = (f32[4,40,128]{2,1,0:T(8,128)}, f32[4,40,128]{2,1,0:T(8,128)S(1)}, u32[]{:S(2)}, u32[]{:S(2)}) collective-permute-start(f32[4,40,128]{2,1,0:T(8,128)} %get-tuple-element.25), channel_id=1, source_target_pairs={{0,64},{64,128},{128,192},{192,0},{1,65},{65,129},{129,193},{193,1... | collective-permute-start | bytes 245768 | tf_op jit(solution)/shard_map/ppermute | solution.py:406
  20.1 1.4 %collective-permute-start.4 = (f32[20,8,128]{2,1,0:T(8,128)}, f32[20,8,128]{2,1,0:T(8,128)S(1)}, u32[]{:S(2)}, u32[]{:S(2)}) collective-permute-start(f32[20,8,128]{2,1,0:T(8,128)} %get-tuple-element.29), channel_id=1, source_target_pairs={{0,4},{4,8},{8,12},{12,16},{16,20},{20,24},{24,28},{28,32},{32,36}... | collective-permute-start | bytes 245768 | tf_op jit(solution)/shard_map/ppermute | solution.py:406
  21.4 2.2 %collective-permute-start.5 = (f32[20,8,128]{2,1,0:T(8,128)}, f32[20,8,128]{2,1,0:T(8,128)S(1)}, u32[]{:S(2)}, u32[]{:S(2)}) collective-permute-start(f32[20,8,128]{2,1,0:T(8,128)} %get-tuple-element.30), channel_id=1, source_target_pairs={{0,60},{4,0},{8,4},{12,8},{16,12},{20,16},{24,20},{28,24},{32,28},... | collective-permute-start | bytes 245768 | tf_op jit(solution)/shard_map/ppermute | solution.py:406
  23.7 1.5 %collective-permute-start.3 = (f32[4,40,128]{2,1,0:T(8,128)S(1)}, f32[4,40,128]{2,1,0:T(8,128)S(1)}, u32[]{:S(2)}, u32[]{:S(2)}) collective-permute-start(f32[4,40,128]{2,1,0:T(8,128)S(1)} %copy-done.1), channel_id=1, source_target_pairs={{0,192},{64,0},{128,64},{192,128},{1,193},{65,1},{129,65},{193,129... | collective-permute-start | bytes 245768 | tf_op jit(solution)/shard_map/ppermute | solution.py:406
  25.2 1.0 %collective-permute-done.4.y0_hbm = f32[20,8,128]{2,1,0:T(8,128)S(1)} collective-permute-done((f32[20,8,128]{2,1,0:T(8,128)}, f32[20,8,128]{2,1,0:T(8,128)S(1)}, u32[]{:S(2)}, u32[]{:S(2)}) %collective-permute-start.4) | collective-permute-done | bytes 81952 | tf_op jit(solution)/shard_map/ppermute | solution.py:406
  26.2 2.6 %all-to-all-done.recv_hbm = f32[64,2,128]{2,1,0:T(2,128)S(1)} async-done(((f32[64,2,128]{2,1,0:T(2,128)}), f32[64,2,128]{2,1,0:T(2,128)S(1)}, u32[]{:S(2)}, u32[]{:S(2)}) %all-to-all-start) | async-done | bytes 65568 | tf_op jit(solution)/shard_map/all_to_all | solution.py:461
  28.9 0.6 %copy-done = f32[64,2,128]{2,1,0:T(2,128)} copy-done((f32[64,2,128]{2,1,0:T(2,128)}, f32[64,2,128]{2,1,0:T(2,128)S(1)}, u32[]{:S(2)}) %copy-start) | copy-done | bytes 65560
  29.5 0.6 %copy-done.7 = f32[4,40,128]{2,1,0:T(8,128)} copy-done((f32[4,40,128]{2,1,0:T(8,128)}, f32[4,40,128]{2,1,0:T(8,128)S(1)}, u32[]{:S(2)}) %copy-start.7) | copy-done | bytes 81944
  30.1 5.1 %shard_map.104 = (f32[40,40,128]{2,1,0:T(8,128)}, f32[3,40,128]{2,1,0:T(8,128)}, f32[4,40,128]{2,1,0:T(8,128)}, f32[4,40,128]{2,1,0:T(8,128)}, f32[20,8,128]{2,1...) custom-call(f32[64,2,128]{2,1,0:T(2,128)} %copy-done, f32[4,40,128]{2,1,0:T(8,128)} %copy-done.2, ...), custom_call_target="tpu_custom_call" | custom-call | flops 10000000000 | bytes 4272128 | tf_op jit(solution)/shard_map/pallas_call | solution.py:429
  35.2 0.6 %collective-permute-start.8 = (f32[104,128]{1,0:T(8,128)}, f32[104,128]{1,0:T(8,128)S(1)}, u32[]{:S(2)}, u32[]{:S(2)}) collective-permute-start(f32[104,128]{1,0:T(8,128)} %get-tuple-element.37.z_hbm), channel_id=1, source_target_pairs={{0,3},{1,0},{2,1},{3,2},{4,7},{5,4},{6,5},{7,6},{8,11},{9,8},{10,9... | collective-permute-start | bytes 159752 | tf_op jit(solution)/shard_map/ppermute | solution.py:406
  35.8 2.7 %collective-permute-start.7 = (f32[104,128]{1,0:T(8,128)}, f32[104,128]{1,0:T(8,128)S(1)}, u32[]{:S(2)}, u32[]{:S(2)}) collective-permute-start(f32[104,128]{1,0:T(8,128)} %get-tuple-element.37.z_hbm), channel_id=1, source_target_pairs={{0,1},{1,2},{2,3},{3,0},{4,5},{5,6},{6,7},{7,4},{8,9},{9,10},{10,1... | collective-permute-start | bytes 159752 | tf_op jit(solution)/shard_map/ppermute | solution.py:406
  38.5 1.2 %collective-permute-start.6 = (f32[4,40,128]{2,1,0:T(8,128)}, f32[4,40,128]{2,1,0:T(8,128)S(1)}, u32[]{:S(2)}, u32[]{:S(2)}) collective-permute-start(f32[4,40,128]{2,1,0:T(8,128)} %get-tuple-element.35), channel_id=1, source_target_pairs={{0,64},{64,128},{128,192},{192,0},{1,65},{65,129},{129,193},{193,1... | collective-permute-start | bytes 245768 | tf_op jit(solution)/shard_map/ppermute | solution.py:406
  39.8 0.5 collective-permute-start.10
  40.3 3.1 %collective-permute-start.11 = (f32[20,8,128]{2,1,0:T(8,128)}, f32[20,8,128]{2,1,0:T(8,128)S(1)}, u32[]{:S(2)}, u32[]{:S(2)}) collective-permute-start(f32[20,8,128]{2,1,0:T(8,128)} %get-tuple-element.40), channel_id=1, source_target_pairs={{0,60},{4,0},{8,4},{12,8},{16,12},{20,16},{24,20},{28,24},{32,28},... | collective-permute-start | bytes 245768 | tf_op jit(solution)/shard_map/ppermute | solution.py:406
  43.3 1.5 %collective-permute-start.9 = (f32[4,40,128]{2,1,0:T(8,128)}, f32[4,40,128]{2,1,0:T(8,128)S(1)}, u32[]{:S(2)}, u32[]{:S(2)}) collective-permute-start(f32[4,40,128]{2,1,0:T(8,128)} %get-tuple-element.38), channel_id=1, source_target_pairs={{0,192},{64,0},{128,64},{192,128},{1,193},{65,1},{129,65},{193,129... | collective-permute-start | bytes 245768 | tf_op jit(solution)/shard_map/ppermute | solution.py:406
  44.9 0.5 collective-permute-done.10.y0_hbm
  45.4 2.1 %collective-permute-done.9.x1_hbm = f32[4,40,128]{2,1,0:T(8,128)S(1)} collective-permute-done((f32[4,40,128]{2,1,0:T(8,128)}, f32[4,40,128]{2,1,0:T(8,128)S(1)}, u32[]{:S(2)}, u32[]{:S(2)}) %collective-permute-start.9) | collective-permute-done | bytes 81952 | tf_op jit(solution)/shard_map/ppermute | solution.py:406
  47.5 0.6 %copy-done.9 = f32[4,40,128]{2,1,0:T(8,128)} copy-done((f32[4,40,128]{2,1,0:T(8,128)}, f32[4,40,128]{2,1,0:T(8,128)S(1)}, u32[]{:S(2)}) %copy-start.9) | copy-done | bytes 81944
  48.1 4.3 %shard_map.105 = (f32[40,40,128]{2,1,0:T(8,128)}, f32[40,40,128]{2,1,0:T(8,128)}) custom-call(f32[40,40,128]{2,1,0:T(8,128)} %get-tuple-element.22.now_hbm, f32[3,40,128]{2,1,0:T(8,128)} %get-tuple-element.34.source_hbm, f32[4,40,128]{2,1,0:T(8,128)} %copy-done.5, f32[4,40,128]{2,1,0:T(8,128)} %copy-done.9, f32[20,8,128]{2,1,0:T(8,128)} %copy-done.6, ...), custom_call_target="tpu_custom_call" | custom-call | flops 10000000000 | bytes 6283264 | tf_op jit(solution)/shard_map/pallas_call | solution.py:429
  (33 shorter events, 0.1 us)
Async XLA Ops:
  2.8 20.8 %copy-start.1 = (f32[4,40,128]{2,1,0:T(8,128)S(1)}, f32[4,40,128]{2,1,0:T(8,128)}, u32[]{:S(2)}) copy-start(f32[4,40,128]{2,1,0:T(8,128)} %get-tuple-element.28) | copy-start | bytes 245764
  2.8 20.8 %collective-permute-start.2 = (f32[104,128]{1,0:T(8,128)}, f32[104,128]{1,0:T(8,128)S(1)}, u32[]{:S(2)}, u32[]{:S(2)}) collective-permute-start(f32[104,128]{1,0:T(8,128)} %get-tuple-element.27.z_hbm), channel_id=1, source_target_pairs={{0,3},{1,0},{2,1},{3,2},{4,7},{5,4},{6,5},{7,6},{8,11},{9,8},{10,9... | collective-permute-start | bytes 159752 | tf_op jit(solution)/shard_map/ppermute | solution.py:406
  6.2 17.5 %collective-permute-start.1 = (f32[104,128]{1,0:T(8,128)}, f32[104,128]{1,0:T(8,128)S(1)}, u32[]{:S(2)}, u32[]{:S(2)}) collective-permute-start(f32[104,128]{1,0:T(8,128)} %get-tuple-element.27.z_hbm), channel_id=1, source_target_pairs={{0,1},{1,2},{2,3},{3,0},{4,5},{5,6},{6,7},{7,4},{8,9},{9,10},{10,1... | collective-permute-start | bytes 159752 | tf_op jit(solution)/shard_map/ppermute | solution.py:406
  7.3 21.5 %all-to-all-start = ((f32[64,2,128]{2,1,0:T(2,128)}), f32[64,2,128]{2,1,0:T(2,128)S(1)}, u32[]{:S(2)}, u32[]{:S(2)}) async-start(f32[64,2,128]{2,1,0:T(2,128)} %get-tuple-element.24), calls=%async_computation | async-start | bytes 131072 | tf_op jit(solution)/shard_map/all_to_all | solution.py:461
  18.8 6.4 %collective-permute-start = (f32[4,40,128]{2,1,0:T(8,128)}, f32[4,40,128]{2,1,0:T(8,128)S(1)}, u32[]{:S(2)}, u32[]{:S(2)}) collective-permute-start(f32[4,40,128]{2,1,0:T(8,128)} %get-tuple-element.25), channel_id=1, source_target_pairs={{0,64},{64,128},{128,192},{192,0},{1,65},{65,129},{129,193},{193,1... | collective-permute-start | bytes 245768 | tf_op jit(solution)/shard_map/ppermute | solution.py:406
  20.1 6.2 %collective-permute-start.4 = (f32[20,8,128]{2,1,0:T(8,128)}, f32[20,8,128]{2,1,0:T(8,128)S(1)}, u32[]{:S(2)}, u32[]{:S(2)}) collective-permute-start(f32[20,8,128]{2,1,0:T(8,128)} %get-tuple-element.29), channel_id=1, source_target_pairs={{0,4},{4,8},{8,12},{12,16},{16,20},{20,24},{24,28},{28,32},{32,36}... | collective-permute-start | bytes 245768 | tf_op jit(solution)/shard_map/ppermute | solution.py:406
  21.4 4.8 %collective-permute-start.5 = (f32[20,8,128]{2,1,0:T(8,128)}, f32[20,8,128]{2,1,0:T(8,128)S(1)}, u32[]{:S(2)}, u32[]{:S(2)}) collective-permute-start(f32[20,8,128]{2,1,0:T(8,128)} %get-tuple-element.30), channel_id=1, source_target_pairs={{0,60},{4,0},{8,4},{12,8},{16,12},{20,16},{24,20},{28,24},{32,28},... | collective-permute-start | bytes 245768 | tf_op jit(solution)/shard_map/ppermute | solution.py:406
  23.6 5.2 %copy-start.10 = (f32[104,128]{1,0:T(8,128)}, f32[104,128]{1,0:T(8,128)S(1)}, u32[]{:S(2)}) copy-start(f32[104,128]{1,0:T(8,128)S(1)} %collective-permute-done.2.z1_hbm) | copy-start | bytes 159748
  23.6 5.2 %copy-start.11 = (f32[104,128]{1,0:T(8,128)}, f32[104,128]{1,0:T(8,128)S(1)}, u32[]{:S(2)}) copy-start(f32[104,128]{1,0:T(8,128)S(1)} %collective-permute-done.1.z0_hbm) | copy-start | bytes 159748
  23.7 5.2 %collective-permute-start.3 = (f32[4,40,128]{2,1,0:T(8,128)S(1)}, f32[4,40,128]{2,1,0:T(8,128)S(1)}, u32[]{:S(2)}, u32[]{:S(2)}) collective-permute-start(f32[4,40,128]{2,1,0:T(8,128)S(1)} %copy-done.1), channel_id=1, source_target_pairs={{0,192},{64,0},{128,64},{192,128},{1,193},{65,1},{129,65},{193,129... | collective-permute-start | bytes 245768 | tf_op jit(solution)/shard_map/ppermute | solution.py:406
  25.2 3.6 %copy-start.2 = (f32[4,40,128]{2,1,0:T(8,128)}, f32[4,40,128]{2,1,0:T(8,128)S(1)}, u32[]{:S(2)}) copy-start(f32[4,40,128]{2,1,0:T(8,128)S(1)} %collective-permute-done.x0_hbm) | copy-start | bytes 245764
  26.2 2.6 %copy-start.3 = (f32[20,8,128]{2,1,0:T(8,128)}, f32[20,8,128]{2,1,0:T(8,128)S(1)}, u32[]{:S(2)}) copy-start(f32[20,8,128]{2,1,0:T(8,128)S(1)} %collective-permute-done.4.y0_hbm) | copy-start | bytes 245764
  26.2 2.7 %copy-start.4 = (f32[20,8,128]{2,1,0:T(8,128)}, f32[20,8,128]{2,1,0:T(8,128)S(1)}, u32[]{:S(2)}) copy-start(f32[20,8,128]{2,1,0:T(8,128)S(1)} %collective-permute-done.5.y1_hbm) | copy-start | bytes 245764
  35.2 8.1 %collective-permute-start.8 = (f32[104,128]{1,0:T(8,128)}, f32[104,128]{1,0:T(8,128)S(1)}, u32[]{:S(2)}, u32[]{:S(2)}) collective-permute-start(f32[104,128]{1,0:T(8,128)} %get-tuple-element.37.z_hbm), channel_id=1, source_target_pairs={{0,3},{1,0},{2,1},{3,2},{4,7},{5,4},{6,5},{7,6},{8,11},{9,8},{10,9... | collective-permute-start | bytes 159752 | tf_op jit(solution)/shard_map/ppermute | solution.py:406
  35.8 7.5 %collective-permute-start.7 = (f32[104,128]{1,0:T(8,128)}, f32[104,128]{1,0:T(8,128)S(1)}, u32[]{:S(2)}, u32[]{:S(2)}) collective-permute-start(f32[104,128]{1,0:T(8,128)} %get-tuple-element.37.z_hbm), channel_id=1, source_target_pairs={{0,1},{1,2},{2,3},{3,0},{4,5},{5,6},{6,7},{7,4},{8,9},{9,10},{10,1... | collective-permute-start | bytes 159752 | tf_op jit(solution)/shard_map/ppermute | solution.py:406
  38.5 6.4 %collective-permute-start.6 = (f32[4,40,128]{2,1,0:T(8,128)}, f32[4,40,128]{2,1,0:T(8,128)S(1)}, u32[]{:S(2)}, u32[]{:S(2)}) collective-permute-start(f32[4,40,128]{2,1,0:T(8,128)} %get-tuple-element.35), channel_id=1, source_target_pairs={{0,64},{64,128},{128,192},{192,0},{1,65},{65,129},{129,193},{193,1... | collective-permute-start | bytes 245768 | tf_op jit(solution)/shard_map/ppermute | solution.py:406
  39.8 5.6 %collective-permute-start.10 = (f32[20,8,128]{2,1,0:T(8,128)}, f32[20,8,128]{2,1,0:T(8,128)S(1)}, u32[]{:S(2)}, u32[]{:S(2)}) collective-permute-start(f32[20,8,128]{2,1,0:T(8,128)} %get-tuple-element.39), channel_id=1, source_target_pairs={{0,4},{4,8},{8,12},{12,16},{16,20},{20,24},{24,28},{28,32},{32,36}... | collective-permute-start | bytes 245768 | tf_op jit(solution)/shard_map/ppermute | solution.py:406
  40.3 5.1 %collective-permute-start.11 = (f32[20,8,128]{2,1,0:T(8,128)}, f32[20,8,128]{2,1,0:T(8,128)S(1)}, u32[]{:S(2)}, u32[]{:S(2)}) collective-permute-start(f32[20,8,128]{2,1,0:T(8,128)} %get-tuple-element.40), channel_id=1, source_target_pairs={{0,60},{4,0},{8,4},{12,8},{16,12},{20,16},{24,20},{28,24},{32,28},... | collective-permute-start | bytes 245768 | tf_op jit(solution)/shard_map/ppermute | solution.py:406
  43.3 4.1 %copy-start.12 = (f32[104,128]{1,0:T(8,128)}, f32[104,128]{1,0:T(8,128)S(1)}, u32[]{:S(2)}) copy-start(f32[104,128]{1,0:T(8,128)S(1)} %collective-permute-done.8.z1_hbm) | copy-start | bytes 159748
  43.3 4.1 %copy-start.13 = (f32[104,128]{1,0:T(8,128)}, f32[104,128]{1,0:T(8,128)S(1)}, u32[]{:S(2)}) copy-start(f32[104,128]{1,0:T(8,128)S(1)} %collective-permute-done.7.z0_hbm) | copy-start | bytes 159748
  43.3 4.1 %collective-permute-start.9 = (f32[4,40,128]{2,1,0:T(8,128)}, f32[4,40,128]{2,1,0:T(8,128)S(1)}, u32[]{:S(2)}, u32[]{:S(2)}) collective-permute-start(f32[4,40,128]{2,1,0:T(8,128)} %get-tuple-element.38), channel_id=1, source_target_pairs={{0,192},{64,0},{128,64},{192,128},{1,193},{65,1},{129,65},{193,129... | collective-permute-start | bytes 245768 | tf_op jit(solution)/shard_map/ppermute | solution.py:406
  44.9 2.5 %copy-start.5 = (f32[4,40,128]{2,1,0:T(8,128)}, f32[4,40,128]{2,1,0:T(8,128)S(1)}, u32[]{:S(2)}) copy-start(f32[4,40,128]{2,1,0:T(8,128)S(1)} %collective-permute-done.6.x0_hbm) | copy-start | bytes 245764
  45.4 2.1 %copy-start.6 = (f32[20,8,128]{2,1,0:T(8,128)}, f32[20,8,128]{2,1,0:T(8,128)S(1)}, u32[]{:S(2)}) copy-start(f32[20,8,128]{2,1,0:T(8,128)S(1)} %collective-permute-done.10.y0_hbm) | copy-start | bytes 245764
  45.4 2.1 %copy-start.8 = (f32[20,8,128]{2,1,0:T(8,128)}, f32[20,8,128]{2,1,0:T(8,128)S(1)}, u32[]{:S(2)}) copy-start(f32[20,8,128]{2,1,0:T(8,128)S(1)} %collective-permute-done.11.y1_hbm) | copy-start | bytes 245764
  (3 other events, 1.9 us)

commit v6 on v5

--- a/solution.py
+++ b/solution.py
@@ -406,11 +406,14 @@
     return lax.ppermute(value, axis, [(i, (i + by) % count) for i in range(count)])
 
 
-def exchange(x_low, x_high, y_low, y_high, z):
+def exchange(x_low, x_high, y_low, y_high, z, both):
     z_before, z_after = turn(z, "gz", 1), turn(z, "gz", -1)
     y_before, y_after = turn(y_high, "gy", 1), turn(y_low, "gy", -1)
     x_before = turn(x_high, "gx", 1)
-    x_low, z_before, z_after = lax.optimization_barrier((x_low, z_before, z_after))
+    if both:
+        x_low, z_before, z_after = lax.optimization_barrier((x_low, z_before, z_after))
+    else:
+        x_low, z_after = lax.optimization_barrier((x_low, z_after))
     x_after = turn(x_low, "gx", -1)
     return x_before, x_after, y_before, y_after, z, z_before, z_after
 
@@ -459,7 +462,7 @@
         10,
     )
     received = lax.all_to_all(packed, ("gz", "gy"), 0, 0)
-    halo = exchange(*out_faces)
+    halo = exchange(*out_faces, False)
     turns = cx // CHUNK
     source = (groups, cy, 128)
     middle, later, *out_faces = call(
@@ -471,7 +474,7 @@
         ),
         15 + 3 * turns,
     )
-    halo = exchange(*out_faces)
+    halo = exchange(*out_faces, True)
     half = vm(cx, cy, cz, dtype=BF16)
     newest, image = call(
         second_kernel, (block, block),

time: 52.7 us -> 52.6 us (level)
  waiting for transfers between devices: 6.16 us -> 3.01 us
  starting transfers between devices: 32 us -> 35 us
    ppermute x12, starting transfers between devices: 20.5 us -> 24.4 us  [turn(): lax.ppermute(value, axis, [(i, (i + by) % count) for i in range(count)])]
    all_to_all x1, waiting for transfers between devices: 2.61 us -> 0.01 us  [on_device(): received = lax.all_to_all(packed, ('gz', 'gy'), 0, 0)]
    all_to_all x1, starting transfers between devices: 11.5 us -> 10.5 us  [on_device(): received = lax.all_to_all(packed, ('gz', 'gy'), 0, 0)]
    ppermute x12, waiting for transfers between devices: 3.55 us -> 3 us  [turn(): lax.ppermute(value, axis, [(i, (i + by) % count) for i in range(count)])]
    unnamed x28 -> x30, local copies, waits for them, and re-layouts: 1.86 us -> 1.91 us
  transfers between devices with their start and end apart: 13 -> 13, of which waited for: 4 -> 2; matrix products, arithmetic and copies ran while one was open for 0% -> 0% of each run, Pallas kernels for 0% -> 0%
where the time goes in v6:
time: 52.6 us; the launch traced here: 52.4 us
  starting transfers between devices  35 us (67%)
  Pallas kernels  11.6 us (22%)
  waiting for transfers between devices  3.01 us (6%)
  local copies, waits for them, and re-layouts  1.91 us (4%)
  between operations  0.96 us (2%)
    ppermute x12, starting transfers between devices, turn(): lax.ppermute(value, axis, [(i, (i + by) % count) for i in range(count)])  24.4 us
    pallas_call x3, Pallas kernels, call(): pl.pallas_call(kernel, out_shape=outs, in_specs=[anywhere] * len(args), o...  11.6 us
    all_to_all x1, starting transfers between devices, on_device(): received = lax.all_to_all(packed, ('gz', 'gy'), 0, 0)  10.5 us
    ppermute x12, waiting for transfers between devices, turn(): lax.ppermute(value, axis, [(i, (i + by) % count) for i in range(count)])  3 us
    unnamed x30, local copies, waits for them, and re-layouts  1.91 us
  transfers between devices with their start and end apart: 13, of which 2 were waited for; matrix products, arithmetic and copies ran while one was open for 0% of the time, Pallas kernels for 0%

profile of v6, /device:TPU:1, one launch (start us, length us, event | category | flops | bytes accessed | tf_op | source)
XLA Modules:
  0.0 52.4 jit_solution(14497297611118972385)
XLA Ops:
  0.6 2.2 %shard_map.103 = (f32[64,2,128]{2,1,0:T(2,128)}, f32[4,40,128]{2,1,0:T(8,128)}, f32[4,40,128]{2,1,0:T(8,128)}, f32[20,8,128]{2,1,0:T(8,128)}, f32[20,8,128]{2,1,0:T(8,128)}, /*index=5*/f32[104,128]{1,0:T(8,128)}) custom-call(f32[2,1024]{1,0:T(2,128)} %traces_hbm.1, s32[8,128]{1,0:T(8,128)} %bitcast.2, s32[8,128]{1,0:T(8,128)} %bitcast.3, f32[40,40,128]{2,1,0:T(8,128)} %late_hbm.3), custom_call_target="tpu_custom_call" | custom-call | flops 10000000000 | bytes 1282048 | tf_op jit(solution)/shard_map/pallas_call | solution.py:432
  2.8 0.0 copy-start.2
  2.8 3.3 %collective-permute-start.1 = (f32[104,128]{1,0:T(8,128)}, f32[104,128]{1,0:T(8,128)S(1)}, u32[]{:S(2)}, u32[]{:S(2)}) collective-permute-start(f32[104,128]{1,0:T(8,128)} %get-tuple-element.26.z_hbm), channel_id=1, source_target_pairs={{0,3},{1,0},{2,1},{3,2},{4,7},{5,4},{6,5},{7,6},{8,11},{9,8},{10,9... | collective-permute-start | bytes 159752 | tf_op jit(solution)/shard_map/ppermute | solution.py:406
  6.1 10.5 %all-to-all-start = ((f32[64,2,128]{2,1,0:T(2,128)}), f32[64,2,128]{2,1,0:T(2,128)S(1)}, u32[]{:S(2)}, u32[]{:S(2)}) async-start(f32[64,2,128]{2,1,0:T(2,128)} %get-tuple-element.23), calls=%async_computation | async-start | bytes 131072 | tf_op jit(solution)/shard_map/all_to_all | solution.py:464
  16.7 1.3 %collective-permute-start = (f32[4,40,128]{2,1,0:T(8,128)}, f32[4,40,128]{2,1,0:T(8,128)S(1)}, u32[]{:S(2)}, u32[]{:S(2)}) collective-permute-start(f32[4,40,128]{2,1,0:T(8,128)} %get-tuple-element.24), channel_id=1, source_target_pairs={{0,64},{64,128},{128,192},{192,0},{1,65},{65,129},{129,193},{193,1... | collective-permute-start | bytes 245768 | tf_op jit(solution)/shard_map/ppermute | solution.py:406
  18.0 1.4 %collective-permute-start.3 = (f32[20,8,128]{2,1,0:T(8,128)}, f32[20,8,128]{2,1,0:T(8,128)S(1)}, u32[]{:S(2)}, u32[]{:S(2)}) collective-permute-start(f32[20,8,128]{2,1,0:T(8,128)} %get-tuple-element.28), channel_id=1, source_target_pairs={{0,4},{4,8},{8,12},{12,16},{16,20},{20,24},{24,28},{28,32},{32,36}... | collective-permute-start | bytes 245768 | tf_op jit(solution)/shard_map/ppermute | solution.py:406
  19.4 2.2 %collective-permute-start.4 = (f32[20,8,128]{2,1,0:T(8,128)}, f32[20,8,128]{2,1,0:T(8,128)S(1)}, u32[]{:S(2)}, u32[]{:S(2)}) collective-permute-start(f32[20,8,128]{2,1,0:T(8,128)} %get-tuple-element.29), channel_id=1, source_target_pairs={{0,60},{4,0},{8,4},{12,8},{16,12},{20,16},{24,20},{28,24},{32,28},... | collective-permute-start | bytes 245768 | tf_op jit(solution)/shard_map/ppermute | solution.py:406
  21.6 1.5 %collective-permute-start.2 = (f32[4,40,128]{2,1,0:T(8,128)S(1)}, f32[4,40,128]{2,1,0:T(8,128)S(1)}, u32[]{:S(2)}, u32[]{:S(2)}) collective-permute-start(f32[4,40,128]{2,1,0:T(8,128)S(1)} %copy-done.2), channel_id=1, source_target_pairs={{0,192},{64,0},{128,64},{192,128},{1,193},{65,1},{129,65},{193,129... | collective-permute-start | bytes 245768 | tf_op jit(solution)/shard_map/ppermute | solution.py:406
  23.1 4.3 %collective-permute-start.5 = (f32[104,128]{1,0:T(8,128)S(1)}, f32[104,128]{1,0:T(8,128)S(1)}, u32[]{:S(2)}, u32[]{:S(2)}) collective-permute-start(f32[104,128]{1,0:T(8,128)S(1)} %copy-done.10), channel_id=1, source_target_pairs={{0,1},{1,2},{2,3},{3,0},{4,5},{5,6},{6,7},{7,4},{8,9},{9,10},{10,1... | collective-permute-start | bytes 159752 | tf_op jit(solution)/shard_map/ppermute | solution.py:406
  27.5 1.2 %collective-permute-done.5.z0_hbm = f32[104,128]{1,0:T(8,128)S(1)} collective-permute-done((f32[104,128]{1,0:T(8,128)S(1)}, f32[104,128]{1,0:T(8,128)S(1)}, u32[]{:S(2)}, u32[]{:S(2)}) %collective-permute-start.5) | collective-permute-done | bytes 53280 | tf_op jit(solution)/shard_map/ppermute | solution.py:406
  28.8 0.5 %copy-done.14 = f32[104,128]{1,0:T(8,128)} copy-done((f32[104,128]{1,0:T(8,128)}, f32[104,128]{1,0:T(8,128)S(1)}, u32[]{:S(2)}) %copy-start.14) | copy-done | bytes 53272
  29.3 0.0 copy-done.1
  29.3 0.0 copy-done.3
  29.4 0.0 copy-done.4
  29.4 0.6 %copy-done.5 = f32[4,40,128]{2,1,0:T(8,128)} copy-done((f32[4,40,128]{2,1,0:T(8,128)}, f32[4,40,128]{2,1,0:T(8,128)S(1)}, u32[]{:S(2)}) %copy-start.5) | copy-done | bytes 81944
  30.0 5.1 %shard_map.104 = (f32[40,40,128]{2,1,0:T(8,128)}, f32[3,40,128]{2,1,0:T(8,128)}, f32[4,40,128]{2,1,0:T(8,128)}, f32[4,40,128]{2,1,0:T(8,128)}, f32[20,8,128]{2,1...) custom-call(f32[64,2,128]{2,1,0:T(2,128)} %copy-done, f32[4,40,128]{2,1,0:T(8,128)} %copy-done.1, ...), custom_call_target="tpu_custom_call" | custom-call | flops 10000000000 | bytes 4272128 | tf_op jit(solution)/shard_map/pallas_call | solution.py:432
  35.1 1.1 %collective-permute-start.8 = (f32[104,128]{1,0:T(8,128)}, f32[104,128]{1,0:T(8,128)S(1)}, u32[]{:S(2)}, u32[]{:S(2)}) collective-permute-start(f32[104,128]{1,0:T(8,128)} %get-tuple-element.35.z_hbm), channel_id=1, source_target_pairs={{0,3},{1,0},{2,1},{3,2},{4,7},{5,4},{6,5},{7,6},{8,11},{9,8},{10,9... | collective-permute-start | bytes 159752 | tf_op jit(solution)/shard_map/ppermute | solution.py:406
  36.3 2.9 %collective-permute-start.7 = (f32[104,128]{1,0:T(8,128)}, f32[104,128]{1,0:T(8,128)S(1)}, u32[]{:S(2)}, u32[]{:S(2)}) collective-permute-start(f32[104,128]{1,0:T(8,128)} %get-tuple-element.35.z_hbm), channel_id=1, source_target_pairs={{0,1},{1,2},{2,3},{3,0},{4,5},{5,6},{6,7},{7,4},{8,9},{9,10},{10,1... | collective-permute-start | bytes 159752 | tf_op jit(solution)/shard_map/ppermute | solution.py:406
  39.2 0.0 collective-permute-start.10
  39.2 3.6 %collective-permute-start.11 = (f32[20,8,128]{2,1,0:T(8,128)}, f32[20,8,128]{2,1,0:T(8,128)S(1)}, u32[]{:S(2)}, u32[]{:S(2)}) collective-permute-start(f32[20,8,128]{2,1,0:T(8,128)} %get-tuple-element.38), channel_id=1, source_target_pairs={{0,60},{4,0},{8,4},{12,8},{16,12},{20,16},{24,20},{28,24},{32,28},... | collective-permute-start | bytes 245768 | tf_op jit(solution)/shard_map/ppermute | solution.py:406
  42.8 2.8 %collective-permute-start.9 = (f32[4,40,128]{2,1,0:T(8,128)}, f32[4,40,128]{2,1,0:T(8,128)S(1)}, u32[]{:S(2)}, u32[]{:S(2)}) collective-permute-start(f32[4,40,128]{2,1,0:T(8,128)} %get-tuple-element.36), channel_id=1, source_target_pairs={{0,192},{64,0},{128,64},{192,128},{1,193},{65,1},{129,65},{193,129... | collective-permute-start | bytes 245768 | tf_op jit(solution)/shard_map/ppermute | solution.py:406
  45.6 1.8 %collective-permute-done.9.x1_hbm = f32[4,40,128]{2,1,0:T(8,128)S(1)} collective-permute-done((f32[4,40,128]{2,1,0:T(8,128)}, f32[4,40,128]{2,1,0:T(8,128)S(1)}, u32[]{:S(2)}, u32[]{:S(2)}) %collective-permute-start.9) | collective-permute-done | bytes 81952 | tf_op jit(solution)/shard_map/ppermute | solution.py:406
  47.4 0.6 %copy-done.9 = f32[4,40,128]{2,1,0:T(8,128)} copy-done((f32[4,40,128]{2,1,0:T(8,128)}, f32[4,40,128]{2,1,0:T(8,128)S(1)}, u32[]{:S(2)}) %copy-start.9) | copy-done | bytes 81944
  48.0 4.3 %shard_map.105 = (f32[40,40,128]{2,1,0:T(8,128)}, f32[40,40,128]{2,1,0:T(8,128)}) custom-call(f32[40,40,128]{2,1,0:T(8,128)} %get-tuple-element.21.now_hbm, f32[3,40,128]{2,1,0:T(8,128)} %get-tuple-element.32.source_hbm, f32[4,40,128]{2,1,0:T(8,128)} %copy-done.6, f32[4,40,128]{2,1,0:T(8,128)} %copy-done.9, f32[20,8,128]{2,1,0:T(8,128)} %copy-done.7, ...), custom_call_target="tpu_custom_call" | custom-call | flops 10000000000 | bytes 6283264 | tf_op jit(solution)/shard_map/pallas_call | solution.py:432
  (35 shorter events, 0.1 us)
Async XLA Ops:
  2.8 18.8 %copy-start.2 = (f32[4,40,128]{2,1,0:T(8,128)S(1)}, f32[4,40,128]{2,1,0:T(8,128)}, u32[]{:S(2)}) copy-start(f32[4,40,128]{2,1,0:T(8,128)} %get-tuple-element.27) | copy-start | bytes 245764
  2.8 18.7 %collective-permute-start.1 = (f32[104,128]{1,0:T(8,128)}, f32[104,128]{1,0:T(8,128)S(1)}, u32[]{:S(2)}, u32[]{:S(2)}) collective-permute-start(f32[104,128]{1,0:T(8,128)} %get-tuple-element.26.z_hbm), channel_id=1, source_target_pairs={{0,3},{1,0},{2,1},{3,2},{4,7},{5,4},{6,5},{7,6},{8,11},{9,8},{10,9... | collective-permute-start | bytes 159752 | tf_op jit(solution)/shard_map/ppermute | solution.py:406
  6.1 17.0 %copy-start.10 = (f32[104,128]{1,0:T(8,128)S(1)}, f32[104,128]{1,0:T(8,128)}, u32[]{:S(2)}) copy-start(f32[104,128]{1,0:T(8,128)} %get-tuple-element.26.z_hbm) | copy-start | bytes 159748
  6.1 22.6 %all-to-all-start = ((f32[64,2,128]{2,1,0:T(2,128)}), f32[64,2,128]{2,1,0:T(2,128)S(1)}, u32[]{:S(2)}, u32[]{:S(2)}) async-start(f32[64,2,128]{2,1,0:T(2,128)} %get-tuple-element.23), calls=%async_computation | async-start | bytes 131072 | tf_op jit(solution)/shard_map/all_to_all | solution.py:464
  16.7 12.0 %collective-permute-start = (f32[4,40,128]{2,1,0:T(8,128)}, f32[4,40,128]{2,1,0:T(8,128)S(1)}, u32[]{:S(2)}, u32[]{:S(2)}) collective-permute-start(f32[4,40,128]{2,1,0:T(8,128)} %get-tuple-element.24), channel_id=1, source_target_pairs={{0,64},{64,128},{128,192},{192,0},{1,65},{65,129},{129,193},{193,1... | collective-permute-start | bytes 245768 | tf_op jit(solution)/shard_map/ppermute | solution.py:406
  18.0 10.7 %collective-permute-start.3 = (f32[20,8,128]{2,1,0:T(8,128)}, f32[20,8,128]{2,1,0:T(8,128)S(1)}, u32[]{:S(2)}, u32[]{:S(2)}) collective-permute-start(f32[20,8,128]{2,1,0:T(8,128)} %get-tuple-element.28), channel_id=1, source_target_pairs={{0,4},{4,8},{8,12},{12,16},{16,20},{20,24},{24,28},{28,32},{32,36}... | collective-permute-start | bytes 245768 | tf_op jit(solution)/shard_map/ppermute | solution.py:406
  19.4 9.3 %collective-permute-start.4 = (f32[20,8,128]{2,1,0:T(8,128)}, f32[20,8,128]{2,1,0:T(8,128)S(1)}, u32[]{:S(2)}, u32[]{:S(2)}) collective-permute-start(f32[20,8,128]{2,1,0:T(8,128)} %get-tuple-element.29), channel_id=1, source_target_pairs={{0,60},{4,0},{8,4},{12,8},{16,12},{20,16},{24,20},{28,24},{32,28},... | collective-permute-start | bytes 245768 | tf_op jit(solution)/shard_map/ppermute | solution.py:406
  21.6 7.2 %copy-start.11 = (f32[104,128]{1,0:T(8,128)}, f32[104,128]{1,0:T(8,128)S(1)}, u32[]{:S(2)}) copy-start(f32[104,128]{1,0:T(8,128)S(1)} %collective-permute-done.1.z1_hbm) | copy-start | bytes 159748
  21.6 7.2 %collective-permute-start.2 = (f32[4,40,128]{2,1,0:T(8,128)S(1)}, f32[4,40,128]{2,1,0:T(8,128)S(1)}, u32[]{:S(2)}, u32[]{:S(2)}) collective-permute-start(f32[4,40,128]{2,1,0:T(8,128)S(1)} %copy-done.2), channel_id=1, source_target_pairs={{0,192},{64,0},{128,64},{192,128},{1,193},{65,1},{129,65},{193,129... | collective-permute-start | bytes 245768 | tf_op jit(solution)/shard_map/ppermute | solution.py:406
  23.1 5.6 %collective-permute-start.5 = (f32[104,128]{1,0:T(8,128)S(1)}, f32[104,128]{1,0:T(8,128)S(1)}, u32[]{:S(2)}, u32[]{:S(2)}) collective-permute-start(f32[104,128]{1,0:T(8,128)S(1)} %copy-done.10), channel_id=1, source_target_pairs={{0,1},{1,2},{2,3},{3,0},{4,5},{5,6},{6,7},{7,4},{8,9},{9,10},{10,1... | collective-permute-start | bytes 159752 | tf_op jit(solution)/shard_map/ppermute | solution.py:406
  28.7 0.7 %copy-start.3 = (f32[20,8,128]{2,1,0:T(8,128)}, f32[20,8,128]{2,1,0:T(8,128)S(1)}, u32[]{:S(2)}) copy-start(f32[20,8,128]{2,1,0:T(8,128)S(1)} %collective-permute-done.3.y0_hbm) | copy-start | bytes 245764
  28.7 0.7 %copy-start.4 = (f32[20,8,128]{2,1,0:T(8,128)}, f32[20,8,128]{2,1,0:T(8,128)S(1)}, u32[]{:S(2)}) copy-start(f32[20,8,128]{2,1,0:T(8,128)S(1)} %collective-permute-done.4.y1_hbm) | copy-start | bytes 245764
  28.7 0.7 %copy-start = (f32[64,2,128]{2,1,0:T(2,128)}, f32[64,2,128]{2,1,0:T(2,128)S(1)}, u32[]{:S(2)}) copy-start(f32[64,2,128]{2,1,0:T(2,128)S(1)} %all-to-all-done.recv_hbm) | copy-start | bytes 196612
  35.1 7.6 %collective-permute-start.8 = (f32[104,128]{1,0:T(8,128)}, f32[104,128]{1,0:T(8,128)S(1)}, u32[]{:S(2)}, u32[]{:S(2)}) collective-permute-start(f32[104,128]{1,0:T(8,128)} %get-tuple-element.35.z_hbm), channel_id=1, source_target_pairs={{0,3},{1,0},{2,1},{3,2},{4,7},{5,4},{6,5},{7,6},{8,11},{9,8},{10,9... | collective-permute-start | bytes 159752 | tf_op jit(solution)/shard_map/ppermute | solution.py:406
  36.3 6.5 %collective-permute-start.7 = (f32[104,128]{1,0:T(8,128)}, f32[104,128]{1,0:T(8,128)S(1)}, u32[]{:S(2)}, u32[]{:S(2)}) collective-permute-start(f32[104,128]{1,0:T(8,128)} %get-tuple-element.35.z_hbm), channel_id=1, source_target_pairs={{0,1},{1,2},{2,3},{3,0},{4,5},{5,6},{6,7},{7,4},{8,9},{9,10},{10,1... | collective-permute-start | bytes 159752 | tf_op jit(solution)/shard_map/ppermute | solution.py:406
  39.2 6.4 %collective-permute-start.6 = (f32[4,40,128]{2,1,0:T(8,128)}, f32[4,40,128]{2,1,0:T(8,128)S(1)}, u32[]{:S(2)}, u32[]{:S(2)}) collective-permute-start(f32[4,40,128]{2,1,0:T(8,128)} %get-tuple-element.33), channel_id=1, source_target_pairs={{0,64},{64,128},{128,192},{192,0},{1,65},{65,129},{129,193},{193,1... | collective-permute-start | bytes 245768 | tf_op jit(solution)/shard_map/ppermute | solution.py:406
  39.2 6.4 %collective-permute-start.10 = (f32[20,8,128]{2,1,0:T(8,128)}, f32[20,8,128]{2,1,0:T(8,128)S(1)}, u32[]{:S(2)}, u32[]{:S(2)}) collective-permute-start(f32[20,8,128]{2,1,0:T(8,128)} %get-tuple-element.37), channel_id=1, source_target_pairs={{0,4},{4,8},{8,12},{12,16},{16,20},{20,24},{24,28},{28,32},{32,36}... | collective-permute-start | bytes 245768 | tf_op jit(solution)/shard_map/ppermute | solution.py:406
  39.2 6.4 %collective-permute-start.11 = (f32[20,8,128]{2,1,0:T(8,128)}, f32[20,8,128]{2,1,0:T(8,128)S(1)}, u32[]{:S(2)}, u32[]{:S(2)}) collective-permute-start(f32[20,8,128]{2,1,0:T(8,128)} %get-tuple-element.38), channel_id=1, source_target_pairs={{0,60},{4,0},{8,4},{12,8},{16,12},{20,16},{24,20},{28,24},{32,28},... | collective-permute-start | bytes 245768 | tf_op jit(solution)/shard_map/ppermute | solution.py:406
  42.7 4.6 %copy-start.12 = (f32[104,128]{1,0:T(8,128)}, f32[104,128]{1,0:T(8,128)S(1)}, u32[]{:S(2)}) copy-start(f32[104,128]{1,0:T(8,128)S(1)} %collective-permute-done.8.z1_hbm) | copy-start | bytes 159748
  42.8 4.6 %copy-start.13 = (f32[104,128]{1,0:T(8,128)}, f32[104,128]{1,0:T(8,128)S(1)}, u32[]{:S(2)}) copy-start(f32[104,128]{1,0:T(8,128)S(1)} %collective-permute-done.7.z0_hbm) | copy-start | bytes 159748
  42.8 4.6 %collective-permute-start.9 = (f32[4,40,128]{2,1,0:T(8,128)}, f32[4,40,128]{2,1,0:T(8,128)S(1)}, u32[]{:S(2)}, u32[]{:S(2)}) collective-permute-start(f32[4,40,128]{2,1,0:T(8,128)} %get-tuple-element.36), channel_id=1, source_target_pairs={{0,192},{64,0},{128,64},{192,128},{1,193},{65,1},{129,65},{193,129... | collective-permute-start | bytes 245768 | tf_op jit(solution)/shard_map/ppermute | solution.py:406
  45.5 1.8 %copy-start.6 = (f32[4,40,128]{2,1,0:T(8,128)}, f32[4,40,128]{2,1,0:T(8,128)S(1)}, u32[]{:S(2)}) copy-start(f32[4,40,128]{2,1,0:T(8,128)S(1)} %collective-permute-done.6.x0_hbm) | copy-start | bytes 245764
  45.5 1.8 %copy-start.7 = (f32[20,8,128]{2,1,0:T(8,128)}, f32[20,8,128]{2,1,0:T(8,128)S(1)}, u32[]{:S(2)}) copy-start(f32[20,8,128]{2,1,0:T(8,128)S(1)} %collective-permute-done.10.y0_hbm) | copy-start | bytes 245764
  45.5 1.8 %copy-start.8 = (f32[20,8,128]{2,1,0:T(8,128)}, f32[20,8,128]{2,1,0:T(8,128)S(1)}, u32[]{:S(2)}) copy-start(f32[20,8,128]{2,1,0:T(8,128)S(1)} %collective-permute-done.11.y1_hbm) | copy-start | bytes 245764
  (4 other events, 2.5 us)
